TPU v7x, 32 devices: a whole 2x2x4 slice. The times are simulated.
32 devices in a mesh: expert: 8 (over z, x), rows: 4 (over y, core).
Axes of the slice: x: 2, y: 2, z: 4, core: 2. Of those that a mesh axis runs over, the one named last changes fastest.
Arguments:
- patches: bfloat16 [32, 1024, 384], P(('expert', 'rows')), may hold values from -6 to 6
- image_ids: int32 [32, 1024], P(('expert', 'rows')), may hold values from 0 to 7, as said below
- first_gain: float32 [384], replicated, may hold values from 0.5 to 1.5
- qkv_weight: bfloat16 [384, 1152], replicated, may hold values from -0.3125 to 0.3125
- proj_weight: bfloat16 [384, 384], replicated, may hold values from -1.25 to 1.25
- second_gain: float32 [384], replicated, may hold values from 0.5 to 1.5
- slot_params: bfloat16 [384, 16], P(None, 'expert'), may hold values from -0.15625 to 0.15625
- up_weight: bfloat16 [16, 384, 1536], P('expert'), may hold values from -1.25 to 1.25
- down_weight: bfloat16 [16, 1536, 384], P('expert'), may hold values from -6 to 6
- cotangent: bfloat16 [32, 1024, 384], P(('expert', 'rows')), may hold values from -6 to 6
Outputs:
- output: bfloat16 [32, 1024, 384], P(('expert', 'rows'))
- patch_grad: float32 [32, 1024, 384], P(('expert', 'rows'))
- first_grad: float32 [384], replicated
- qkv_grad: float32 [384, 1152], replicated
- proj_grad: float32 [384, 384], replicated
- second_grad: float32 [384], replicated
- slot_grad: float32 [384, 16], P(None, 'expert')
- up_grad: float32 [16, 384, 1536], P('expert')
- down_grad: float32 [16, 1536, 384], P('expert')
Inputs may be any that keep to these rules, and one draw needn't show every extreme that they name: `image_ids`: in each row the ids start at 0 and rise by one at the first patch of each next image; a row holds 4 to 8 images, and some row holds 8.
All inputs are finite; a program needn't handle non-finite values.
Results may differ from a plain program's by a relative error of at most 0.017.
Values may be sent and summed in bfloat16 or wider, within the bound.
No kernel may reach another device: no remote copies, remote signals or barrier semaphores. Data moves between devices by JAX's collectives and lax.ppermute only.
A program may use at most 128 MiB of HBM per device.

v0:
```python
import jax
import jax.numpy as jnp
from jax import lax
from jax.sharding import PartitionSpec as P

HEADS = 6
IMG_ROW = 8


epsilon = 1e-06
masked_fill = -1e30


def norm_parts(values, gain):
    centred = values - jnp.mean(values, axis=-1, keepdims=True)
    factor = lax.rsqrt(jnp.mean(centred * centred, axis=-1, keepdims=True) + epsilon)
    normed = centred * factor
    return (normed * gain, normed, factor)


def norm_back(grad_norm, normed, factor, gain):
    scaled = grad_norm * gain
    inner = (
        scaled
        - jnp.mean(scaled, axis=-1, keepdims=True)
        - normed * jnp.mean(scaled * normed, axis=-1, keepdims=True)
    )
    return (factor * inner, jnp.sum(grad_norm * normed, axis=0))


def block_scores(queries, keys, query_ids, key_ids, factor):
    scores = jnp.einsum("qhd,khd->hqk", queries, keys, preferred_element_type=jnp.float32) * factor
    same = query_ids[:, None] == key_ids[None, :]
    return jnp.where(same[None], scores, masked_fill)


def attend_row(queries, keys, values, key_ids, factor):
    length, heads, head_dim = queries.shape
    block = min(512, length)
    count = length // block

    def one_block(item):
        query_block, block_ids = item
        scores = block_scores(query_block, keys, block_ids, key_ids, factor)
        top = jnp.max(scores, axis=-1, keepdims=True)
        raised = jnp.exp(scores - top)
        total = jnp.sum(raised, axis=-1, keepdims=True)
        probs = (raised / total).astype(jnp.bfloat16)
        mixed = jnp.einsum("hqk,khd->qhd", probs, values, preferred_element_type=jnp.float32)
        return (mixed.astype(jnp.bfloat16), (top + jnp.log(total))[..., 0])

    mixed, lse = lax.map(
        one_block, (queries.reshape(count, block, heads, head_dim), key_ids.reshape(count, block))
    )
    return (mixed.reshape(length, heads * head_dim), lse)


def attend_back(queries, keys, values, key_ids, lse, grad_mixed, factor):
    length, heads, head_dim = queries.shape
    block = min(512, length)
    count = length // block

    def one_block(carry, item):
        grad_keys, grad_values = carry
        query_block, block_ids, block_lse, grad_block = item
        scores = block_scores(query_block, keys, block_ids, key_ids, factor)
        probs = jnp.exp(scores - block_lse[..., None])
        grad_values = grad_values + jnp.einsum(
            "hqk,qhd->khd",
            probs.astype(jnp.bfloat16),
            grad_block,
            preferred_element_type=jnp.float32,
        )
        grad_probs = jnp.einsum(
            "qhd,khd->hqk", grad_block, values, preferred_element_type=jnp.float32
        )
        grad_scores = (
            probs * (grad_probs - jnp.sum(probs * grad_probs, axis=-1, keepdims=True))
        ).astype(jnp.bfloat16)
        grad_query = (
            jnp.einsum("hqk,khd->qhd", grad_scores, keys, preferred_element_type=jnp.float32)
            * factor
        )
        grad_keys = (
            grad_keys
            + jnp.einsum(
                "hqk,qhd->khd", grad_scores, query_block, preferred_element_type=jnp.float32
            )
            * factor
        )
        return ((grad_keys, grad_values), grad_query)

    start = jnp.zeros((length, heads, head_dim), jnp.float32)
    items = (
        queries.reshape(count, block, heads, head_dim),
        key_ids.reshape(count, block),
        lse,
        grad_mixed.reshape(count, block, heads, head_dim),
    )
    (grad_keys, grad_values), grad_queries = lax.scan(one_block, (start, start), items)
    flat = heads * head_dim
    return jnp.concatenate(
        [
            grad_queries.reshape(length, flat),
            grad_keys.reshape(length, flat),
            grad_values.reshape(length, flat),
        ],
        axis=-1,
    )


def per_device(
    patches,
    image_ids,
    first_gain,
    qkv_weight,
    proj_weight,
    second_gain,
    slot_params,
    up_weight,
    down_weight,
    cotangent,
):
    rows_dev, length, width = patches.shape
    heads = HEADS
    head_dim = width // heads
    factor = head_dim ** (-0.5)
    images = IMG_ROW
    slot_full = lax.all_gather(slot_params, "expert", axis=1, tiled=True)
    experts = slot_full.shape[1]
    tokens = patches.astype(jnp.float32).reshape(rows_dev * length, width)
    first_norm, first_hat, first_factor = norm_parts(tokens, first_gain)
    first_in = first_norm.astype(jnp.bfloat16)
    qkv = jnp.dot(first_in, qkv_weight, preferred_element_type=jnp.float32).astype(jnp.bfloat16)
    row = 0
    queries = qkv[:, :width].reshape(length, heads, head_dim)
    keys = qkv[:, width : 2 * width].reshape(length, heads, head_dim)
    values = qkv[:, 2 * width :].reshape(length, heads, head_dim)
    mixed, lse = attend_row(queries, keys, values, image_ids[row], factor)
    row_parts = [(queries, keys, values, lse, mixed)]
    attn = jnp.concatenate([entry[4] for entry in row_parts], axis=0)
    resid = tokens + jnp.dot(attn, proj_weight, preferred_element_type=jnp.float32)
    second_norm, second_hat, second_factor = norm_parts(resid, second_gain)
    second_in = second_norm.astype(jnp.bfloat16)
    second_rows = second_in.reshape(rows_dev, length, width)
    logits = jnp.dot(second_in, slot_full, preferred_element_type=jnp.float32).reshape(
        rows_dev, length, experts
    )
    member = (image_ids[:, :, None] == jnp.arange(images, dtype=jnp.int32)[None, None, :]).astype(
        jnp.float32
    )
    masked = jnp.where(member[..., None] > 0, logits[:, :, None, :], masked_fill)
    top = jnp.max(masked, axis=1, keepdims=True)
    raised = member[..., None] * jnp.exp(masked - top)
    present = jnp.max(member, axis=1)
    total = jnp.sum(raised, axis=1, keepdims=True) + (1.0 - present)[:, None, :, None]
    dispatch = raised / total
    dispatch_low = dispatch.astype(jnp.bfloat16)
    slot_in = jnp.einsum(
        "rpjs,rpd->rjsd", dispatch_low, second_rows, preferred_element_type=jnp.float32
    ).astype(jnp.bfloat16)
    combine = jax.nn.softmax(logits, axis=-1)
    combine_low = (member[..., None] * combine[:, :, None, :]).astype(jnp.bfloat16)

    def expert_pre(received):
        return jnp.einsum("rjed,edf->rjef", received, up_weight, preferred_element_type=jnp.float32)

    whole = lax.all_to_all(slot_in, "expert", split_axis=2, concat_axis=0, tiled=True)
    pre = expert_pre(whole)
    hidden = jax.nn.gelu(pre, approximate=False).astype(jnp.bfloat16)
    out = jnp.einsum(
        "rjef,efd->rjed", hidden, down_weight, preferred_element_type=jnp.float32
    ).astype(jnp.bfloat16)
    slot_out = lax.all_to_all(out, "expert", split_axis=0, concat_axis=2, tiled=True)
    moe = jnp.einsum("rpjs,rjsd->rpd", combine_low, slot_out, preferred_element_type=jnp.float32)
    output = (
        (resid + moe.reshape(rows_dev * length, width))
        .astype(jnp.bfloat16)
        .reshape(rows_dev, length, width)
    )
    grad_out = cotangent.astype(jnp.float32).reshape(rows_dev * length, width)
    grad_slot_out = jnp.einsum(
        "rpjs,rpd->rjsd", combine_low, cotangent, preferred_element_type=jnp.float32
    ).astype(jnp.bfloat16)
    grad_combine = jnp.einsum(
        "rpd,rjsd->rpjs", cotangent, slot_out, preferred_element_type=jnp.float32
    )
    grad_own = jnp.sum(member[..., None] * grad_combine, axis=2)
    grad_logits = combine * (grad_own - jnp.sum(combine * grad_own, axis=-1, keepdims=True))
    received_grad = lax.all_to_all(grad_slot_out, "expert", split_axis=2, concat_axis=0, tiled=True)
    received = whole
    pre = expert_pre(received)
    hidden_full, gelu_pull = jax.vjp(lambda value: jax.nn.gelu(value, approximate=False), pre)
    hidden = hidden_full.astype(jnp.bfloat16)
    down_local = jnp.einsum(
        "rjef,rjed->efd", hidden, received_grad, preferred_element_type=jnp.float32
    )
    grad_hidden = jnp.einsum(
        "rjed,efd->rjef", received_grad, down_weight, preferred_element_type=jnp.float32
    )
    grad_pre = gelu_pull(grad_hidden)[0].astype(jnp.bfloat16)
    up_local = jnp.einsum("rjed,rjef->edf", received, grad_pre, preferred_element_type=jnp.float32)
    grad_terms = jnp.einsum(
        "rjef,edf->rjed", grad_pre, up_weight, preferred_element_type=jnp.float32
    )
    grad_received = grad_terms.astype(jnp.bfloat16)
    grad_slot_in = lax.all_to_all(grad_received, "expert", split_axis=0, concat_axis=2, tiled=True)
    grad_dispatch = jnp.einsum(
        "rpd,rjsd->rpjs", second_rows, grad_slot_in, preferred_element_type=jnp.float32
    )
    weighted = jnp.sum(dispatch * grad_dispatch, axis=1, keepdims=True)
    grad_logits = grad_logits + jnp.sum(dispatch * (grad_dispatch - weighted), axis=2)
    grad_logits_low = grad_logits.astype(jnp.bfloat16).reshape(rows_dev * length, experts)
    slot_local = jnp.einsum(
        "pd,ps->ds", second_in, grad_logits_low, preferred_element_type=jnp.float32
    )
    grad_second_in = jnp.einsum(
        "rpjs,rjsd->rpd", dispatch_low, grad_slot_in, preferred_element_type=jnp.float32
    ).reshape(rows_dev * length, width)
    grad_second_in = grad_second_in + jnp.einsum(
        "ps,ds->pd", grad_logits_low, slot_full, preferred_element_type=jnp.float32
    )
    grad_second_norm, second_local = norm_back(
        grad_second_in, second_hat, second_factor, second_gain
    )
    grad_resid = grad_out + grad_second_norm
    grad_branch = grad_resid.astype(jnp.bfloat16)
    proj_local = jnp.einsum("pa,pb->ab", attn, grad_branch, preferred_element_type=jnp.float32)
    grad_attn = jnp.einsum(
        "pb,ab->pa", grad_branch, proj_weight, preferred_element_type=jnp.float32
    ).astype(jnp.bfloat16)
    row = 0
    queries, keys, values, lse, mixed = row_parts[row]
    grad_piece = grad_attn.reshape(length, heads, head_dim)
    grad_rows = attend_back(queries, keys, values, image_ids[row], lse, grad_piece, factor)
    grad_qkv = grad_rows.astype(jnp.bfloat16)
    qkv_local = jnp.einsum("pa,pb->ab", first_in, grad_qkv, preferred_element_type=jnp.float32)
    grad_first_in = jnp.einsum(
        "pb,ab->pa", grad_qkv, qkv_weight, preferred_element_type=jnp.float32
    )
    grad_first_norm, first_local = norm_back(grad_first_in, first_hat, first_factor, first_gain)
    patch_grad = (grad_resid + grad_first_norm).reshape(rows_dev, length, width)
    slot_share = lax.psum_scatter(slot_local, "expert", scatter_dimension=1, tiled=True)
    dense = lax.psum((first_local, qkv_local, proj_local, second_local), ("expert", "rows"))
    expert_sums = (
        lax.psum(up_local.astype(jnp.bfloat16), "rows").astype(jnp.float32),
        lax.psum(down_local.astype(jnp.bfloat16), "rows").astype(jnp.float32),
        lax.psum(slot_share.astype(jnp.bfloat16), "rows").astype(jnp.float32),
    )
    slot_grad = expert_sums[2]
    up_grad = expert_sums[0]
    down_grad = expert_sums[1]
    return (
        output,
        patch_grad,
        dense[0],
        dense[1],
        dense[2],
        dense[3],
        slot_grad,
        up_grad,
        down_grad,
    )


def solution(mesh):
    return jax.shard_map(
        per_device,
        mesh=mesh,
        in_specs=(
            P(("expert", "rows"), None, None),
            P(("expert", "rows"), None),
            P(),
            P(),
            P(),
            P(),
            P(None, "expert"),
            P("expert", None, None),
            P("expert", None, None),
            P(("expert", "rows"), None, None),
        ),
        out_specs=(
            P(("expert", "rows"), None, None),
            P(("expert", "rows"), None, None),
            P(),
            P(),
            P(),
            P(),
            P(None, "expert"),
            P("expert", None, None),
            P("expert", None, None),
        ),
        check_vma=False,
    )
```

profile of v0, /device:TPU:0, one launch (start us, length us, event | category | flops | bytes accessed | tf_op | source)
XLA Modules:
  0.0 402.7 jit_solution(4583588212467637539)
XLA Ops:
  10.8 27.8 %all-gather = bf16[8,2,384]{2,1,0:T(2,128)(2,1)S(1)} all-gather(bf16[1,2,384]{2,1,0:T(2,128)(2,1)} %bitcast.373), channel_id=1, replica_groups=mesh['expert'=8,'rows'=4] {'expert'}, dimensions={0}, use_global_device_ids=true | all-gather | bytes 13824 | tf_op jit(solution)/shard_map/all_gather | solution.py:129
  38.6 1.4 copy.137
  40.5 2.8 convolution_convert_fusion
  43.3 1.5 fusion.148
  44.8 2.3 copy.140
  47.1 1.4 copy.139
  48.5 2.3 copy.138
  50.8 3.4 reshape_reshape.7
  54.2 2.1 copy.141
  56.3 25.5 %while.27 = (s32[]{:T(128)}, bf16[2,512,6,64]{1,3,2,0:T(8,128)(2,1)}, f32[2,6,512]{2,1,0:T(8,128)S(1)}, s32[2,512]{1,0:T(2,128)S(1)}, s32[1,1024]{1,0:T(1,128)S(...) while((s32[]{:T(128)}, ...), condition=%wide.region_5.6_spmd, body=%wide.region_2.5_spmd.sunk | while | flops 843772928 | bytes 51771592 | solution.py:52
  56.7 3.4 fusion.194
  60.1 3.6 fusion.195
  63.8 4.4 %fusion.196 = bf16[2,512,6,64]{1,3,2,0:T(8,128)(2,1)S(1)} fusion(bf16[2,512,6,64]{1,3,2,0:T(8,128)(2,1)S(1)} %copy-done.33, s32[]{:T(128)S(6)} %copy.217, bf16[1024,6,64]{0,2,1:T(8,128)(2,1)S(1)} %copy-done.6, f32[6,512,1024]{2,1,0:T(8,128)S(1)} %get-tuple-element.473, f32[6,512]{1,0:T(8,128)S(1)} %fusion.195, f32[6,512]{1,0:T(8,128)S(1)} %get-tuple-element.474, ...), kind=kOutput, calls=%fused_computation.8.clone.1 | convolution fusion | flops 418578432 | bytes 14319620 | tf_op jit(solution)/shard_map/while/body/eval_jaxpr/hqk,khd->qhd/dot_general | solution.py:49
  69.5 3.4 fusion.194
  72.9 3.6 fusion.195
  76.5 4.4 %fusion.196 = bf16[2,512,6,64]{1,3,2,0:T(8,128)(2,1)S(1)} fusion(bf16[2,512,6,64]{1,3,2,0:T(8,128)(2,1)S(1)} %copy-done.33, s32[]{:T(128)S(6)} %copy.217, bf16[1024,6,64]{0,2,1:T(8,128)(2,1)S(1)} %copy-done.6, f32[6,512,1024]{2,1,0:T(8,128)S(1)} %get-tuple-element.473, f32[6,512]{1,0:T(8,128)S(1)} %fusion.195, f32[6,512]{1,0:T(8,128)S(1)} %get-tuple-element.474, ...), kind=kOutput, calls=%fused_computation.8.clone.1 | convolution fusion | flops 418578432 | bytes 14319620 | tf_op jit(solution)/shard_map/while/body/eval_jaxpr/hqk,khd->qhd/dot_general | solution.py:49
  81.8 2.0 copy.142
  87.0 10.8 %all_to_all.66 = bf16[1,8,16,384]{3,1,0,2:T(8,128)(2,1)S(1)} all-to-all(bf16[1,8,16,384]{3,1,0,2:T(8,128)(2,1)S(1)} %copy.144), channel_id=1, replica_groups=mesh['expert'=8,'rows'=4] {'expert'}, dimensions={2} | all-to-all | bytes 196608 | tf_op jit(solution)/shard_map/all_to_all | solution.py:168
  97.8 3.0 fusion.86
  102.2 3.6 all-to-all-start.1
  105.8 2.3 copy.149
  109.4 3.5 all-to-all-done.1
  112.8 1.5 fusion.65
  115.0 1.5 fusion.73
  117.1 3.4 all-to-all-start.2
  120.5 2.7 fusion.61
  123.2 2.3 copy.165
  125.5 2.1 all-to-all-done.2
  127.6 3.4 bitcast_convert_fusion
  131.0 1.8 fusion.92
  134.2 3.9 all-to-all-start.3
  138.2 3.1 bitcast_convert_fusion.1
  141.4 3.8 all-to-all-done.3
  150.7 1.6 convolution_convert_fusion.1
  152.3 1.5 copy.159
  153.8 1.5 reshape_reshape.8
  155.3 2.1 copy.161
  157.4 50.2 %while.28 = (s32[]{:T(128)}, f32[1024,6,64]{0,2,1:T(8,128)S(1)}, f32[1024,6,64]{0,2,1:T(8,128)}, bf16[2,512,6,64]{1,3,2,0:T(8,128)(2,1)}, bf16[2,512,6,64]{1,3,2...) while((s32[]{:T(128)}, f32[1024,6,64]{0,2,1:T(8,128)S(1)}, ...), condition=%wide.region_21.22_spmd.clone, body=%wide.region_19.21_spmd.clone.sunk | while | flops 2063135744 | bytes 135895408 | solution.py:100
  158.3 3.0 fusion.206
  161.3 3.5 bitcast_add_fusion.7
  164.8 7.2 %multiply_reduce_fusion.9 = (f32[6,512]{1,0:T(8,128)S(1)}, f32[6,512,1024]{2,1,0:T(8,128)}) fusion(f32[6,512,1024]{2,1,0:T(8,128)S(1)} %fusion.206, f32[6,512]{1,0:T(8,128)S(1)} %dynamic-slice_bitcast_fusion.2, pred[512,1024]{1,0:T(8,128)(4,1)S(1)} %broadcast_compare_fusion.6, bf16[1024,6,64]{0,2,1:T(8,128)(2,1)S(1)} %copy-done.7, ...), kind=kOutput, calls=%fused_computation.19.clone.1 | convolution fusion | flops 418378752 | bytes 26898436 | tf_op jit(solution)/shard_map/while/body/eval_jaxpr/qhd,khd->hqk/dot_general | solution.py:74
  172.0 7.0 %multiply_convert_fusion.6 = bf16[6,512,1024]{2,1,0:T(8,128)(2,1)S(1)} fusion(f32[6,512,1024]{2,1,0:T(8,128)} %get-tuple-element.486, f32[6,512,1024]{2,1,0:T(8,128)S(1)} %fusion.206, f32[6,512]{1,0:T(8,128)S(1)} %get-tuple-element.487, f32[6,512]{1,0:T(8,128)S(1)} %dynamic-slice_bitcast_fusion.2, pred[512,1024]{1,0:T(8,128)(4,1)S(1)} %broadcast_compare_fusion.6), kind=kLoop, calls=%fused_computation.18.clone.1 | loop fusion | flops 18874368 | bytes 32006144 | tf_op jit(solution)/shard_map/while/body/eval_jaxpr/convert_element_type | solution.py:79
  179.0 2.0 fusion.207
  181.0 1.4 bitcast_add_fusion.6
  182.9 3.0 fusion.206
  185.9 3.5 bitcast_add_fusion.7
  189.4 7.2 %multiply_reduce_fusion.9 = (f32[6,512]{1,0:T(8,128)S(1)}, f32[6,512,1024]{2,1,0:T(8,128)}) fusion(f32[6,512,1024]{2,1,0:T(8,128)S(1)} %fusion.206, f32[6,512]{1,0:T(8,128)S(1)} %dynamic-slice_bitcast_fusion.2, pred[512,1024]{1,0:T(8,128)(4,1)S(1)} %broadcast_compare_fusion.6, bf16[1024,6,64]{0,2,1:T(8,128)(2,1)S(1)} %copy-done.7, ...), kind=kOutput, calls=%fused_computation.19.clone.1 | convolution fusion | flops 418378752 | bytes 26898436 | tf_op jit(solution)/shard_map/while/body/eval_jaxpr/qhd,khd->hqk/dot_general | solution.py:74
  196.6 7.6 %multiply_convert_fusion.6 = bf16[6,512,1024]{2,1,0:T(8,128)(2,1)S(1)} fusion(f32[6,512,1024]{2,1,0:T(8,128)} %get-tuple-element.486, f32[6,512,1024]{2,1,0:T(8,128)S(1)} %fusion.206, f32[6,512]{1,0:T(8,128)S(1)} %get-tuple-element.487, f32[6,512]{1,0:T(8,128)S(1)} %dynamic-slice_bitcast_fusion.2, pred[512,1024]{1,0:T(8,128)(4,1)S(1)} %broadcast_compare_fusion.6), kind=kLoop, calls=%fused_computation.18.clone.1 | loop fusion | flops 18874368 | bytes 32006144 | tf_op jit(solution)/shard_map/while/body/eval_jaxpr/convert_element_type | solution.py:79
  204.2 2.0 fusion.207
  207.7 1.4 fusion.152
  209.1 34.7 %all-reduce = bf16[384,16]{0,1:T(8,128)(2,1)S(1)} all-reduce(f32[384,16]{0,1:T(8,128)S(1)} %fusion.152), channel_id=2, replica_groups=mesh['expert'=8,'rows'=4] {'expert'}, use_global_device_ids=true, to_apply=%region_30.31.clone | all-reduce | flops 6144 | bytes 36864
  243.8 5.8 %psum.53 = bf16[384,2]{0,1:T(2,128)(2,1)S(1)} all-reduce(bf16[384,2]{0,1:T(2,128)(2,1)S(1)} %dynamic-slice_convert_fusion), channel_id=1, replica_groups=mesh['expert'=8,'rows'=4] {'rows'}, use_global_device_ids=true, to_apply=%region_31.32 | all-reduce | flops 768 | bytes 3072 | tf_op jit(solution)/shard_map/psum | solution.py:248
  250.2 1.9 copy.162
  252.5 1.7 copy-done.24
  254.8 1.4 fusion.114
  256.3 2.5 fusion.80
  259.9 3.1 fusion.58
  263.1 1.7 fusion.57
  264.7 3.0 copy.166
  267.8 36.9 %all-reduce.1 = (f32[384]{0:T(512)}, f32[384]{0:T(512)}) all-reduce(f32[384]{0:T(512)S(1)} %get-tuple-element.294, f32[384]{0:T(512)S(1)} %copy-done.65), channel_id=1, replica_groups=mesh['expert'=8,'rows'=4] {'expert','rows'}, use_global_device_ids=true, to_apply=%region_25.26 | all-reduce | flops 768 | bytes 6144 | tf_op jit(solution)/shard_map/psum | solution.py:244
  304.7 4.7 %convert_element_type.151 = f32[2,384,1536]{2,1,0:T(8,128)} convert(bf16[2,384,1536]{2,1,0:T(8,128)(2,1)} %get-tuple-element.340) | non-fusion elementwise | flops 1179648 | bytes 7077888 | tf_op jit(solution)/shard_map/convert_element_type | solution.py:246
  309.3 2.5 convert_element_type.153
  311.8 80.1 %all-reduce.7.cloned.1.call-done = (f32[384,1152]{1,0:T(8,128)}, f32[384,384]{1,0:T(8,128)}) async-done(((f32[384,1152]{1,0:T(8,128)}, f32[384,384]{1,0:T(8,128)}), (f32[384,1152]{1,0:T(8,128)}, f32[384,384]{1,0:T(8,128)})) %all-reduce.7.cloned.1.call-update) | async-done | bytes 2359312 | tf_op jit(solution)/shard_map/psum | solution.py:244
  391.9 2.9 copy.239
  (234 shorter events, 25.3 us)
Async XLA Ops:
  7.2 90.6 %copy-start = (bf16[2,384,1536]{2,1,0:T(8,128)(2,1)S(1)}, bf16[2,384,1536]{2,1,0:T(8,128)(2,1)}, u32[]{:S(2)}) copy-start(bf16[2,384,1536]{2,1,0:T(8,128)(2,1)} %param.21) | copy-start | bytes 7077892
  7.2 33.3 %copy-start.70 = (f32[384]{0:T(512)S(1)}, f32[384]{0:T(512)}, u32[]{:S(2)}) copy-start(f32[384]{0:T(512)} %param.16) | copy-start | bytes 4612
  8.9 77.6 %copy-start.58 = (pred[1024,8]{0,1:T(8,128)(4,1)}, pred[1024,8]{0,1:T(8,128)(4,1)S(1)}, u32[]{:S(2)}) copy-start(pred[1024,8]{0,1:T(8,128)(4,1)S(1)} %get-tuple-element.353) | copy-start | bytes 24580
  8.9 111.6 %copy-start.47 = (f32[1024,8]{0,1:T(8,128)}, f32[1024,8]{0,1:T(8,128)S(1)}, u32[]{:S(2)}) copy-start(f32[1024,8]{0,1:T(8,128)S(1)} %get-tuple-element.354) | copy-start | bytes 98308
  38.6 46.7 %copy-start.53 = (bf16[16,384]{1,0:T(8,128)(2,1)}, bf16[16,384]{1,0:T(8,128)(2,1)S(1)}, u32[]{:S(2)}) copy-start(bf16[16,384]{1,0:T(8,128)(2,1)S(1)} %reshape.427) | copy-start | bytes 36868
  40.1 3.2 copy-start.10
  40.2 3.1 copy-start.56
  40.5 2.8 copy-start.63
  48.5 7.8 %copy-start.41 = (s32[1,1024]{1,0:T(1,128)S(1)}, s32[1,1024]{1,0:T(1,128)}, u32[]{:S(2)}) copy-start(s32[1,1024]{1,0:T(1,128)} %param.15) | copy-start | bytes 12292
  60.1 3.7 copy-start.6
  60.1 3.7 copy-start.33
  72.8 3.7 copy-start.6
  72.8 3.7 copy-start.33
  81.8 2.9 copy-start.51
  81.8 2.2 copy-start.11
  81.8 2.2 copy-start.25
  86.0 28.3 %copy-start.27 = (f32[1024,16]{0,1:T(8,128)}, f32[1024,16]{0,1:T(8,128)S(1)}, u32[]{:S(2)}) copy-start(f32[1024,16]{0,1:T(8,128)S(1)} %get-tuple-element.359) | copy-start | bytes 196612
  86.2 14.6 %copy-start.66 = (f32[8,16]{1,0:T(8,128)}, f32[8,16]{1,0:T(8,128)S(1)}, u32[]{:S(2)}) copy-start(f32[8,16]{1,0:T(8,128)S(1)} %select_reduce_fusion) | copy-start | bytes 1540
  86.5 14.3 %copy-start.68 = (f32[8,16]{1,0:T(8,128)}, f32[8,16]{1,0:T(8,128)S(1)}, u32[]{:S(2)}) copy-start(f32[8,16]{1,0:T(8,128)S(1)} %broadcast_add_fusion) | copy-start | bytes 1540
  97.8 3.0 copy-start.55
  97.8 3.0 copy-start.14
  100.8 7.3 %copy-start.72 = (u32[32]{0:T(128)S(1)}, u32[32]{0:T(128)}, u32[]{:S(2)}) copy-start(u32[32]{0:T(128)} %constant.138) | copy-start | bytes 388
  102.2 10.6 %all-to-all-start.1 = ((bf16[8,8,2,384]{3,1,2,0:T(8,128)(2,1)}), bf16[8,8,2,384]{3,1,2,0:T(8,128)(2,1)S(1)}, u32[]{:S(2)}, u32[]{:S(2)}) async-start(bf16[8,8,2,384]{3,1,2,0:T(8,128)(2,1)} %copy.146), calls=%async_computation.1 | async-start | bytes 196608 | tf_op jit(solution)/shard_map/all_to_all | solution.py:174
  115.0 10.5 %copy-start.29 = (f32[1024,16]{0,1:T(8,128)}, f32[1024,16]{0,1:T(8,128)S(1)}, u32[]{:S(2)}) copy-start(f32[1024,16]{0,1:T(8,128)S(1)} %get-tuple-element.343) | copy-start | bytes 196612
  117.1 10.4 %all-to-all-start.2 = ((bf16[1,8,16,384]{3,1,0,2:T(8,128)(2,1)}), bf16[1,8,16,384]{3,1,0,2:T(8,128)(2,1)S(1)}, u32[]{:S(2)}, u32[]{:S(2)}) async-start(bf16[1,8,16,384]{3,1,0,2:T(8,128)(2,1)} %copy.151), calls=%async_computation.2 | async-start | bytes 196608 | tf_op jit(solution)/shard_map/all_to_all | solution.py:190
  127.5 3.4 copy-start.44
  127.5 3.4 copy-start.15
  127.6 3.4 copy-start.39
  127.6 3.4 copy-start.40
  134.2 11.0 %all-to-all-start.3 = ((bf16[8,8,2,384]{3,1,2,0:T(8,128)(2,1)}), bf16[8,8,2,384]{3,1,2,0:T(8,128)(2,1)S(1)}, u32[]{:S(2)}, u32[]{:S(2)}) async-start(bf16[8,8,2,384]{3,1,2,0:T(8,128)(2,1)} %copy.153), calls=%async_computation.3 | async-start | bytes 196608 | tf_op jit(solution)/shard_map/all_to_all | solution.py:207
  138.1 166.5 %all-reduce.9.cloned.1.call-start = ((), (), s32[]{:S(2)}) async-start(), calls=%async_computation.5 | async-start | bytes 9437184 | tf_op jit(solution)/shard_map/psum | solution.py:246
  141.3 4.0 copy-start.19
  141.3 4.3 %copy-start.28 = (f32[1024,16]{0,1:T(8,128)S(1)}, f32[1024,16]{0,1:T(8,128)}, u32[]{:S(2)}) copy-start(f32[1024,16]{0,1:T(8,128)} %copy-done.27) | copy-start | bytes 196612
  141.3 4.3 %copy-start.48 = (f32[1024,8]{0,1:T(8,128)S(1)}, f32[1024,8]{0,1:T(8,128)}, u32[]{:S(2)}) copy-start(f32[1024,8]{0,1:T(8,128)} %copy-done.47) | copy-start | bytes 98308
  141.3 4.3 %copy-start.59 = (pred[1024,8]{0,1:T(8,128)(4,1)S(1)}, pred[1024,8]{0,1:T(8,128)(4,1)}, u32[]{:S(2)}) copy-start(pred[1024,8]{0,1:T(8,128)(4,1)} %copy-done.58) | copy-start | bytes 24580
  141.3 4.3 %copy-start.67 = (f32[8,16]{1,0:T(8,128)S(1)}, f32[8,16]{1,0:T(8,128)}, u32[]{:S(2)}) copy-start(f32[8,16]{1,0:T(8,128)} %copy-done.66) | copy-start | bytes 1540
  141.4 4.3 %copy-start.69 = (f32[8,16]{1,0:T(8,128)S(1)}, f32[8,16]{1,0:T(8,128)}, u32[]{:S(2)}) copy-start(f32[8,16]{1,0:T(8,128)} %copy-done.68) | copy-start | bytes 1540
  141.4 250.5 %all-reduce.7.cloned.1.call-start = ((), (), s32[]{:S(2)}) async-start(), calls=%async_computation.4 | async-start | bytes 4718592 | tf_op jit(solution)/shard_map/psum | solution.py:244
  152.3 5.1 %copy-start.2 = (f32[1024,6,64]{0,2,1:T(8,128)S(1)}, f32[1024,6,64]{0,2,1:T(8,128)}, u32[]{:S(2)}) copy-start(f32[1024,6,64]{0,2,1:T(8,128)} %custom-call) | copy-start | bytes 4718596
  152.3 5.1 %copy-start.52 = (f32[2,6,512]{2,1,0:T(8,128)S(1)}, f32[2,6,512]{2,1,0:T(8,128)}, u32[]{:S(2)}) copy-start(f32[2,6,512]{2,1,0:T(8,128)} %copy-done.51) | copy-start | bytes 73732
  157.4 50.2 %copy-start.46 = (bf16[1024,16]{0,1:T(8,128)(2,1)S(1)}, bf16[1024,16]{0,1:T(8,128)(2,1)}, u32[]{:S(2)}) copy-start(bf16[1024,16]{0,1:T(8,128)(2,1)} %copy-done.45) | copy-start | bytes 98308
  158.3 3.0 copy-start.13
  158.3 3.0 copy-start.22
  161.3 3.5 copy-start.7
  164.8 7.2 %copy-start.23 = (f32[1024,6,64]{0,2,1:T(8,128)}, f32[1024,6,64]{0,2,1:T(8,128)S(1)}, u32[]{:S(2)}) copy-start(f32[1024,6,64]{0,2,1:T(8,128)S(1)} %bitcast_add_fusion.7) | copy-start | bytes 4718596 | tf_op jit(solution)/shard_map/while
  172.0 7.0 %copy-start.31 = (bf16[2,512,6,64]{1,3,2,0:T(8,128)(2,1)S(1)}, bf16[2,512,6,64]{1,3,2,0:T(8,128)(2,1)}, u32[]{:S(2)}) copy-start(bf16[2,512,6,64]{1,3,2,0:T(8,128)(2,1)} %get-tuple-element.531) | copy-start | bytes 2359300 | tf_op jit(solution)/shard_map/while
  182.8 3.0 copy-start.13
  182.9 3.0 copy-start.22
  185.9 3.5 copy-start.7
  189.4 7.2 %copy-start.23 = (f32[1024,6,64]{0,2,1:T(8,128)}, f32[1024,6,64]{0,2,1:T(8,128)S(1)}, u32[]{:S(2)}) copy-start(f32[1024,6,64]{0,2,1:T(8,128)S(1)} %bitcast_add_fusion.7) | copy-start | bytes 4718596 | tf_op jit(solution)/shard_map/while
  196.6 7.6 %copy-start.31 = (bf16[2,512,6,64]{1,3,2,0:T(8,128)(2,1)S(1)}, bf16[2,512,6,64]{1,3,2,0:T(8,128)(2,1)}, u32[]{:S(2)}) copy-start(bf16[2,512,6,64]{1,3,2,0:T(8,128)(2,1)} %get-tuple-element.531) | copy-start | bytes 2359300 | tf_op jit(solution)/shard_map/while
  204.2 2.0 copy-start.3
  252.3 3.9 copy-start.35
  252.3 2.3 copy-start.9
  252.4 2.5 copy-start.17
  252.5 3.8 copy-start.37
  254.2 2.1 copy-start.12
  254.2 2.1 copy-start.57
  254.2 2.1 copy-start.64
  254.2 2.1 copy-start.71
  264.7 3.0 copy-start.65
  304.7 4.7 %copy-start.21 = (bf16[2,1536,384]{2,1,0:T(8,128)(2,1)S(1)}, bf16[2,1536,384]{2,1,0:T(8,128)(2,1)}, u32[]{:S(2)}) copy-start(bf16[2,1536,384]{2,1,0:T(8,128)(2,1)} %get-tuple-element.341) | copy-start | bytes 7077892
  391.9 3.0 copy-start.42
  391.9 3.8 copy-start.1
  (24 other events, 29.7 us)
Sparse Core Ops, SparseCore 0:
  142.5 95.6 all-reduce.8
  258.9 132.9 all-reduce.6
where the time goes:
time: 408 us; the launch traced here: 403 us
  blocking collectives  116 us (28%)
  waiting for transfers between devices  89.5 us (22%)
  matrix products  84.3 us (21%)
  local copies, waits for them, and re-layouts  46.4 us (11%)
  other arithmetic  39.1 us (10%)
  between operations  15.7 us (4%)
  starting transfers between devices  10.9 us (3%)
    psum x1, waiting for transfers between devices, per_device(): lax.psum((first_local, qkv_local, proj_local, second_local), ('expert', '...  80.1 us
    psum x1, blocking collectives, per_device(): lax.psum((first_local, qkv_local, proj_local, second_local), ('expert', '...  36.9 us
    unnamed x1, blocking collectives  34.7 us
    all_gather x1, blocking collectives, per_device(): slot_full = lax.all_gather(slot_params, 'expert', axis=1, tiled=True)  27.8 us
    unnamed x138, local copies, waits for them, and re-layouts  22.6 us
    convert_element_type x2, other arithmetic, one_block(): grad_scores = (probs * (grad_probs - jnp.sum(probs * grad_probs, axis=-1,...  14.5 us
    dot_general x2, matrix products, one_block(): jnp.einsum('qhd,khd->hqk', grad_block, values, preferred_element_type=jnp...  14.4 us
    dot_general x4, matrix products, block_scores(): jnp.einsum('qhd,khd->hqk', queries, keys, preferred_element_type=jnp.floa...  12.7 us
  transfers between devices with their start and end apart: 5, of which 4 were waited for; matrix products, arithmetic and copies ran while one was open for 23% of the time, Pallas kernels for 0%

commit v1 on v0

v1 whole, which is shorter than its diff:
```python
import jax
import jax.numpy as jnp
from jax import lax
from jax.experimental import pallas as pl
from jax.experimental.pallas import tpu as pltpu
from jax.sharding import PartitionSpec as P

HEADS = 6
IMG_ROW = 8
LANES = 128
TILE = 256

epsilon = 1e-06
masked_fill = -1e30
low = jnp.bfloat16
full = jnp.float32
whole_vmem = pl.BlockSpec(memory_space=pltpu.VMEM)
both_axes = ("expert", "rows")


def dot(left, right, left_dim=1, right_dim=0):
    return lax.dot_general(
        left, right, (((left_dim,), (right_dim,)), ((), ())), preferred_element_type=full
    )


def shape_of(shape, dtype):
    return jax.ShapeDtypeStruct(shape, dtype)


def params(mib):
    return pltpu.CompilerParams(vmem_limit_bytes=mib << 20)


def norm_parts(values):
    centred = values - jnp.mean(values, axis=-1, keepdims=True)
    factor = lax.rsqrt(jnp.mean(centred * centred, axis=-1, keepdims=True) + epsilon)
    return centred * factor, factor


def norm_back(grad_norm, normed, factor, gain):
    scaled = grad_norm * gain
    return factor * (
        scaled
        - jnp.mean(scaled, axis=-1, keepdims=True)
        - normed * jnp.mean(scaled * normed, axis=-1, keepdims=True)
    )


def member_of(ids):
    images = lax.broadcasted_iota(jnp.int32, (IMG_ROW, ids.shape[1]), 0)
    return images == ids


def gelu_parts(pre):
    cdf = 0.5 * (1.0 + lax.erf(pre * 0.7071067811865476))
    pdf = 0.3989422804014327 * jnp.exp(-0.5 * pre * pre)
    return cdf, pdf


def attend_kernel(
    x_ref, ids_ref, gain_ref, weight_ref,
    probs_ref, attn_ref, queries_ref, keys_ref, value_rows_ref, first_ref,
    key_rows, values, mask_rows, same,
):
    pair = pl.program_id(0)
    length, width = x_ref.shape
    pairs = width // LANES
    half = LANES // 2

    @pl.when(pair == 0)
    def _():
        normed, _ = norm_parts(x_ref[...].astype(full))
        first_in = (normed * gain_ref[...]).astype(low)
        first_ref[...] = first_in.T
        turned = dot(weight_ref[...], first_in, 0, 1).astype(low)
        queries_ref[...] = turned[:width].reshape(pairs, LANES, length)
        keys_ref[...] = turned[width : 2 * width].reshape(pairs, LANES, length)
        values[...] = turned[2 * width :].reshape(pairs, LANES, length)
        rows = dot(first_in, weight_ref[:, width:]).astype(low)
        for index in range(pairs):
            key_rows[index] = rows[:, index * LANES : (index + 1) * LANES]
            value_rows_ref[index] = rows[:, width + index * LANES : width + (index + 1) * LANES]
        images = lax.broadcasted_iota(jnp.int32, (LANES, length), 0)
        matching = images == ids_ref[...]
        same[...] = matching.astype(full).astype(low)
        other = jnp.where(jnp.logical_or(matching, images >= IMG_ROW), 0.0, masked_fill)
        mask_rows[...] = other.T.astype(low)

    keys = jnp.concatenate([key_rows[pair], mask_rows[...]], axis=1)
    scaled = queries_ref[pair] * jnp.asarray(half**-0.5, low)
    none = jnp.zeros((half, TILE), low)
    for head in range(2):
        value = values[pair, head * half : (head + 1) * half, :]
        for start in range(0, length, TILE):
            span = slice(start, start + TILE)
            query = scaled[head * half : (head + 1) * half, span]
            parts = [query, none] if head == 0 else [none, query]
            scores = dot(keys, jnp.concatenate(parts + [same[:, span]], axis=0))
            top = jnp.max(scores, axis=0, keepdims=True)
            raised = jnp.exp(scores - top)
            total = jnp.sum(raised, axis=0, keepdims=True)
            probs = (raised * (1.0 / total)).astype(low)
            probs_ref[head, :, span] = probs
            attn_ref[0, head * half : (head + 1) * half, span] = dot(value, probs).astype(low)


def attend(patches, ids, gain, weight):
    length, width = patches.shape
    pairs = width // LANES
    stack = (pairs, LANES, length)
    rows = (pairs, length, LANES)
    return pl.pallas_call(
        attend_kernel,
        grid=(pairs,),
        in_specs=[whole_vmem] * 4,
        out_specs=[
            pl.BlockSpec((2, length, length), lambda pair: (pair, 0, 0)),
            pl.BlockSpec((1, LANES, length), lambda pair: (pair, 0, 0)),
            pl.BlockSpec(stack, lambda pair: (0, 0, 0)),
            pl.BlockSpec(stack, lambda pair: (0, 0, 0)),
            pl.BlockSpec(rows, lambda pair: (0, 0, 0)),
            pl.BlockSpec((width, length), lambda pair: (0, 0)),
        ],
        out_shape=[
            shape_of((2 * pairs, length, length), low),
            shape_of(stack, low),
            shape_of(stack, low),
            shape_of(stack, low),
            shape_of(rows, low),
            shape_of((width, length), low),
        ],
        scratch_shapes=[
            pltpu.VMEM(rows, low),
            pltpu.VMEM(stack, low),
            pltpu.VMEM((length, LANES), low),
            pltpu.VMEM((LANES, length), low),
        ],
        compiler_params=params(48),
        name="attend",
    )(patches, ids, gain, weight)


def slot_rows(slots):
    experts = slots.shape[0]
    row = lax.broadcasted_iota(jnp.int32, (experts * IMG_ROW, experts), 0) // IMG_ROW
    column = lax.broadcasted_iota(jnp.int32, (experts * IMG_ROW, experts), 1)
    return dot((row == column).astype(full).astype(low), slots).astype(low)


def route_kernel(
    x_ref, attn_ref, proj_ref, gain_ref, slots_ref, ids_ref, cotangent_ref,
    resid_ref, second_ref, dispatch_ref, combine_ref, send_ref,
):
    length, width = x_ref.shape
    experts = slots_ref.shape[0]
    shape = (experts, IMG_ROW, length)
    resid = x_ref[...].astype(full) + dot(attn_ref[...].reshape(width, length), proj_ref[...], 0, 0)
    resid_ref[...] = resid
    normed, _ = norm_parts(resid)
    second_in = (normed * gain_ref[...]).astype(low)
    second_ref[...] = second_in
    logits = dot(slot_rows(slots_ref[...]), second_in, 1, 1).reshape(shape)
    member = member_of(ids_ref[...])
    raised = jnp.exp(logits - jnp.max(logits, axis=0, keepdims=True))
    combine = raised * (1.0 / jnp.sum(raised, axis=0, keepdims=True))
    combine_ref[...] = combine
    combine_low = jnp.where(member[None], combine, 0.0).astype(low).reshape(-1, length)
    masked = jnp.where(member[None], logits, masked_fill)
    top = jnp.max(masked, axis=2, keepdims=True)
    raised = jnp.where(member[None], jnp.exp(masked - top), 0.0)
    present = jnp.max(member.astype(full), axis=1, keepdims=True)
    total = jnp.sum(raised, axis=2, keepdims=True) + (1.0 - present)[None]
    dispatch = raised * (1.0 / total)
    dispatch_ref[...] = dispatch
    dispatch_low = dispatch.astype(low).reshape(-1, length)
    block = (send_ref.shape[0], send_ref.shape[2], width)
    send_ref[:, 0] = dot(dispatch_low, second_in).astype(low).reshape(block)
    send_ref[:, 1] = dot(combine_low, cotangent_ref[...]).astype(low).reshape(block)


def route(patches, attn, proj, gain, slots, ids, cotangent, groups):
    length, width = patches.shape
    experts = slots.shape[0]
    own = experts // groups * IMG_ROW
    return pl.pallas_call(
        route_kernel,
        in_specs=[whole_vmem] * 7,
        out_specs=[whole_vmem] * 5,
        out_shape=[
            shape_of((length, width), full),
            shape_of((length, width), low),
            shape_of((experts, IMG_ROW, length), full),
            shape_of((experts, IMG_ROW, length), full),
            shape_of((groups, 2, own, width), low),
        ],
        compiler_params=params(48),
        name="route",
    )(patches, attn, proj, gain, slots, ids, cotangent)


def own_rows(received, expert):
    groups, _, width = received.shape
    rows = received[:, expert * IMG_ROW : (expert + 1) * IMG_ROW]
    return rows.reshape(groups * IMG_ROW, width).astype(low)


def expert_kernel(received_ref, up_ref, down_ref, back_ref, stage):
    expert = pl.program_id(0)
    groups, _, own, width = received_ref.shape
    slots = received_ref[:, 0].astype(full)
    grads = received_ref[:, 1].astype(full)
    for index in range(own // IMG_ROW):

        @pl.when(expert == index)
        def _():
            up = up_ref[0]
            down = down_ref[0]
            pre = dot(own_rows(slots, index), up)
            cdf, pdf = gelu_parts(pre)
            out = dot((pre * cdf).astype(low), down)
            grad_hidden = dot(own_rows(grads, index), down, 1, 1)
            grad_pre = (grad_hidden * (cdf + pre * pdf)).astype(low)
            grad_slots = dot(grad_pre, up, 1, 1)
            rows = slice(index * IMG_ROW, (index + 1) * IMG_ROW)
            stage[0, :, rows] = out.reshape(groups, IMG_ROW, width)
            stage[1, :, rows] = grad_slots.reshape(groups, IMG_ROW, width)

    @pl.when(expert == own // IMG_ROW - 1)
    def _():
        back_ref[:, 0] = stage[0].astype(low)
        back_ref[:, 1] = stage[1].astype(low)


def run_experts(received, up, down):
    groups, _, own, width = received.shape
    experts, _, hidden = up.shape
    return pl.pallas_call(
        expert_kernel,
        grid=(experts,),
        in_specs=[
            whole_vmem,
            pl.BlockSpec((1, width, hidden), lambda expert: (expert, 0, 0)),
            pl.BlockSpec((1, hidden, width), lambda expert: (expert, 0, 0)),
        ],
        out_specs=pl.BlockSpec(received.shape, lambda expert: (0, 0, 0, 0)),
        out_shape=shape_of(received.shape, low),
        scratch_shapes=[pltpu.VMEM((2, groups, own, width), full)],
        compiler_params=params(48),
        name="run_experts",
    )(received, up, down)


def slots_back_kernel(
    back_ref, second_ref, resid_ref, dispatch_ref, combine_ref, ids_ref, cotangent_ref,
    slots_ref, gain_ref, attn_ref, proj_ref,
    output_ref, grad_resid_ref, grad_attn_ref, delta_ref, sums_ref,
):
    length, width = resid_ref.shape
    experts = slots_ref.shape[0]
    count = experts * IMG_ROW
    shape = (experts, IMG_ROW, length)
    slot_out = back_ref[:, 0].reshape(count, width)
    grad_slots = back_ref[:, 1].reshape(count, width)
    cotangent = cotangent_ref[...]
    second_in = second_ref[...]
    combine = combine_ref[...]
    dispatch = dispatch_ref[...]
    member = member_of(ids_ref[...])
    grad_combine = dot(slot_out, cotangent, 1, 1).reshape(shape)
    grad_own = jnp.sum(jnp.where(member[None], grad_combine, 0.0), axis=1, keepdims=True)
    inner = jnp.sum(combine * grad_own, axis=0, keepdims=True)
    grad_logits = combine * (grad_own - inner)
    grad_dispatch = dot(grad_slots, second_in, 1, 1).reshape(shape)
    weighted = jnp.sum(dispatch * grad_dispatch, axis=2, keepdims=True)
    routed = jnp.sum(dispatch * (grad_dispatch - weighted), axis=1, keepdims=True)
    grad_low = (grad_logits + routed).astype(low).reshape(count, length)
    row = lax.broadcasted_iota(jnp.int32, (experts, count), 0) * IMG_ROW
    column = lax.broadcasted_iota(jnp.int32, (experts, count), 1)
    grad_low = dot((row == column).astype(full).astype(low), grad_low).astype(low)
    slot_grad = dot(grad_low, second_in)
    mixing = jnp.concatenate([dispatch.astype(low).reshape(count, length), grad_low], axis=0)
    sources = jnp.concatenate([grad_slots, slots_ref[...]], axis=0)
    grad_second = dot(mixing, sources, 0, 0)
    resid = resid_ref[...]
    combine_low = jnp.where(member[None], combine, 0.0).astype(low).reshape(count, length)
    output_ref[...] = (resid + dot(combine_low, slot_out, 0, 0)).astype(low)
    normed, factor = norm_parts(resid)
    second_grad = jnp.sum(grad_second * normed, axis=0, keepdims=True)
    grad_resid = cotangent.astype(full) + norm_back(grad_second, normed, factor, gain_ref[...])
    grad_resid_ref[...] = grad_resid
    grad_branch = grad_resid.astype(low)
    attn = attn_ref[...].reshape(width, length)
    proj_grad = dot(attn, grad_branch).astype(low)
    grad_attn = dot(proj_ref[...], grad_branch, 1, 1).astype(low)
    grad_attn_ref[...] = grad_attn.reshape(grad_attn_ref.shape)
    product = grad_attn.astype(full) * attn.astype(full)
    heads = 2 * width // LANES
    delta_ref[...] = jnp.sum(product.reshape(heads, width // heads, length), axis=1)
    slot_low = slot_grad.astype(low)
    second_low = jnp.broadcast_to(second_grad, (16, width)).astype(low)
    for index in range(width // LANES):
        lanes = slice(index * LANES, (index + 1) * LANES)
        sums_ref[index * width : (index + 1) * width] = proj_grad[:, lanes]
        base = width * width // LANES + index * experts
        sums_ref[base : base + experts] = slot_low[:, lanes]
        base = (width + experts) * width // LANES + index * 16
        sums_ref[base : base + 16] = second_low[:, lanes]


def slots_back(back, second_in, resid, dispatch, combine, ids, cotangent, slots, gain, attn, proj):
    length, width = resid.shape
    experts = slots.shape[0]
    pairs = width // LANES
    return pl.pallas_call(
        slots_back_kernel,
        in_specs=[whole_vmem] * 11,
        out_specs=[whole_vmem] * 5,
        out_shape=[
            shape_of((length, width), low),
            shape_of((length, width), full),
            shape_of((pairs, LANES, length), low),
            shape_of((2 * pairs, length), full),
            shape_of(((width + experts + 16) * pairs, LANES), low),
        ],
        compiler_params=params(56),
        name="slots_back",
    )(back, second_in, resid, dispatch, combine, ids, cotangent, slots, gain, attn, proj)


def attend_back_kernel(
    first_head, probs_ref, queries_ref, keys_ref, values_ref, grad_attn_ref, delta_ref, first_ref,
    grads_ref, sums_ref, grad_scores,
):
    width, length = first_ref.shape
    half = LANES // 2
    factor = half**-0.5
    none = jnp.zeros((half, TILE), low)
    for head in range(2):
        rows = slice(head * half, (head + 1) * half)
        grad_mixed = grad_attn_ref[0, rows, :]
        delta = delta_ref[first_head + head : first_head + head + 1, :]
        for start in range(0, length, TILE):
            span = slice(start, start + TILE)
            grad = grad_mixed[:, span]
            parts = [grad, none] if head == 0 else [none, grad]
            grad_probs = dot(values_ref[0], jnp.concatenate(parts, axis=0))
            probs = probs_ref[head, :, span].astype(full)
            grad_scores[head, :, span] = (probs * (grad_probs - delta[:, span])).astype(low)
        grads_ref[2, rows, :] = dot(grad_mixed, probs_ref[head], 1, 1).astype(low)
        grads_ref[0, rows, :] = (dot(keys_ref[0, rows, :], grad_scores[head]) * factor).astype(low)
        grads_ref[1, rows, :] = (
            dot(queries_ref[0, rows, :], grad_scores[head], 1, 1) * factor
        ).astype(low)
    sums = dot(first_ref[...], grads_ref[...].reshape(3 * LANES, length), 1, 1).astype(low)
    for index in range(3):
        sums_ref[index * width : (index + 1) * width] = sums[:, index * LANES : (index + 1) * LANES]


def attend_back(pair, probs, queries, keys, values, grad_attn, delta, first_in):
    width, length = first_in.shape

    def kernel(*refs):
        attend_back_kernel(2 * pair, *refs)

    block = pl.BlockSpec((1, LANES, length), lambda _: (pair, 0, 0))
    return pl.pallas_call(
        kernel,
        grid=(1,),
        in_specs=[
            pl.BlockSpec((2, length, length), lambda _: (pair, 0, 0)),
            block,
            block,
            pl.BlockSpec((1, length, LANES), lambda _: (pair, 0, 0)),
            block,
            whole_vmem,
            whole_vmem,
        ],
        out_specs=[whole_vmem, whole_vmem],
        out_shape=[shape_of((3, LANES, length), low), shape_of((3 * width, LANES), low)],
        scratch_shapes=[pltpu.VMEM((2, length, length), low)],
        compiler_params=params(48),
        name="attend_back",
    )(probs, queries, keys, values, grad_attn, delta, first_in)


def patch_back_kernel(x_ref, gain_ref, weight_ref, resid_ref, *refs):
    pieces, result_ref = refs[:-1], refs[-1]
    grads = jnp.concatenate([piece[part] for part in range(3) for piece in pieces], axis=0)
    grad_first = dot(weight_ref[...], grads).T
    normed, factor = norm_parts(x_ref[...].astype(full))
    result_ref[...] = resid_ref[...] + norm_back(grad_first, normed, factor, gain_ref[...])


def patch_back(patches, gain, weight, grad_resid, pieces):
    return pl.pallas_call(
        patch_back_kernel,
        in_specs=[whole_vmem] * (4 + len(pieces)),
        out_specs=whole_vmem,
        out_shape=shape_of(patches.shape, full),
        compiler_params=params(48),
        name="patch_back",
    )(patches, gain, weight, grad_resid, *pieces)


def weights_kernel(copies, *refs):
    received = refs[:copies]
    up_ref, down_ref, up_grad_ref, down_grad_ref, slots, grads = refs[copies:]
    expert = pl.program_id(0)
    groups, _, own, width = received[0].shape
    count = groups * IMG_ROW
    for index in range(own // IMG_ROW):

        @pl.when(jnp.logical_and(expert == index, pl.program_id(1) == 0))
        def _():
            for copy, ref in enumerate(received):
                rows = slice(copy * count, (copy + 1) * count)
                slots[rows] = own_rows(ref[:, 0].astype(full), index)
                grads[rows] = own_rows(ref[:, 1].astype(full), index)

    pre = dot(slots[...], up_ref[0])
    cdf, pdf = gelu_parts(pre)
    down_grad_ref[0] = dot((pre * cdf).astype(low), grads[...], 0, 0)
    grad_hidden = dot(grads[...], down_ref[0], 1, 1)
    grad_pre = (grad_hidden * (cdf + pre * pdf)).astype(low)
    up_grad_ref[0] = dot(slots[...], grad_pre, 0, 0)


def weight_grads(received, up, down):
    groups, _, _, width = received[0].shape
    experts, _, hidden = up.shape
    copies = len(received)
    tile = hidden // 3
    up_spec = pl.BlockSpec((1, width, tile), lambda expert, step: (expert, 0, step))
    down_spec = pl.BlockSpec((1, tile, width), lambda expert, step: (expert, step, 0))
    rows = (copies * groups * IMG_ROW, width)

    def kernel(*refs):
        weights_kernel(copies, *refs)

    return pl.pallas_call(
        kernel,
        grid=(experts, 3),
        in_specs=[whole_vmem] * copies + [up_spec, down_spec],
        out_specs=[up_spec, down_spec],
        out_shape=[shape_of(up.shape, full), shape_of(down.shape, full)],
        scratch_shapes=[pltpu.VMEM(rows, low)] * 2,
        compiler_params=params(48),
        name="weight_grads",
    )(*received, up, down)


def add_kernel(terms_ref, sums_ref):
    sums = jnp.sum(terms_ref[...].astype(full), axis=0).astype(low)
    sums_ref[...] = jnp.broadcast_to(sums[None], sums_ref.shape)


def add_terms(terms):
    return pl.pallas_call(
        add_kernel,
        in_specs=[whole_vmem],
        out_specs=whole_vmem,
        out_shape=shape_of(terms.shape, low),
        compiler_params=params(32),
        name="add_terms",
    )(terms)


def finish_kernel(
    total, place_ref, sums_ref, weight_ref, gain_ref,
    first_ref, qkv_ref, proj_ref, second_ref, slot_ref,
):
    width = weight_ref.shape[0]
    pairs = width // LANES
    own = slot_ref.shape[1]
    rows = sums_ref.shape[0] * sums_ref.shape[1]
    sums = sums_ref[...].reshape(rows, LANES)
    base = (width + total + 16) * pairs
    for index in range(pairs):
        lanes = slice(index * LANES, (index + 1) * LANES)
        proj_ref[:, lanes] = sums[index * width : (index + 1) * width].astype(full)
        start = (width + total) * pairs + index * 16
        second_ref[:, lanes] = sums[start : start + 1].astype(full)
        start = width * pairs + index * total
        block = sums[start : start + total]
        row = lax.broadcasted_iota(jnp.int32, (total, own), 0)
        column = lax.broadcasted_iota(jnp.int32, (total, own), 1) + place_ref[0] * own
        slot_ref[lanes, :] = dot(block, (row == column).astype(full).astype(low), 0, 0)
    first = jnp.zeros((width, 1), full)
    for pair in range(pairs):
        for part in range(3):
            lanes = slice(part * width + pair * LANES, part * width + (pair + 1) * LANES)
            start = base + (pair * 3 + part) * width
            grad = sums[start : start + width].astype(full)
            qkv_ref[:, lanes] = grad
            product = grad * weight_ref[:, lanes].astype(full)
            first = first + jnp.sum(product, axis=1, keepdims=True)
    first_ref[...] = jnp.broadcast_to(first, (width, LANES)).T[0:1] / gain_ref[...]


def finish(place, sums, weight, gain, experts, own):
    width = weight.shape[0]

    def kernel(*refs):
        finish_kernel(experts, *refs)

    return pl.pallas_call(
        kernel,
        in_specs=[pl.BlockSpec(memory_space=pltpu.SMEM)] + [whole_vmem] * 3,
        out_specs=[whole_vmem] * 5,
        out_shape=[
            shape_of((1, width), full),
            shape_of(weight.shape, full),
            shape_of((width, width), full),
            shape_of((1, width), full),
            shape_of((width, own), full),
        ],
        compiler_params=params(48),
        name="finish",
    )(place, sums, weight, gain)


def per_device(
    patches,
    image_ids,
    first_gain,
    qkv_weight,
    proj_weight,
    second_gain,
    slot_params,
    up_weight,
    down_weight,
    cotangent,
):
    groups = lax.axis_size("expert")
    copies = lax.axis_size("rows")
    devices = groups * copies
    _, length, width = patches.shape
    own = slot_params.shape[1]
    experts = own * groups
    spread = jnp.broadcast_to(slot_params.T[None], (groups, own, width))
    slots = lax.all_to_all(spread, "expert", 0, 0, tiled=True).reshape(experts, width)
    patches = patches[0]
    cotangent = cotangent[0]
    first_gain = first_gain[None]
    second_gain = second_gain[None]
    probs, attn, queries, keys, values, first_in = attend(
        patches, image_ids, first_gain, qkv_weight
    )
    resid, second_in, dispatch, combine, send = route(
        patches, attn, proj_weight, second_gain, slots, image_ids, cotangent, groups
    )
    received = lax.all_to_all(send, "expert", 0, 0, tiled=True)
    back = run_experts(received, up_weight, down_weight)
    back = lax.all_to_all(back, "expert", 0, 0, tiled=True)
    others = [
        lax.ppermute(received, "rows", [(place, place ^ step) for place in range(copies)])
        for step in range(1, copies)
    ]
    output, grad_resid, grad_attn, delta, sums = slots_back(
        back, second_in, resid, dispatch, combine, image_ids, cotangent,
        slots, second_gain, attn, proj_weight,
    )
    pieces = []
    bundle = [sums]
    for pair in range(width // LANES):
        grads, sums = attend_back(
            pair, probs, queries, keys, values, grad_attn, delta, first_in
        )
        pieces.append(grads)
        bundle.append(sums)
    patch_grad = patch_back(patches, first_gain, qkv_weight, grad_resid, pieces)
    up_grad, down_grad = weight_grads([received] + others, up_weight, down_weight)
    count = sum(piece.shape[0] for piece in bundle)
    share = -(-count // (16 * devices)) * 16
    bundle.append(jnp.zeros((share * devices - count, LANES), low))
    terms = jnp.concatenate(bundle, axis=0).reshape(devices, share, LANES)
    terms = lax.all_to_all(terms, both_axes, 0, 0, tiled=True)
    sums = lax.all_to_all(add_terms(terms), both_axes, 0, 0, tiled=True)
    place = lax.axis_index("expert").astype(jnp.int32).reshape(1)
    first_grad, qkv_grad, proj_grad, second_grad, slot_grad = finish(
        place, sums, qkv_weight, first_gain, experts, own
    )
    return (
        output[None],
        patch_grad[None],
        first_grad[0],
        qkv_grad,
        proj_grad,
        second_grad[0],
        slot_grad,
        up_grad,
        down_grad,
    )


def solution(mesh):
    return jax.shard_map(
        per_device,
        mesh=mesh,
        in_specs=(
            P(("expert", "rows"), None, None),
            P(("expert", "rows"), None),
            P(),
            P(),
            P(),
            P(),
            P(None, "expert"),
            P("expert", None, None),
            P("expert", None, None),
            P(("expert", "rows"), None, None),
        ),
        out_specs=(
            P(("expert", "rows"), None, None),
            P(("expert", "rows"), None, None),
            P(),
            P(),
            P(),
            P(),
            P(None, "expert"),
            P("expert", None, None),
            P("expert", None, None),
        ),
        check_vma=False,
    )
```

time: 408 us -> 195 us (0.48); the launches traced: 403 us -> 194 us
  matrix products: 84.3 us -> 0 us
  Pallas kernels: 0 us -> 71.9 us
  waiting for transfers between devices: 89.5 us -> 19.1 us
  blocking collectives: 116 us -> 60.1 us
  other arithmetic: 39.1 us -> 1.19 us
  local copies, waits for them, and re-layouts: 46.4 us -> 28.3 us
  between operations: 15.7 us -> 0.92 us
    dot_general x35 -> x0, matrix products: 84.3 us -> none  [the longest x2 14.4 us: one_block(): jnp.einsum('qhd,khd->hqk', grad_block, values, preferred_element_type=jnp...]
    psum x2 -> x0, waiting for transfers between devices: 80.1 us -> none  [the longest x1 80.1 us: per_device(): lax.psum((first_local, qkv_local, proj_local, second_local), ('expert', '...]
    pallas_call x0 -> x11, Pallas kernels: none -> 71.9 us  [the longest x1 25.2 us: attend(): pl.pallas_call(attend_kernel, grid=(pairs,), in_specs=[whole_vmem] * 4, o...]
    all_to_all x1 -> x3, blocking collectives: 10.8 us -> 60.1 us  [the longest x1 35.7 us: per_device(): terms = lax.all_to_all(terms, both_axes, 0, 0, tiled=True)]
    psum x2 -> x0, blocking collectives: 42.7 us -> none  [the longest x1 36.9 us: per_device(): lax.psum((first_local, qkv_local, proj_local, second_local), ('expert', '...]
    unnamed x1 -> x0, blocking collectives: 34.7 us -> none
    all_gather x1 -> x0, blocking collectives: 27.8 us -> none  [per_device(): slot_full = lax.all_gather(slot_params, 'expert', axis=1, tiled=True)]
    convert_element_type x7 -> x0, other arithmetic: 22.5 us -> none  [the longest x2 14.5 us: one_block(): grad_scores = (probs * (grad_probs - jnp.sum(probs * grad_probs, axis=-1,...]
  transfers between devices with their start and end apart: 5 -> 5, of which waited for: 4 -> 2; matrix products, arithmetic and copies ran while one was open for 23% -> 1% of each run, Pallas kernels for 0% -> 18%
where the time goes in v1:
time: 195 us; the launch traced here: 194 us
  Pallas kernels  71.9 us (37%)
  blocking collectives  60.1 us (31%)
  local copies, waits for them, and re-layouts  28.3 us (15%)
  waiting for transfers between devices  19.1 us (10%)
  starting transfers between devices  12.6 us (6%)
    all_to_all x1, blocking collectives, per_device(): terms = lax.all_to_all(terms, both_axes, 0, 0, tiled=True)  35.7 us
    unnamed x89, local copies, waits for them, and re-layouts  25.6 us
    pallas_call x1, Pallas kernels, attend(): pl.pallas_call(attend_kernel, grid=(pairs,), in_specs=[whole_vmem] * 4, o...  25.2 us
    pallas_call x3, Pallas kernels, attend_back(): pl.pallas_call(kernel, grid=(1,), in_specs=[pl.BlockSpec((2, length, leng...  20.7 us
    ppermute x3, waiting for transfers between devices, per_device(): lax.ppermute(received, 'rows', [(place, place ^ step) for place in range(...  19.1 us
    all_to_all x1, blocking collectives, per_device(): received = lax.all_to_all(send, 'expert', 0, 0, tiled=True)  13.6 us
    all_to_all x1, blocking collectives, per_device(): back = lax.all_to_all(back, 'expert', 0, 0, tiled=True)  10.8 us
    pallas_call x1, Pallas kernels, weight_grads(): pl.pallas_call(kernel, grid=(experts, 3), in_specs=[whole_vmem] * copies...  7.28 us
  transfers between devices with their start and end apart: 5, of which 2 were waited for; matrix products, arithmetic and copies ran while one was open for 1% of the time, Pallas kernels for 18%

profile of v1, /device:TPU:0, one launch (start us, length us, event | category | flops | bytes accessed | tf_op | source)
XLA Modules:
  0.0 194.1 jit_solution(13982779330387011794)
XLA Ops:
  0.6 0.0 copy-start.39
  0.7 1.3 broadcast_in_dim.23
  1.9 7.3 %all-to-all-start = ((bf16[8,2,384]{2,1,0:T(2,128)(2,1)}), bf16[8,2,384]{2,1,0:T(2,128)(2,1)S(1)}, u32[]{:S(2)}, u32[]{:S(2)}) async-start(bf16[8,2,384]{2,1,0:T(2,128)(2,1)} %broadcast_in_dim.23), calls=%async_computation | async-start | bytes 24576 | tf_op jit(solution)/shard_map/all_to_all | solution.py:542
  9.2 0.7 broadcast_in_dim.21.gain_ref.refs_3_
  9.9 0.7 broadcast_in_dim.22.gain_ref
  10.6 1.2 copy-done.3
  11.7 1.1 copy-done.12
  12.9 0.7 copy-done.38
  13.6 25.2 %attend.1 = (bf16[6,1024,1024]{2,1,0:T(8,128)(2,1)}, bf16[3,128,1024]{2,1,0:T(8,128)(2,1)S(1)}, bf16[3,128,1024]{2,1,0:T(8,128)(2,1)S(1)}, bf16[3,128,1024]{2,1,...) custom-call(bf16[1024,384]{1,0:T(8,128)(2,1)S(1)} %bitcast.7, ...), custom_call_target="tpu_custom_call" | custom-call | tf_op jit(solution)/shard_map/attend/pallas_call | solution.py:113
  38.7 0.9 copy-done.5
  39.6 0.9 copy-done.7
  40.5 0.9 copy-done.9
  41.4 0.9 copy-done.17
  42.3 0.0 all-to-all-done
  42.3 0.0 copy-done.39
  42.3 0.0 copy-done.20
  42.3 0.0 copy-start.13
  42.3 1.1 copy-done.13
  43.5 1.1 copy-done.16
  44.6 1.1 copy-done.18
  45.7 2.9 %route.1 = (f32[1024,384]{1,0:T(8,128)}, bf16[1024,384]{1,0:T(8,128)(2,1)S(1)}, f32[16,8,1024]{2,1,0:T(8,128)S(1)}, f32[16,8,1024]{2,1,0:T(8,128)S(1)}, bf16[8,2,16,384]{3,2,1,0:T(8,128)(2,1)S(1)}) custom-call(bf16[1024,384]{1,0:T(8,128)(2,1)S(1)} %bitcast.8, bf16[3,128,1024]{2,1,0:T(8,128)(2,1)S(1)} %copy-done.18, bf16[384,384]{1,0:T(8,128)(2,1)S(1)} %copy-done.20, ...), custom_call_target="tpu_custom_call" | custom-call | tf_op jit(solution)/shard_map/route/pallas_call | solution.py:186
  48.6 0.9 copy-done.21
  49.5 13.6 %all_to_all.25.received_ref.refs_0_ = bf16[8,2,16,384]{3,2,1,0:T(8,128)(2,1)S(1)} all-to-all(bf16[8,2,16,384]{3,2,1,0:T(8,128)(2,1)S(1)} %get-tuple-element.39), channel_id=1, replica_groups=mesh['expert'=8,'rows'=4] {'expert'}, dimensions={0} | all-to-all | bytes 393216 | tf_op jit(solution)/shard_map/all_to_all | solution.py:553
  63.1 1.7 copy-done.1
  64.7 2.7 %run_experts.1 = bf16[8,2,16,384]{3,2,1,0:T(8,128)(2,1)S(1)} custom-call(bf16[8,2,16,384]{3,2,1,0:T(8,128)(2,1)S(1)} %all_to_all.25.received_ref.refs_0_, bf16[2,384,1536]{2,1,0:T(8,128)(2,1)S(1)} %copy-done, bf16[2,1536,384]{2,1,0:T(8,128)(2,1)S(1)} %copy-done.1), custom_call_target="tpu_custom_call" | custom-call | tf_op jit(solution)/shard_map/run_experts/pallas_call | solution.py:238
  67.5 10.8 %all_to_all.26.back_ref = bf16[8,2,16,384]{3,2,1,0:T(8,128)(2,1)} all-to-all(bf16[8,2,16,384]{3,2,1,0:T(8,128)(2,1)S(1)} %run_experts.1), channel_id=1, replica_groups=mesh['expert'=8,'rows'=4] {'expert'}, dimensions={0} | all-to-all | bytes 393216 | tf_op jit(solution)/shard_map/all_to_all | solution.py:555
  78.3 6.8 %slots_back.1 = (bf16[1024,384]{1,0:T(8,128)(2,1)}, f32[1024,384]{1,0:T(8,128)}, bf16[3,128,1024]{2,1,0:T(8,128)(2,1)}, f32[6,1024]{1,0:T(8,128)}, bf16[1248,128]{1,0:T(8,128)(2,1)}) custom-call(bf16[8,2,16,384]{3,2,1,0:T(8,128)(2,1)} %all_to_all.26.back_ref, bf16[1024,384]{1,0:T(8,128)(2,1)} %copy-done.21, f32[1024,384]{1,0:T(8,128)} %get-tuple-element.41.resid_ref, ...), custom_call_target="tpu_custom_call" | custom-call | tf_op jit(solution)/shard_map/slots_back/pallas_call | solution.py:315
  85.1 0.0 copy-done.10
  85.2 0.0 copy-start.11
  85.2 1.1 copy-done.11
  86.3 0.8 copy-done.30
  87.1 6.8 %attend_back.3 = (bf16[3,128,1024]{2,1,0:T(8,128)(2,1)S(1)}, bf16[1152,128]{1,0:T(8,128)(2,1)S(1)}) custom-call(bf16[6,1024,1024]{2,1,0:T(8,128)(2,1)} %get-tuple-element.46.refs_0_, bf16[3,128,1024]{2,1,0:T(8,128)(2,1)S(1)} %get-tuple-element.47.refs_1_, bf16[3,128,1024]{2,1,0:T(8,128)(2,1)S(1)} %copy-done.6, bf16[3,1024,128]{2,1,0:T(8,128)(2,1)S(1)} %copy-done.8, ...), custom_call_target="tpu_custom_call" | custom-call | tf_op jit(solution)/shard_map/attend_back/pallas_call | solution.py:367
  93.9 0.0 copy-start.22
  93.9 0.9 copy-done.22
  94.8 6.8 %attend_back.4 = (bf16[3,128,1024]{2,1,0:T(8,128)(2,1)S(1)}, bf16[1152,128]{1,0:T(8,128)(2,1)S(1)}) custom-call(bf16[6,1024,1024]{2,1,0:T(8,128)(2,1)} %get-tuple-element.46.refs_0_, bf16[3,128,1024]{2,1,0:T(8,128)(2,1)S(1)} %get-tuple-element.47.refs_1_, bf16[3,128,1024]{2,1,0:T(8,128)(2,1)S(1)} %copy-done.6, bf16[3,1024,128]{2,1,0:T(8,128)(2,1)S(1)} %copy-done.8, ...), custom_call_target="tpu_custom_call" | custom-call | tf_op jit(solution)/shard_map/attend_back/pallas_call | solution.py:367
  101.6 0.9 copy-done.24
  102.5 7.1 %attend_back.5 = (bf16[3,128,1024]{2,1,0:T(8,128)(2,1)S(1)}, bf16[1152,128]{1,0:T(8,128)(2,1)S(1)}) custom-call(bf16[6,1024,1024]{2,1,0:T(8,128)(2,1)} %get-tuple-element.46.refs_0_, bf16[3,128,1024]{2,1,0:T(8,128)(2,1)S(1)} %get-tuple-element.47.refs_1_, bf16[3,128,1024]{2,1,0:T(8,128)(2,1)S(1)} %copy-done.6, bf16[3,1024,128]{2,1,0:T(8,128)(2,1)S(1)} %copy-done.8, ...), custom_call_target="tpu_custom_call" | custom-call | tf_op jit(solution)/shard_map/attend_back/pallas_call | solution.py:367
  109.5 0.0 copy-start.26
  109.5 0.0 copy-done.41
  109.7 35.7 %all_to_all.27.terms_ref = bf16[32,160,128]{2,1,0:T(8,128)(2,1)S(1)} all-to-all(bf16[32,160,128]{2,1,0:T(8,128)(2,1)S(1)} %bitcast.12), channel_id=1, replica_groups=mesh['expert'=8,'rows'=4] {'expert','rows'}, dimensions={0} | all-to-all | bytes 2621440 | tf_op jit(solution)/shard_map/all_to_all | solution.py:578
  145.4 0.2 add_terms.1
  145.6 1.0 copy-done.15
  146.7 3.4 %all-to-all-start.4 = ((bf16[32,160,128]{2,1,0:T(8,128)(2,1)}), bf16[32,160,128]{2,1,0:T(8,128)(2,1)}, u32[]{:S(2)}, u32[]{:S(2)}) async-start(bf16[32,160,128]{2,1,0:T(8,128)(2,1)} %copy-done.15), calls=%async_computation.4 | async-start | bytes 2621440 | tf_op jit(solution)/shard_map/all_to_all | solution.py:579
  150.1 0.1 collective-permute-start
  150.2 1.7 collective-permute-start.1
  151.9 0.1 collective-permute-start.2
  152.0 0.0 collective-permute-done.refs_1_
  152.0 0.7 copy-done.31
  152.7 15.7 %collective-permute-done.1.refs_2_ = bf16[8,2,16,384]{3,2,1,0:T(8,128)(2,1)S(1)} collective-permute-done((bf16[8,2,16,384]{3,2,1,0:T(8,128)(2,1)S(1)}, bf16[8,2,16,384]{3,2,1,0:T(8,128)(2,1)S(1)}, u32[]{:S(2)}, u32[]{:S(2)}) %collective-permute-start.1) | collective-permute-done | bytes 196640 | tf_op jit(solution)/shard_map/ppermute | solution.py:557
  168.4 0.7 copy-done.33
  169.1 3.5 %collective-permute-done.2.refs_3_ = bf16[8,2,16,384]{3,2,1,0:T(8,128)(2,1)S(1)} collective-permute-done((bf16[8,2,16,384]{3,2,1,0:T(8,128)(2,1)S(1)}, bf16[8,2,16,384]{3,2,1,0:T(8,128)(2,1)S(1)}, u32[]{:S(2)}, u32[]{:S(2)}) %collective-permute-start.2) | collective-permute-done | bytes 196640 | tf_op jit(solution)/shard_map/ppermute | solution.py:557
  172.5 0.7 copy-done.35
  173.2 1.7 copy-done.2
  174.9 0.9 copy-done.32
  175.8 0.9 copy-done.34
  176.7 0.9 copy-done.36
  177.7 7.3 %weight_grads.1 = (f32[2,384,1536]{2,1,0:T(8,128)}, f32[2,1536,384]{2,1,0:T(8,128)}) custom-call(bf16[8,2,16,384]{3,2,1,0:T(8,128)(2,1)S(1)} %all_to_all.25.received_ref.refs_0_, bf16[8,2,16,384]{3,2,1,0:T(8,128)(2,1)S(1)} %copy-done.32, bf16[8,2,16,384]{3,2,1,0:T(8,128)(2,1)S(1)} %copy-done.34, bf16[8,2,16,384]{3,2,1,0:T(8,128)(2,1)S(1)} %copy-done.36, ...), custom_call_target="tpu_custom_call" | custom-call | tf_op jit(solution)/shard_map/weight_grads/pallas_call | solution.py:441
  185.0 1.1 copy-done.27
  186.1 2.9 %patch_back.1 = f32[1024,384]{1,0:T(8,128)} custom-call(bf16[1024,384]{1,0:T(8,128)(2,1)S(1)} %bitcast.9, f32[1,384]{1,0:T(1,128)S(1)} %broadcast_in_dim.21.gain_ref.refs_3_, bf16[384,1152]{1,0:T(8,128)(2,1)S(1)} %copy-done.4, f32[1024,384]{1,0:T(8,128)S(1)} %copy-done.19, bf16[3,128,1024]{2,1,0:T(8,128)(2,1)S(1)} %copy-done.23, ...), custom_call_target="tpu_custom_call" | custom-call | tf_op jit(solution)/shard_map/patch_back/pallas_call | solution.py:396
  189.1 0.0 all-to-all-done.4.refs_1_
  189.1 3.2 %finish.1 = (f32[1,384]{1,0:T(1,128)S(1)}, f32[384,1152]{1,0:T(8,128)}, f32[384,384]{1,0:T(8,128)}, f32[1,384]{1,0:T(1,128)S(1)}, f32[384,2]{1,0:T(8,128)S(1)}) custom-call(s32[1]{0:T(128)} %bitcast.5.refs_0_, bf16[32,160,128]{2,1,0:T(8,128)(2,1)} %all-to-all-done.4.refs_1_, bf16[384,1152]{1,0:T(8,128)(2,1)S(1)} %copy-done.4, ...), custom_call_target="tpu_custom_call" | custom-call | tf_op jit(solution)/shard_map/finish/pallas_call | solution.py:507
  192.3 0.6 reduce
  192.9 0.6 reduce.1
  193.5 0.7 copy.19
  (56 shorter events, 0.3 us)
Async XLA Ops:
  0.6 41.7 %copy-start.39 = (s32[1,1024]{1,0:T(1,128)S(1)}, s32[1,1024]{1,0:T(1,128)}, u32[]{:S(2)}) copy-start(s32[1,1024]{1,0:T(1,128)} %ids_ref.5) | copy-start | bytes 12292
  1.9 40.3 %all-to-all-start = ((bf16[8,2,384]{2,1,0:T(2,128)(2,1)}), bf16[8,2,384]{2,1,0:T(2,128)(2,1)S(1)}, u32[]{:S(2)}, u32[]{:S(2)}) async-start(bf16[8,2,384]{2,1,0:T(2,128)(2,1)} %broadcast_in_dim.23), calls=%async_computation | async-start | bytes 24576 | tf_op jit(solution)/shard_map/all_to_all | solution.py:542
  10.6 38.0 %copy-start.40 = (f32[1,384]{1,0:T(1,128)}, f32[1,384]{1,0:T(1,128)S(1)}, u32[]{:S(2)}) copy-start(f32[1,384]{1,0:T(1,128)S(1)} %broadcast_in_dim.22.gain_ref) | copy-start | bytes 4612
  10.6 1.2 copy-start.3
  11.7 1.1 copy-start.12
  12.9 0.7 copy-start.38
  13.6 28.7 %copy-start.20 = (bf16[384,384]{1,0:T(8,128)(2,1)S(1)}, bf16[384,384]{1,0:T(8,128)(2,1)}, u32[]{:S(2)}) copy-start(bf16[384,384]{1,0:T(8,128)(2,1)} %proj_ref.3) | copy-start | bytes 884740
  38.7 0.9 copy-start.5
  39.6 0.9 copy-start.7
  40.5 0.9 copy-start.9
  41.4 0.9 copy-start.17
  42.3 6.3 %copy-start.37 = (bf16[16,384]{1,0:T(8,128)(2,1)}, bf16[16,384]{1,0:T(8,128)(2,1)S(1)}, u32[]{:S(2)}) copy-start(bf16[16,384]{1,0:T(8,128)(2,1)S(1)} %reshape.28.slots_ref) | copy-start | bytes 36868
  42.3 1.1 copy-start.13
  43.5 1.1 copy-start.16
  44.6 1.1 copy-start.18
  45.7 17.3 %copy-start = (bf16[2,384,1536]{2,1,0:T(8,128)(2,1)S(1)}, bf16[2,384,1536]{2,1,0:T(8,128)(2,1)}, u32[]{:S(2)}) copy-start(bf16[2,384,1536]{2,1,0:T(8,128)(2,1)} %refs_4_.1) | copy-start | bytes 7077892
  48.6 0.9 copy-start.21
  49.5 17.9 %copy-start.28 = (f32[16,8,1024]{2,1,0:T(8,128)}, f32[16,8,1024]{2,1,0:T(8,128)S(1)}, u32[]{:S(2)}) copy-start(f32[16,8,1024]{2,1,0:T(8,128)S(1)} %get-tuple-element.42.dispatch_ref) | copy-start | bytes 1572868
  49.5 17.9 %copy-start.29 = (f32[16,8,1024]{2,1,0:T(8,128)}, f32[16,8,1024]{2,1,0:T(8,128)S(1)}, u32[]{:S(2)}) copy-start(f32[16,8,1024]{2,1,0:T(8,128)S(1)} %get-tuple-element.43.combine_ref) | copy-start | bytes 1572868
  63.1 1.7 copy-start.1
  78.3 6.8 %copy-start.6 = (bf16[3,128,1024]{2,1,0:T(8,128)(2,1)S(1)}, bf16[3,128,1024]{2,1,0:T(8,128)(2,1)}, u32[]{:S(2)}) copy-start(bf16[3,128,1024]{2,1,0:T(8,128)(2,1)} %copy-done.5) | copy-start | bytes 2359300
  78.3 6.8 %copy-start.8 = (bf16[3,1024,128]{2,1,0:T(8,128)(2,1)S(1)}, bf16[3,1024,128]{2,1,0:T(8,128)(2,1)}, u32[]{:S(2)}) copy-start(bf16[3,1024,128]{2,1,0:T(8,128)(2,1)} %copy-done.7) | copy-start | bytes 2359300
  78.3 6.8 %copy-start.10 = (bf16[384,1024]{1,0:T(8,128)(2,1)S(1)}, bf16[384,1024]{1,0:T(8,128)(2,1)}, u32[]{:S(2)}) copy-start(bf16[384,1024]{1,0:T(8,128)(2,1)} %copy-done.9) | copy-start | bytes 2359300
  85.2 1.1 copy-start.11
  86.3 0.8 copy-start.30
  93.9 0.9 copy-start.22
  101.6 0.9 copy-start.24
  102.5 7.1 %copy-start.41 = (bf16[1248,128]{1,0:T(8,128)(2,1)S(1)}, bf16[1248,128]{1,0:T(8,128)(2,1)}, u32[]{:S(2)}) copy-start(bf16[1248,128]{1,0:T(8,128)(2,1)} %get-tuple-element.56) | copy-start | bytes 958468
  109.5 35.9 %copy-start.26 = (bf16[3,128,1024]{2,1,0:T(8,128)(2,1)}, bf16[3,128,1024]{2,1,0:T(8,128)(2,1)S(1)}, u32[]{:S(2)}) copy-start(bf16[3,128,1024]{2,1,0:T(8,128)(2,1)S(1)} %get-tuple-element.55.refs_2_) | copy-start | bytes 2359300
  145.6 1.1 copy-start.15
  146.7 42.4 %all-to-all-start.4 = ((bf16[32,160,128]{2,1,0:T(8,128)(2,1)}), bf16[32,160,128]{2,1,0:T(8,128)(2,1)}, u32[]{:S(2)}, u32[]{:S(2)}) async-start(bf16[32,160,128]{2,1,0:T(8,128)(2,1)} %copy-done.15), calls=%async_computation.4 | async-start | bytes 2621440 | tf_op jit(solution)/shard_map/all_to_all | solution.py:579
  150.1 1.9 %collective-permute-start = (bf16[8,2,16,384]{3,2,1,0:T(8,128)(2,1)S(1)}, bf16[8,2,16,384]{3,2,1,0:T(8,128)(2,1)S(1)}, u32[]{:S(2)}, u32[]{:S(2)}) collective-permute-start(bf16[8,2,16,384]{3,2,1,0:T(8,128)(2,1)S(1)} %all_to_all.25.received_ref.refs_0_), channel_id=1, source_target_pairs={{0,1},{1,0},{2,3},{3,2},{4,5},{5,4},{6,7},{7,6},{8,9},{9,8},{10,11... | collective-permute-start | bytes 589832 | tf_op jit(solution)/shard_map/ppermute | solution.py:557
  150.2 18.2 %collective-permute-start.1 = (bf16[8,2,16,384]{3,2,1,0:T(8,128)(2,1)S(1)}, bf16[8,2,16,384]{3,2,1,0:T(8,128)(2,1)S(1)}, u32[]{:S(2)}, u32[]{:S(2)}) collective-permute-start(bf16[8,2,16,384]{3,2,1,0:T(8,128)(2,1)S(1)} %all_to_all.25.received_ref.refs_0_), channel_id=1, source_target_pairs={{0,2},{1,3},{2,0},{3,1},{4,6},{5,7},{6,4},{7,5},{8,10},{9,11},{10,... | collective-permute-start | bytes 589832 | tf_op jit(solution)/shard_map/ppermute | solution.py:557
  151.9 20.6 %collective-permute-start.2 = (bf16[8,2,16,384]{3,2,1,0:T(8,128)(2,1)S(1)}, bf16[8,2,16,384]{3,2,1,0:T(8,128)(2,1)S(1)}, u32[]{:S(2)}, u32[]{:S(2)}) collective-permute-start(bf16[8,2,16,384]{3,2,1,0:T(8,128)(2,1)S(1)} %all_to_all.25.received_ref.refs_0_), channel_id=1, source_target_pairs={{0,3},{1,2},{2,1},{3,0},{4,7},{5,6},{6,5},{7,4},{8,11},{9,10},{10,... | collective-permute-start | bytes 589832 | tf_op jit(solution)/shard_map/ppermute | solution.py:557
  152.0 0.7 copy-start.31
  168.4 0.7 copy-start.33
  172.5 0.7 copy-start.35
  173.2 1.7 copy-start.2
  174.9 0.9 copy-start.32
  175.8 0.9 copy-start.34
  176.7 0.9 copy-start.36
  177.6 7.3 %copy-start.4 = (bf16[384,1152]{1,0:T(8,128)(2,1)S(1)}, bf16[384,1152]{1,0:T(8,128)(2,1)}, u32[]{:S(2)}) copy-start(bf16[384,1152]{1,0:T(8,128)(2,1)} %refs_2_.1) | copy-start | bytes 2654212
  177.6 7.3 %copy-start.14 = (bf16[1,1024,384]{2,1,0:T(8,128)(2,1)S(1)}, bf16[1,1024,384]{2,1,0:T(8,128)(2,1)}, u32[]{:S(2)}) copy-start(bf16[1,1024,384]{2,1,0:T(8,128)(2,1)} %param.10) | copy-start | bytes 2359300
  177.6 7.3 %copy-start.19 = (f32[1024,384]{1,0:T(8,128)S(1)}, f32[1024,384]{1,0:T(8,128)}, u32[]{:S(2)}) copy-start(f32[1024,384]{1,0:T(8,128)} %get-tuple-element.45.resid_ref) | copy-start | bytes 4718596
  177.7 7.3 %copy-start.23 = (bf16[3,128,1024]{2,1,0:T(8,128)(2,1)S(1)}, bf16[3,128,1024]{2,1,0:T(8,128)(2,1)}, u32[]{:S(2)}) copy-start(bf16[3,128,1024]{2,1,0:T(8,128)(2,1)} %copy-done.22) | copy-start | bytes 2359300
  177.7 7.3 %copy-start.25 = (bf16[3,128,1024]{2,1,0:T(8,128)(2,1)S(1)}, bf16[3,128,1024]{2,1,0:T(8,128)(2,1)}, u32[]{:S(2)}) copy-start(bf16[3,128,1024]{2,1,0:T(8,128)(2,1)} %copy-done.24) | copy-start | bytes 2359300
  185.0 1.1 copy-start.27

commit v2 on v1

v2 whole, which is shorter than its diff:
```python
import jax
import jax.numpy as jnp
from jax import lax
from jax.experimental import pallas as pl
from jax.experimental.pallas import tpu as pltpu
from jax.sharding import PartitionSpec as P

HEADS = 6
IMG_ROW = 8
LANES = 128
TILE = 256

epsilon = 1e-06
masked_fill = -1e30
score_bound = 64.0
log2_e = 1.4426950408889634
low = jnp.bfloat16
full = jnp.float32
whole_vmem = pl.BlockSpec(memory_space=pltpu.VMEM)
anywhere = pl.BlockSpec(memory_space=pl.ANY)
both_axes = ("expert", "rows")


def dot(left, right, left_dim=1, right_dim=0):
    return lax.dot_general(
        left, right, (((left_dim,), (right_dim,)), ((), ())), preferred_element_type=full
    )


def shape_of(shape, dtype):
    return jax.ShapeDtypeStruct(shape, dtype)


def kept(shape, dtype):
    return pltpu.HBM(shape, dtype)


def keep(*arrays):
    return [pltpu.with_memory_space_constraint(array, pltpu.HBM) for array in arrays]


def params(mib):
    return pltpu.CompilerParams(vmem_limit_bytes=mib << 20)


def cost(microseconds):
    return pl.CostEstimate(
        flops=0, transcendentals=0, bytes_accessed=int(microseconds * 3.6e6)
    )


def norm_parts(values):
    centred = values - jnp.mean(values, axis=-1, keepdims=True)
    factor = lax.rsqrt(jnp.mean(centred * centred, axis=-1, keepdims=True) + epsilon)
    return centred * factor, factor


def norm_back(grad_norm, normed, factor, gain):
    scaled = grad_norm * gain
    return factor * (
        scaled
        - jnp.mean(scaled, axis=-1, keepdims=True)
        - normed * jnp.mean(scaled * normed, axis=-1, keepdims=True)
    )


def member_of(ids):
    images = lax.broadcasted_iota(jnp.int32, (IMG_ROW, ids.shape[1]), 0)
    return images == ids


def gelu_parts(pre):
    cdf = 0.5 * (1.0 + lax.erf(pre * 0.7071067811865476))
    pdf = 0.3989422804014327 * jnp.exp(-0.5 * pre * pre)
    return cdf, pdf


def attend_kernel(
    x_ref, ids_ref, gain_ref, weight_ref,
    probs_ref, attn_ref, inverse_ref, queries_out, keys_out, value_rows_out, first_out,
    queries_ref, keys_ref, value_rows_ref, first_ref,
    key_rows, values, mask_rows, same, bound, semaphores,
):
    pair = pl.program_id(0)
    length, width = x_ref.shape
    pairs = width // LANES
    half = LANES // 2
    saves = [
        pltpu.make_async_copy(source, target, semaphores.at[index])
        for index, (source, target) in enumerate(
            [
                (queries_ref, queries_out),
                (keys_ref, keys_out),
                (value_rows_ref, value_rows_out),
                (first_ref, first_out),
            ]
        )
    ]

    @pl.when(pair == 0)
    def _():
        normed, _ = norm_parts(x_ref[...].astype(full))
        first_in = (normed * gain_ref[...].reshape(1, width)).astype(low)
        first_ref[...] = first_in.T
        turned = dot(weight_ref[...], first_in, 0, 1)
        scaled = (turned[:width] * (half**-0.5 * log2_e)).astype(low)
        turned = turned[width:].astype(low)
        queries_ref[...] = scaled.reshape(pairs, LANES, length)
        keys_ref[...] = turned[:width].reshape(pairs, LANES, length)
        values[...] = turned[width:].reshape(pairs, LANES, length)
        norms = []
        for part in (scaled, turned[:width]):
            square = part.astype(full).reshape(2 * pairs, half, length)
            norms.append(jnp.max(jnp.sum(square * square, axis=1), axis=1, keepdims=True))
        bound[0] = jnp.max(norms[0] * norms[1])
        rows = dot(first_in, weight_ref[:, width:]).astype(low)
        for index in range(pairs):
            key_rows[index] = rows[:, index * LANES : (index + 1) * LANES]
            value_rows_ref[index] = rows[:, width + index * LANES : width + (index + 1) * LANES]
        images = lax.broadcasted_iota(jnp.int32, (LANES, length), 0)
        matching = images == ids_ref[...]
        same[...] = matching.astype(full).astype(low)
        other = jnp.where(jnp.logical_or(matching, images >= IMG_ROW), 0.0, masked_fill)
        mask_rows[...] = other.T.astype(low)
        for save in saves:
            save.start()

    def attend_pair(raise_scores):
        keys = jnp.concatenate([key_rows[pair], mask_rows[...]], axis=1)
        none = jnp.zeros((half, TILE), low)
        ones = jnp.ones((16, length), low)
        for head in range(2):
            rows = slice(head * half, (head + 1) * half)
            value = jnp.concatenate([values[pair, rows, :], ones], axis=0)
            for start in range(0, length, TILE):
                span = slice(start, start + TILE)
                query = queries_ref[pair, rows, span]
                parts = [query, none] if head == 0 else [none, query]
                scores = dot(keys, jnp.concatenate(parts + [same[:, span]], axis=0))
                probs = raise_scores(scores).astype(low)
                probs_ref[head, :, span] = probs
                mixed = dot(value, probs)
                inverse = 1.0 / mixed[half : half + 1]
                inverse_ref[0, head : head + 1, span] = inverse
                attn_ref[0, rows, span] = (mixed[:half] * inverse).astype(low)

    small = bound[0] < score_bound * score_bound

    @pl.when(small)
    def _():
        attend_pair(jnp.exp2)

    @pl.when(jnp.logical_not(small))
    def _():
        attend_pair(lambda scores: jnp.exp2(scores - jnp.max(scores, axis=0, keepdims=True)))

    @pl.when(pair == pairs - 1)
    def _():
        for save in saves:
            save.wait()


def attend(patches, ids, gain, weight):
    length, width = patches.shape
    pairs = width // LANES
    stack = (pairs, LANES, length)
    rows = (pairs, length, LANES)
    return pl.pallas_call(
        attend_kernel,
        grid=(pairs,),
        in_specs=[whole_vmem] * 4,
        out_specs=[
            pl.BlockSpec((2, length, length), lambda pair: (pair, 0, 0)),
            pl.BlockSpec((1, LANES, length), lambda pair: (pair, 0, 0)),
            pl.BlockSpec((1, 2, length), lambda pair: (pair, 0, 0)),
            anywhere,
            anywhere,
            anywhere,
            anywhere,
        ],
        out_shape=[
            kept((2 * pairs, length, length), low),
            kept(stack, low),
            kept((pairs, 2, length), full),
            kept(stack, low),
            kept(stack, low),
            kept(rows, low),
            kept((width, length), low),
        ],
        scratch_shapes=[
            pltpu.VMEM(stack, low),
            pltpu.VMEM(stack, low),
            pltpu.VMEM(rows, low),
            pltpu.VMEM((width, length), low),
            pltpu.VMEM(rows, low),
            pltpu.VMEM(stack, low),
            pltpu.VMEM((length, LANES), low),
            pltpu.VMEM((LANES, length), low),
            pltpu.SMEM((1,), full),
            pltpu.SemaphoreType.DMA((4,)),
        ],
        compiler_params=params(24),
        cost_estimate=cost(25),
        name="attend",
    )(*keep(patches, ids, gain, weight))


def slot_rows(slots):
    experts = slots.shape[0]
    row = lax.broadcasted_iota(jnp.int32, (experts * IMG_ROW, experts), 0) // IMG_ROW
    column = lax.broadcasted_iota(jnp.int32, (experts * IMG_ROW, experts), 1)
    return dot((row == column).astype(full).astype(low), slots).astype(low)


def route_kernel(
    x_ref, attn_ref, proj_ref, gain_ref, slots_ref, ids_ref, cotangent_ref,
    resid_out, second_out, dispatch_out, combine_out, send_ref,
    resid_ref, second_ref, dispatch_ref, combine_ref, semaphores,
):
    length, width = x_ref.shape
    saves = [
        pltpu.make_async_copy(source, target, semaphores.at[index])
        for index, (source, target) in enumerate(
            [
                (resid_ref, resid_out),
                (second_ref, second_out),
                (combine_ref, combine_out),
                (dispatch_ref, dispatch_out),
            ]
        )
    ]
    experts = slots_ref.shape[0]
    shape = (experts, IMG_ROW, length)
    resid = x_ref[...].astype(full) + dot(attn_ref[...].reshape(width, length), proj_ref[...], 0, 0)
    resid_ref[...] = resid
    saves[0].start()
    normed, _ = norm_parts(resid)
    second_in = (normed * gain_ref[...].reshape(1, width)).astype(low)
    second_ref[...] = second_in
    saves[1].start()
    logits = dot(slot_rows(slots_ref[...]), second_in, 1, 1).reshape(shape)
    member = member_of(ids_ref[...])
    raised = jnp.exp(logits - jnp.max(logits, axis=0, keepdims=True))
    combine = raised * (1.0 / jnp.sum(raised, axis=0, keepdims=True))
    combine_ref[...] = combine
    saves[2].start()
    combine_low = jnp.where(member[None], combine, 0.0).astype(low).reshape(-1, length)
    masked = jnp.where(member[None], logits, masked_fill)
    top = jnp.max(masked, axis=2, keepdims=True)
    raised = jnp.where(member[None], jnp.exp(masked - top), 0.0)
    present = jnp.max(member.astype(full), axis=1, keepdims=True)
    total = jnp.sum(raised, axis=2, keepdims=True) + (1.0 - present)[None]
    dispatch = raised * (1.0 / total)
    dispatch_ref[...] = dispatch
    saves[3].start()
    dispatch_low = dispatch.astype(low).reshape(-1, length)
    block = (send_ref.shape[0], send_ref.shape[2], width)
    send_ref[:, 0] = dot(dispatch_low, second_in).astype(low).reshape(block)
    send_ref[:, 1] = dot(combine_low, cotangent_ref[...]).astype(low).reshape(block)
    for save in saves:
        save.wait()


def route(patches, attn, proj, gain, slots, ids, cotangent, groups):
    length, width = patches.shape
    experts = slots.shape[0]
    own = experts // groups * IMG_ROW
    return pl.pallas_call(
        route_kernel,
        in_specs=[whole_vmem] * 7,
        out_specs=[anywhere] * 4 + [whole_vmem],
        out_shape=[
            kept((length, width), full),
            kept((length, width), low),
            kept((experts, IMG_ROW, length), full),
            kept((experts, IMG_ROW, length), full),
            shape_of((groups, 2, own, width), low),
        ],
        scratch_shapes=[
            pltpu.VMEM((length, width), full),
            pltpu.VMEM((length, width), low),
            pltpu.VMEM((experts, IMG_ROW, length), full),
            pltpu.VMEM((experts, IMG_ROW, length), full),
            pltpu.SemaphoreType.DMA((4,)),
        ],
        compiler_params=params(16 + experts // 4),
        cost_estimate=cost(3),
        name="route",
    )(*keep(patches, attn, proj, gain), slots, *keep(ids, cotangent))


def own_rows(received, expert):
    groups, _, width = received.shape
    rows = received[:, expert * IMG_ROW : (expert + 1) * IMG_ROW]
    return rows.reshape(groups * IMG_ROW, width).astype(low)


def expert_kernel(received_ref, up_ref, down_ref, back_ref, stage):
    expert = pl.program_id(0)
    groups, _, own, width = received_ref.shape
    slots = received_ref[:, 0].astype(full)
    grads = received_ref[:, 1].astype(full)
    for index in range(own // IMG_ROW):

        @pl.when(expert == index)
        def _():
            up = up_ref[0]
            down = down_ref[0]
            pre = dot(own_rows(slots, index), up)
            cdf, pdf = gelu_parts(pre)
            out = dot((pre * cdf).astype(low), down)
            grad_hidden = dot(own_rows(grads, index), down, 1, 1)
            grad_pre = (grad_hidden * (cdf + pre * pdf)).astype(low)
            grad_slots = dot(grad_pre, up, 1, 1)
            rows = slice(index * IMG_ROW, (index + 1) * IMG_ROW)
            stage[0, :, rows] = out.reshape(groups, IMG_ROW, width)
            stage[1, :, rows] = grad_slots.reshape(groups, IMG_ROW, width)

    @pl.when(expert == own // IMG_ROW - 1)
    def _():
        back_ref[:, 0] = stage[0].astype(low)
        back_ref[:, 1] = stage[1].astype(low)


def run_experts(received, up, down):
    groups, _, own, width = received.shape
    experts, _, hidden = up.shape
    return pl.pallas_call(
        expert_kernel,
        grid=(experts,),
        in_specs=[
            whole_vmem,
            pl.BlockSpec((1, width, hidden), lambda expert: (expert, 0, 0)),
            pl.BlockSpec((1, hidden, width), lambda expert: (expert, 0, 0)),
        ],
        out_specs=pl.BlockSpec(received.shape, lambda expert: (0, 0, 0, 0)),
        out_shape=shape_of(received.shape, low),
        scratch_shapes=[pltpu.VMEM((2, groups, own, width), full)],
        compiler_params=params(40),
        cost_estimate=cost(3),
        name="run_experts",
    )(received, *keep(up, down))


def backward_kernel(
    back_ref, slots_ref, gain_ref, ids_ref, inverse_ref, *refs
):
    sources = refs[:12]
    output_ref, grad_resid_ref, grads_ref, sums_ref = refs[-20:-16]
    targets = refs[-16:-4]
    grad_attn, delta, grad_scores, semaphores = refs[-4:]
    loads = [
        pltpu.make_async_copy(source, target, semaphores.at[index])
        for index, (source, target) in enumerate(zip(sources, targets, strict=True))
    ]
    for load in loads:
        load.start()
    cotangent_ref, combine_ref, second_ref, dispatch_ref, resid_ref, attn_ref, proj_ref = targets[:7]
    values_ref, probs_ref, keys_ref, queries_ref, first_ref = targets[7:]
    for load in loads[:4]:
        load.wait()
    length, width = resid_ref.shape
    pairs = width // LANES
    half = LANES // 2
    experts = slots_ref.shape[0]
    count = experts * IMG_ROW
    shape = (experts, IMG_ROW, length)
    slot_out = back_ref[:, 0].reshape(count, width)
    grad_slots = back_ref[:, 1].reshape(count, width)
    cotangent = cotangent_ref[...]
    second_in = second_ref[...]
    combine = combine_ref[...]
    dispatch = dispatch_ref[...]
    member = member_of(ids_ref[...])
    grad_combine = dot(slot_out, cotangent, 1, 1).reshape(shape)
    grad_own = jnp.sum(jnp.where(member[None], grad_combine, 0.0), axis=1, keepdims=True)
    inner = jnp.sum(combine * grad_own, axis=0, keepdims=True)
    grad_logits = combine * (grad_own - inner)
    grad_dispatch = dot(grad_slots, second_in, 1, 1).reshape(shape)
    weighted = jnp.sum(dispatch * grad_dispatch, axis=2, keepdims=True)
    routed = jnp.sum(dispatch * (grad_dispatch - weighted), axis=1, keepdims=True)
    grad_low = (grad_logits + routed).astype(low).reshape(count, length)
    row = lax.broadcasted_iota(jnp.int32, (experts, count), 0) * IMG_ROW
    column = lax.broadcasted_iota(jnp.int32, (experts, count), 1)
    grad_low = dot((row == column).astype(full).astype(low), grad_low).astype(low)
    slot_grad = dot(grad_low, second_in)
    mixing = jnp.concatenate([dispatch.astype(low).reshape(count, length), grad_low], axis=0)
    mixed = jnp.concatenate([grad_slots, slots_ref[...]], axis=0)
    grad_second = dot(mixing, mixed, 0, 0)
    for load in loads[4:7]:
        load.wait()
    resid = resid_ref[...]
    combine_low = jnp.where(member[None], combine, 0.0).astype(low).reshape(count, length)
    output_ref[...] = (resid + dot(combine_low, slot_out, 0, 0)).astype(low)
    normed, factor = norm_parts(resid)
    second_grad = jnp.sum(grad_second * normed, axis=0, keepdims=True)
    gain = gain_ref[...].reshape(1, width)
    grad_resid = cotangent.astype(full) + norm_back(grad_second, normed, factor, gain)
    grad_resid_ref[...] = grad_resid
    grad_branch = grad_resid.astype(low)
    attn = attn_ref[...]
    proj_grad = dot(attn.reshape(width, length), grad_branch).astype(low)
    scaled = dot(proj_ref[...], grad_branch, 1, 1).reshape(pairs, 2, half, length)
    scaled = (scaled * inverse_ref[...][:, :, None, :]).astype(low)
    product = scaled.astype(full) * attn.reshape(scaled.shape).astype(full)
    delta[...] = jnp.sum(product, axis=2)
    grad_attn[...] = scaled.reshape(grad_attn.shape)
    slot_low = slot_grad.astype(low)
    second_low = jnp.broadcast_to(second_grad, (16, width)).astype(low)
    early = pairs * (width + experts + 16)
    for index in range(pairs):
        lanes = slice(index * LANES, (index + 1) * LANES)
        sums_ref[index * width : (index + 1) * width] = proj_grad[:, lanes]
        base = width * pairs + index * experts
        sums_ref[base : base + experts] = slot_low[:, lanes]
        base = (width + experts) * pairs + index * 16
        sums_ref[base : base + 16] = second_low[:, lanes]
    used = early + pairs * 3 * width
    if used < sums_ref.shape[0]:
        sums_ref[used:] = jnp.zeros((sums_ref.shape[0] - used, LANES), low)

    for load in loads[7:]:
        load.wait()
    factor = half**-0.5
    none = jnp.zeros((half, TILE), low)

    def one_pair(pair, carry):
        for head in range(2):
            rows = slice(head * half, (head + 1) * half)
            for start in range(0, length, TILE):
                span = slice(start, start + TILE)
                grad = grad_attn[pair, rows, span]
                parts = [grad, none] if head == 0 else [none, grad]
                grad_probs = dot(values_ref[pair], jnp.concatenate(parts, axis=0))
                probs = probs_ref[2 * pair + head, :, span].astype(full)
                grad_probs = grad_probs - delta[pair, head : head + 1, span]
                grad_scores[head, :, span] = (probs * grad_probs).astype(low)
            scores = grad_scores[head]
            probs = probs_ref[2 * pair + head]
            grads_ref[pair, 2, rows, :] = dot(grad_attn[pair, rows, :], probs, 1, 1).astype(low)
            grads_ref[pair, 0, rows, :] = (dot(keys_ref[pair, rows, :], scores) * factor).astype(low)
            grads_ref[pair, 1, rows, :] = (
                dot(queries_ref[pair, rows, :], scores, 1, 1) * (1.0 / log2_e)
            ).astype(low)
        sums = dot(first_ref[...], grads_ref[pair].reshape(3 * LANES, length), 1, 1).astype(low)

        for index in range(3):
            base = pl.multiple_of(early + (pair * 3 + index) * width, 16)
            sums_ref[pl.ds(base, width)] = sums[:, index * LANES : (index + 1) * LANES]
        return carry

    lax.fori_loop(0, pairs, one_pair, 0)


def padded(rows, devices):
    return -(-rows // (16 * devices)) * 16 * devices


def backward(back, slots, gain, ids, inverse, arrays, devices):
    length, width = arrays[0].shape
    experts = slots.shape[0]
    pairs = width // LANES
    rows = padded(pairs * (4 * width + experts + 16), devices)
    return pl.pallas_call(
        backward_kernel,
        in_specs=[whole_vmem] * 5 + [anywhere] * len(arrays),
        out_specs=[whole_vmem] * 4,
        out_shape=[
            kept((length, width), low),
            kept((length, width), full),
            kept((pairs, 3, LANES, length), low),
            shape_of((rows, LANES), low),
        ],
        scratch_shapes=[pltpu.VMEM(array.shape, array.dtype) for array in arrays]
        + [
            pltpu.VMEM((pairs, LANES, length), low),
            pltpu.VMEM((pairs, 2, length), full),
            pltpu.VMEM((2, length, length), low),
            pltpu.SemaphoreType.DMA((len(arrays),)),
        ],
        compiler_params=params(44 + experts // 8),
        cost_estimate=cost(20),
        name="backward",
    )(back, *keep(slots, gain, ids, inverse, *arrays))


def patch_back_kernel(x_ref, gain_ref, weight_ref, resid_ref, grads_ref, *refs):
    result_ref = refs[-1]
    length, width = x_ref.shape
    pairs = width // LANES
    grads = [grads_ref[pair, part] for part in range(3) for pair in range(pairs)]
    grad_first = dot(weight_ref[...], jnp.concatenate(grads, axis=0)).T
    normed, factor = norm_parts(x_ref[...].astype(full))
    gain = gain_ref[...].reshape(1, width)
    result_ref[...] = resid_ref[...] + norm_back(grad_first, normed, factor, gain)


def patch_back(patches, gain, weight, grad_resid, grads, after):
    return pl.pallas_call(
        patch_back_kernel,
        in_specs=[whole_vmem] * 5 + [anywhere] * len(after),
        out_specs=whole_vmem,
        out_shape=kept(patches.shape, full),
        compiler_params=params(20),
        cost_estimate=cost(3),
        name="patch_back",
    )(*keep(patches, gain, weight, grad_resid, grads, *after))


def weights_kernel(copies, *refs):
    received = refs[:copies]
    up_ref, down_ref, _, up_grad_ref, down_grad_ref, slots, grads = refs[copies:]
    expert = pl.program_id(0)
    groups, _, own, width = received[0].shape
    count = groups * IMG_ROW
    for index in range(own // IMG_ROW):

        @pl.when(jnp.logical_and(expert == index, pl.program_id(1) == 0))
        def _():
            for copy, ref in enumerate(received):
                rows = slice(copy * count, (copy + 1) * count)
                slots[rows] = own_rows(ref[:, 0].astype(full), index)
                grads[rows] = own_rows(ref[:, 1].astype(full), index)

    pre = dot(slots[...], up_ref[0])
    cdf, pdf = gelu_parts(pre)
    down_grad_ref[0] = dot((pre * cdf).astype(low), grads[...], 0, 0)
    grad_hidden = dot(grads[...], down_ref[0], 1, 1)
    grad_pre = (grad_hidden * (cdf + pre * pdf)).astype(low)
    up_grad_ref[0] = dot(slots[...], grad_pre, 0, 0)


def weight_grads(received, up, down, after):
    groups, _, _, width = received[0].shape
    experts, _, hidden = up.shape
    copies = len(received)
    tile = hidden // 3
    up_spec = pl.BlockSpec((1, width, tile), lambda expert, step: (expert, 0, step))
    down_spec = pl.BlockSpec((1, tile, width), lambda expert, step: (expert, step, 0))
    rows = (copies * groups * IMG_ROW, width)

    def kernel(*refs):
        weights_kernel(copies, *refs)

    return pl.pallas_call(
        kernel,
        grid=(experts, 3),
        in_specs=[whole_vmem] * copies + [up_spec, down_spec, pl.BlockSpec(memory_space=pl.ANY)],
        out_specs=[up_spec, down_spec],
        out_shape=[kept(up.shape, full), kept(down.shape, full)],
        scratch_shapes=[pltpu.VMEM(rows, low)] * 2,
        compiler_params=params(40),
        cost_estimate=cost(9),
        name="weight_grads",
    )(*keep(*received, up, down, after))


def half_kernel(place_ref, mine_ref, other_ref, sums_ref):
    count, share, lanes = sums_ref.shape
    rows = pl.ds(pl.multiple_of(place_ref[0] * count * share, 16), count * share)
    sums = mine_ref[rows].astype(full) + other_ref[rows].astype(full)
    sums_ref[...] = sums.astype(low).reshape(sums_ref.shape)


def add_half(place, mine, other, count):
    rows, lanes = mine.shape
    return pl.pallas_call(
        half_kernel,
        in_specs=[pl.BlockSpec(memory_space=pltpu.SMEM), whole_vmem, whole_vmem],
        out_specs=whole_vmem,
        out_shape=shape_of((count, rows // (2 * count), lanes), low),
        compiler_params=params(12),
        cost_estimate=cost(1),
        name="add_half",
    )(place, mine, other)


def add_kernel(terms_ref, *refs):
    sums_ref = refs[-1]
    sums = jnp.sum(terms_ref[...].astype(full), axis=0).astype(low)
    sums_ref[...] = jnp.broadcast_to(sums[None], sums_ref.shape)


def add_terms(terms, after):
    return pl.pallas_call(
        add_kernel,
        in_specs=[whole_vmem] + [anywhere] * len(after),
        out_specs=whole_vmem,
        out_shape=shape_of(terms.shape, low),
        compiler_params=params(12),
        cost_estimate=cost(1),
        name="add_terms",
    )(terms, *keep(*after))


def finish_kernel(
    total, place_ref, mine_ref, other_ref, weight_ref, gain_ref,
    first_ref, qkv_ref, proj_ref, second_ref, slot_ref,
):
    width = weight_ref.shape[0]
    pairs = width // LANES
    own = slot_ref.shape[0]
    ahead = place_ref[1] == 0

    mine = mine_ref[...].reshape(-1, LANES)
    other = other_ref[...].reshape(-1, LANES)
    sums = jnp.concatenate(
        [jnp.where(ahead, mine, other), jnp.where(ahead, other, mine)], axis=0
    )
    base = (width + total + 16) * pairs
    seconds = []
    for index in range(pairs):
        lanes = slice(index * LANES, (index + 1) * LANES)
        proj_ref[:, lanes] = sums[index * width : (index + 1) * width].astype(full)
        start = (width + total) * pairs + index * 16
        seconds.append(sums[start : start + 16].astype(full)[0:1])
        start = width * pairs + index * total
        row = lax.broadcasted_iota(jnp.int32, (own, total), 0) + place_ref[0] * own
        column = lax.broadcasted_iota(jnp.int32, (own, total), 1)
        chosen = (row == column).astype(full).astype(low)
        slot_ref[:, lanes] = dot(chosen, sums[start : start + total])
    second_ref[...] = jnp.concatenate(seconds, axis=1).reshape(width)
    first = jnp.zeros((width, 1), full)
    for pair in range(pairs):
        for part in range(3):
            lanes = slice(part * width + pair * LANES, part * width + (pair + 1) * LANES)
            start = base + (pair * 3 + part) * width
            grad = sums[start : start + width].astype(full)
            qkv_ref[:, lanes] = grad
            product = grad * weight_ref[:, lanes].astype(full)
            first = first + jnp.sum(product, axis=1, keepdims=True)
    row = jnp.broadcast_to(first, (width, LANES)).T[0:1]
    first_ref[...] = (row / gain_ref[...].reshape(1, width)).reshape(width)


def finish(place, mine, other, weight, gain, experts, own):
    width = weight.shape[0]

    def kernel(*refs):
        finish_kernel(experts, *refs)

    return pl.pallas_call(
        kernel,
        in_specs=[pl.BlockSpec(memory_space=pltpu.SMEM)] + [whole_vmem] * 4,
        out_specs=[whole_vmem] * 5,
        out_shape=[
            shape_of((width,), full),
            shape_of(weight.shape, full),
            shape_of((width, width), full),
            shape_of((width,), full),
            shape_of((own, width), full),
        ],
        compiler_params=params(20),
        cost_estimate=cost(3),
        name="finish",
    )(place, mine, other, *keep(weight, gain))


def per_device(
    patches,
    image_ids,
    first_gain,
    qkv_weight,
    proj_weight,
    second_gain,
    slot_params,
    up_weight,
    down_weight,
    cotangent,
):
    groups = lax.axis_size("expert")
    copies = lax.axis_size("rows")
    devices = groups * copies
    _, length, width = patches.shape
    own = slot_params.shape[1]
    experts = own * groups
    spread = jnp.broadcast_to(slot_params.T[None], (groups, own, width))
    slots = lax.all_to_all(spread, "expert", 0, 0, tiled=True).reshape(experts, width)
    patches = patches[0]
    cotangent = cotangent[0]
    probs, attn, inverse, queries, keys, values, first_in = attend(
        patches, image_ids, first_gain, qkv_weight
    )
    resid, second_in, dispatch, combine, send = route(
        patches, attn, proj_weight, second_gain, slots, image_ids, cotangent, groups
    )
    received = lax.all_to_all(send, "expert", 0, 0, tiled=True)
    back = run_experts(received, up_weight, down_weight)
    back = lax.all_to_all(back, "expert", 0, 0, tiled=True)
    others = [
        lax.ppermute(received, "rows", [(index, index ^ step) for index in range(copies)])
        for step in range(1, copies)
    ]
    saved = [cotangent, combine, second_in, dispatch, resid, attn, proj_weight]
    saved += [values, probs, keys, queries, first_in]
    output, grad_resid, grads, terms = backward(
        back, slots, second_gain, image_ids, inverse, saved, devices
    )
    core = lax.axis_index("rows") % 2
    place = jnp.stack([lax.axis_index("expert"), core]).astype(jnp.int32)
    swap = [(index, index ^ 1) for index in range(copies)]
    halves = [list(range(index, devices, 2)) for index in range(2)]

    def exchange(array):
        return lax.all_to_all(array, both_axes, 0, 0, tiled=True, axis_index_groups=halves)

    half = add_half(place[1:], terms, lax.ppermute(terms, "rows", swap), devices // 2)
    patch_grad = patch_back(patches, first_gain, qkv_weight, grad_resid, grads, [half] + others)
    sums = add_terms(exchange(half), [patch_grad])
    up_grad, down_grad = weight_grads([received] + others, up_weight, down_weight, sums)
    sums, up_grad, down_grad = lax.optimization_barrier((exchange(sums), up_grad, down_grad))
    first_grad, qkv_grad, proj_grad, second_grad, slot_grad = finish(
        place, sums, lax.ppermute(sums, "rows", swap), qkv_weight, first_gain, experts, own
    )
    return (
        output[None],
        patch_grad[None],
        first_grad,
        qkv_grad,
        proj_grad,
        second_grad,
        slot_grad.T,
        up_grad,
        down_grad,
    )


def solution(mesh):
    return jax.shard_map(
        per_device,
        mesh=mesh,
        in_specs=(
            P(("expert", "rows"), None, None),
            P(("expert", "rows"), None),
            P(),
            P(),
            P(),
            P(),
            P(None, "expert"),
            P("expert", None, None),
            P("expert", None, None),
            P(("expert", "rows"), None, None),
        ),
        out_specs=(
            P(("expert", "rows"), None, None),
            P(("expert", "rows"), None, None),
            P(),
            P(),
            P(),
            P(),
            P(None, "expert"),
            P("expert", None, None),
            P("expert", None, None),
        ),
        check_vma=False,
    )
```

time: 195 us -> 145 us (0.74)
  blocking collectives: 60.1 us -> 23.9 us
  local copies, waits for them, and re-layouts: 28.3 us -> 1.99 us
  waiting for transfers between devices: 19.1 us -> 28.7 us
  starting transfers between devices: 12.6 us -> 19.2 us
  Pallas kernels: 71.9 us -> 69.6 us
    all_to_all x1 -> x0, blocking collectives: 35.7 us -> none  [per_device(): terms = lax.all_to_all(terms, both_axes, 0, 0, tiled=True)]
    unnamed x89 -> x10, local copies, waits for them, and re-layouts: 25.6 us -> 0.69 us
    all_to_all x1 -> x2, waiting for transfers between devices: 0.01 us -> 8.36 us  [exchange(): lax.all_to_all(array, both_axes, 0, 0, tiled=True, axis_index_groups=halves)]
    pallas_call x1, Pallas kernels: 25.2 us -> 17.4 us  [attend(): pl.pallas_call(attend_kernel, grid=(pairs,), in_specs=[whole_vmem] * 4, o...]
    all_to_all x1 -> x2, starting transfers between devices: 3.4 us -> 9.77 us  [exchange(): lax.all_to_all(array, both_axes, 0, 0, tiled=True, axis_index_groups=halves)]
    pallas_call x1, Pallas kernels: 7.28 us -> 9.33 us  [weight_grads(): pl.pallas_call(kernel, grid=(experts, 3), in_specs=[whole_vmem] * copies...]
    pallas_call x7 -> x5, Pallas kernels: 33.5 us -> 35.3 us  [the longest x1 23.5 us: backward(): pl.pallas_call(backward_kernel, in_specs=[whole_vmem] * 5 + [anywhere] *...]
    ppermute x3 -> x5, waiting for transfers between devices: 19.1 us -> 20.3 us  [the longest x3 15.3 us: per_device(): lax.ppermute(received, 'rows', [(index, index ^ step) for index in range(...]
  transfers between devices with their start and end apart: 5 -> 8, of which waited for: 2 -> 5; matrix products, arithmetic and copies ran while one was open for 1% -> 0% of each run, Pallas kernels for 18% -> 22%
where the time goes in v2:
time: 145 us; the launch traced here: 144 us
  Pallas kernels  69.6 us (48%)
  waiting for transfers between devices  28.7 us (20%)
  blocking collectives  23.9 us (16%)
  starting transfers between devices  19.2 us (13%)
  local copies, waits for them, and re-layouts  1.99 us (1%)
    pallas_call x1, Pallas kernels, backward(): pl.pallas_call(backward_kernel, in_specs=[whole_vmem] * 5 + [anywhere] *...  23.5 us
    pallas_call x1, Pallas kernels, attend(): pl.pallas_call(attend_kernel, grid=(pairs,), in_specs=[whole_vmem] * 4, o...  17.4 us
    ppermute x3, waiting for transfers between devices, per_device(): lax.ppermute(received, 'rows', [(index, index ^ step) for index in range(...  15.3 us
    all_to_all x1, blocking collectives, per_device(): received = lax.all_to_all(send, 'expert', 0, 0, tiled=True)  13.6 us
    all_to_all x1, blocking collectives, per_device(): back = lax.all_to_all(back, 'expert', 0, 0, tiled=True)  10.3 us
    all_to_all x2, starting transfers between devices, exchange(): lax.all_to_all(array, both_axes, 0, 0, tiled=True, axis_index_groups=halves)  9.77 us
    pallas_call x1, Pallas kernels, weight_grads(): pl.pallas_call(kernel, grid=(experts, 3), in_specs=[whole_vmem] * copies...  9.33 us
    all_to_all x2, waiting for transfers between devices, exchange(): lax.all_to_all(array, both_axes, 0, 0, tiled=True, axis_index_groups=halves)  8.36 us
  transfers between devices with their start and end apart: 8, of which 5 were waited for; matrix products, arithmetic and copies ran while one was open for 0% of the time, Pallas kernels for 22%

profile of v2, /device:TPU:0, one launch (start us, length us, event | category | flops | bytes accessed | tf_op | source)
XLA Modules:
  0.0 144.1 jit_solution(8944082541041291995)
XLA Ops:
  0.6 1.3 broadcast_in_dim.12
  1.9 7.3 %all-to-all-start = ((bf16[8,2,384]{2,1,0:T(2,128)(2,1)}), bf16[8,2,384]{2,1,0:T(2,128)(2,1)S(1)}, u32[]{:S(2)}, u32[]{:S(2)}) async-start(bf16[8,2,384]{2,1,0:T(2,128)(2,1)} %broadcast_in_dim.12), calls=%async_computation | async-start | bytes 24576 | tf_op jit(solution)/shard_map/all_to_all | solution.py:678
  9.2 17.4 %attend.1 = (bf16[6,1024,1024]{2,1,0:T(8,128)(2,1)}, bf16[3,128,1024]{2,1,0:T(8,128)(2,1)}, f32[3,2,1024]{2,1,0:T(2,128)}, bf16[3,128,1024]{2,1,0:T(8,128)(2,1)}...) custom-call(bf16[1024,384]{1,0:T(8,128)(2,1)} %bitcast.8, ...), custom_call_target="tpu_custom_call" | custom-call | bytes 90000000 | tf_op jit(solution)/shard_map/attend/pallas_call | solution.py:168
  26.6 0.0 all-to-all-done
  26.7 0.0 copy-start.1
  26.7 4.3 %route.1 = (f32[1024,384]{1,0:T(8,128)}, bf16[1024,384]{1,0:T(8,128)(2,1)}, f32[16,8,1024]{2,1,0:T(8,128)}, f32[16,8,1024]{2,1,0:T(8,128)}, bf16[8,2,16,384]{3,2,1,0:T(8,128)(2,1)S(1)}) custom-call(bf16[1024,384]{1,0:T(8,128)(2,1)} %bitcast.9, bf16[3,128,1024]{2,1,0:T(8,128)(2,1)} %get-tuple-element.35.attn_ref.refs_5_, bf16[384,384]{1,0:T(8,128)(2,1)} %refs_6_.1, ...), custom_call_target="tpu_custom_call" | custom-call | bytes 10800000 | tf_op jit(solution)/shard_map/route/pallas_call | solution.py:268
  31.0 13.6 %all_to_all.25.received_ref.refs_0_ = bf16[8,2,16,384]{3,2,1,0:T(8,128)(2,1)S(1)} all-to-all(bf16[8,2,16,384]{3,2,1,0:T(8,128)(2,1)S(1)} %get-tuple-element.36), channel_id=1, replica_groups=mesh['expert'=8,'rows'=4] {'expert'}, dimensions={0} | all-to-all | bytes 393216 | tf_op jit(solution)/shard_map/all_to_all | solution.py:687
  44.6 0.0 copy-start
  44.6 4.4 %run_experts.1 = bf16[8,2,16,384]{3,2,1,0:T(8,128)(2,1)S(1)} custom-call(bf16[8,2,16,384]{3,2,1,0:T(8,128)(2,1)S(1)} %all_to_all.25.received_ref.refs_0_, bf16[2,384,1536]{2,1,0:T(8,128)(2,1)} %refs_4_.2, bf16[2,1536,384]{2,1,0:T(8,128)(2,1)} %refs_5_.1), custom_call_target="tpu_custom_call" | custom-call | bytes 10800000 | tf_op jit(solution)/shard_map/run_experts/pallas_call | solution.py:328
  49.0 0.0 copy-done.1
  49.0 10.3 %all_to_all.26.back_ref = bf16[8,2,16,384]{3,2,1,0:T(8,128)(2,1)S(1)} all-to-all(bf16[8,2,16,384]{3,2,1,0:T(8,128)(2,1)S(1)} %run_experts.1), channel_id=1, replica_groups=mesh['expert'=8,'rows'=4] {'expert'}, dimensions={0} | all-to-all | bytes 393216 | tf_op jit(solution)/shard_map/all_to_all | solution.py:689
  59.3 23.5 %backward.1 = (bf16[1024,384]{1,0:T(8,128)(2,1)}, f32[1024,384]{1,0:T(8,128)}, bf16[3,3,128,1024]{3,2,1,0:T(8,128)(2,1)}, bf16[5120,128]{1,0:T(8,128)(2,1)S(1)}) custom-call(bf16[8,2,16,384]{3,2,1,0:T(8,128)(2,1)S(1)} %all_to_all.26.back_ref, bf16[16,384]{1,0:T(8,128)(2,1)} %copy-done.1, f32[384]{0:T(512)} %gain_ref.6, s32[1,1024]{1,0:T(1,128)} %ids_ref.5, ...), custom_call_target="tpu_custom_call" | custom-call | bytes 72000000 | tf_op jit(solution)/shard_map/backward/pallas_call | solution.py:464
  82.8 0.1 collective-permute-start
  82.9 3.0 %collective-permute-done.other_ref = bf16[5120,128]{1,0:T(8,128)(2,1)S(1)} collective-permute-done((bf16[5120,128]{1,0:T(8,128)(2,1)S(1)}, bf16[5120,128]{1,0:T(8,128)(2,1)S(1)}, u32[]{:S(2)}, u32[]{:S(2)}) %collective-permute-start) | collective-permute-done | bytes 1310752 | tf_op jit(solution)/shard_map/ppermute | solution.py:707
  85.9 1.0 add_half.1.refs_0_
  86.9 3.7 %all-to-all-start.3 = ((bf16[16,160,128]{2,1,0:T(8,128)(2,1)}), bf16[16,160,128]{2,1,0:T(8,128)(2,1)S(1)}, u32[]{:S(2)}, u32[]{:S(2)}) async-start(bf16[16,160,128]{2,1,0:T(8,128)(2,1)} %add_half.1.refs_0_), calls=%async_computation.3 | async-start | bytes 1310720 | tf_op jit(solution)/shard_map/all_to_all | solution.py:705
  90.6 0.1 collective-permute-start.1
  90.7 1.9 %collective-permute-start.2 = (bf16[8,2,16,384]{3,2,1,0:T(8,128)(2,1)S(1)}, bf16[8,2,16,384]{3,2,1,0:T(8,128)(2,1)S(1)}, u32[]{:S(2)}, u32[]{:S(2)}) collective-permute-start(bf16[8,2,16,384]{3,2,1,0:T(8,128)(2,1)S(1)} %all_to_all.25.received_ref.refs_0_), channel_id=1, source_target_pairs={{0,2},{1,3},{2,0},{3,1},{4,6},{5,7},{6,4},{7,5},{8,10},{9,11},{10,... | collective-permute-start | bytes 589832 | tf_op jit(solution)/shard_map/ppermute | solution.py:691
  92.6 0.0 copy-done
  92.6 0.1 collective-permute-start.3
  92.7 0.0 collective-permute-done.1.refs_1_
  92.7 0.0 copy-start.2
  92.7 11.2 %collective-permute-done.2.refs_2_ = bf16[8,2,16,384]{3,2,1,0:T(8,128)(2,1)S(1)} collective-permute-done((bf16[8,2,16,384]{3,2,1,0:T(8,128)(2,1)S(1)}, bf16[8,2,16,384]{3,2,1,0:T(8,128)(2,1)S(1)}, u32[]{:S(2)}, u32[]{:S(2)}) %collective-permute-start.2) | collective-permute-done | bytes 196640 | tf_op jit(solution)/shard_map/ppermute | solution.py:691
  103.8 0.0 copy-start.3
  103.8 4.1 %collective-permute-done.3.refs_3_ = bf16[8,2,16,384]{3,2,1,0:T(8,128)(2,1)S(1)} collective-permute-done((bf16[8,2,16,384]{3,2,1,0:T(8,128)(2,1)S(1)}, bf16[8,2,16,384]{3,2,1,0:T(8,128)(2,1)S(1)}, u32[]{:S(2)}, u32[]{:S(2)}) %collective-permute-start.3) | collective-permute-done | bytes 196640 | tf_op jit(solution)/shard_map/ppermute | solution.py:691
  107.9 0.0 copy-start.4
  107.9 0.0 copy-done.2
  107.9 0.0 copy-done.3
  107.9 0.7 copy-done.4
  108.6 5.6 %patch_back.1.refs_0_ = f32[1024,384]{1,0:T(8,128)} custom-call(bf16[1024,384]{1,0:T(8,128)(2,1)} %bitcast.10, f32[384]{0:T(512)} %refs_4_.3, bf16[384,1152]{1,0:T(8,128)(2,1)} %refs_3_.1, f32[1024,384]{1,0:T(8,128)} %get-tuple-element.48.resid_ref, bf16[3,3,128,1024]{3,2,1,0:T(8,128)(2,1)} %get-tuple-element.49.grads_ref, ...), custom_call_target="tpu_custom_call" | custom-call | bytes 10800000 | tf_op jit(solution)/shard_map/patch_back/pallas_call | solution.py:499
  114.2 0.0 all-to-all-done.3.terms_ref
  114.2 0.9 add_terms.1.refs_6_
  115.1 6.1 %all-to-all-start.4 = ((bf16[16,160,128]{2,1,0:T(8,128)(2,1)}), bf16[16,160,128]{2,1,0:T(8,128)(2,1)S(1)}, u32[]{:S(2)}, u32[]{:S(2)}) async-start(bf16[16,160,128]{2,1,0:T(8,128)(2,1)} %add_terms.1.refs_6_), calls=%async_computation.4 | async-start | bytes 1310720 | tf_op jit(solution)/shard_map/all_to_all | solution.py:705
  121.2 9.3 %weight_grads.1 = (f32[2,384,1536]{2,1,0:T(8,128)}, f32[2,1536,384]{2,1,0:T(8,128)}) custom-call(bf16[8,2,16,384]{3,2,1,0:T(8,128)(2,1)} %copy-done, bf16[8,2,16,384]{3,2,1,0:T(8,128)(2,1)} %copy-done.2, bf16[8,2,16,384]{3,2,1,0:T(8,128)(2,1)} %copy-done.3, bf16[8,2,16,384]{3,2,1,0:T(8,128)(2,1)} %copy-done.4, bf16[2,384,1536]{2,1,0:T(8,128)(2,1)} %refs_4_.2, ...), custom_call_target="tpu_custom_call" | custom-call | bytes 32400000 | tf_op jit(solution)/shard_map/weight_grads/pallas_call | solution.py:545
  130.6 8.4 %all-to-all-done.4.refs_1_ = bf16[16,160,128]{2,1,0:T(8,128)(2,1)S(1)} async-done(((bf16[16,160,128]{2,1,0:T(8,128)(2,1)}), bf16[16,160,128]{2,1,0:T(8,128)(2,1)S(1)}, u32[]{:S(2)}, u32[]{:S(2)}) %all-to-all-start.4) | async-done | bytes 655392 | tf_op jit(solution)/shard_map/all_to_all | solution.py:705
  138.9 0.0 collective-permute-start.4
  138.9 0.1 pad_add_fusion.refs_0_
  139.0 2.0 %collective-permute-done.4.refs_2_ = bf16[16,160,128]{2,1,0:T(8,128)(2,1)S(1)} collective-permute-done((bf16[16,160,128]{2,1,0:T(8,128)(2,1)S(1)}, bf16[16,160,128]{2,1,0:T(8,128)(2,1)S(1)}, u32[]{:S(2)}, u32[]{:S(2)}) %collective-permute-start.4) | collective-permute-done | bytes 655392 | tf_op jit(solution)/shard_map/ppermute | solution.py:713
  141.0 3.1 %finish.1 = (f32[384]{0:T(512)}, f32[384,1152]{1,0:T(8,128)}, f32[384,384]{1,0:T(8,128)}, f32[384]{0:T(512)}, f32[2,384]{1,0:T(2,128)}) custom-call(s32[2]{0:T(128)S(1)} %pad_add_fusion.refs_0_, bf16[16,160,128]{2,1,0:T(8,128)(2,1)S(1)} %all-to-all-done.4.refs_1_, bf16[16,160,128]{2,1,0:T(8,128)(2,1)S(1)} %collective-permute-done.4.refs_2_, ...), custom_call_target="tpu_custom_call" | custom-call | bytes 10800000 | tf_op jit(solution)/shard_map/finish/pallas_call | solution.py:642
  (1 shorter events, 0.0 us)
Async XLA Ops:
  1.9 24.7 %all-to-all-start = ((bf16[8,2,384]{2,1,0:T(2,128)(2,1)}), bf16[8,2,384]{2,1,0:T(2,128)(2,1)S(1)}, u32[]{:S(2)}, u32[]{:S(2)}) async-start(bf16[8,2,384]{2,1,0:T(2,128)(2,1)} %broadcast_in_dim.12), calls=%async_computation | async-start | bytes 24576 | tf_op jit(solution)/shard_map/all_to_all | solution.py:678
  26.7 22.3 %copy-start.1 = (bf16[16,384]{1,0:T(8,128)(2,1)}, bf16[16,384]{1,0:T(8,128)(2,1)S(1)}, u32[]{:S(2)}) copy-start(bf16[16,384]{1,0:T(8,128)(2,1)S(1)} %reshape.22.slots_ref) | copy-start | bytes 36868
  44.6 48.0 %copy-start = (bf16[8,2,16,384]{3,2,1,0:T(8,128)(2,1)}, bf16[8,2,16,384]{3,2,1,0:T(8,128)(2,1)S(1)}, u32[]{:S(2)}) copy-start(bf16[8,2,16,384]{3,2,1,0:T(8,128)(2,1)S(1)} %all_to_all.25.received_ref.refs_0_) | copy-start | bytes 589828
  82.8 3.1 %collective-permute-start = (bf16[5120,128]{1,0:T(8,128)(2,1)S(1)}, bf16[5120,128]{1,0:T(8,128)(2,1)S(1)}, u32[]{:S(2)}, u32[]{:S(2)}) collective-permute-start(bf16[5120,128]{1,0:T(8,128)(2,1)S(1)} %get-tuple-element.50.mine_ref), channel_id=1, source_target_pairs={{0,1},{1,0},{2,3},{3,2},{4,5},{5,4},{6,7},{7,6},{8,9},{9,8},{10,11... | collective-permute-start | bytes 3932168 | tf_op jit(solution)/shard_map/ppermute | solution.py:707
  86.9 27.3 %all-to-all-start.3 = ((bf16[16,160,128]{2,1,0:T(8,128)(2,1)}), bf16[16,160,128]{2,1,0:T(8,128)(2,1)S(1)}, u32[]{:S(2)}, u32[]{:S(2)}) async-start(bf16[16,160,128]{2,1,0:T(8,128)(2,1)} %add_half.1.refs_0_), calls=%async_computation.3 | async-start | bytes 1310720 | tf_op jit(solution)/shard_map/all_to_all | solution.py:705
  90.6 2.1 %collective-permute-start.1 = (bf16[8,2,16,384]{3,2,1,0:T(8,128)(2,1)S(1)}, bf16[8,2,16,384]{3,2,1,0:T(8,128)(2,1)S(1)}, u32[]{:S(2)}, u32[]{:S(2)}) collective-permute-start(bf16[8,2,16,384]{3,2,1,0:T(8,128)(2,1)S(1)} %all_to_all.25.received_ref.refs_0_), channel_id=1, source_target_pairs={{0,1},{1,0},{2,3},{3,2},{4,5},{5,4},{6,7},{7,6},{8,9},{9,8},{10,11... | collective-permute-start | bytes 589832 | tf_op jit(solution)/shard_map/ppermute | solution.py:691
  90.7 13.1 %collective-permute-start.2 = (bf16[8,2,16,384]{3,2,1,0:T(8,128)(2,1)S(1)}, bf16[8,2,16,384]{3,2,1,0:T(8,128)(2,1)S(1)}, u32[]{:S(2)}, u32[]{:S(2)}) collective-permute-start(bf16[8,2,16,384]{3,2,1,0:T(8,128)(2,1)S(1)} %all_to_all.25.received_ref.refs_0_), channel_id=1, source_target_pairs={{0,2},{1,3},{2,0},{3,1},{4,6},{5,7},{6,4},{7,5},{8,10},{9,11},{10,... | collective-permute-start | bytes 589832 | tf_op jit(solution)/shard_map/ppermute | solution.py:691
  92.6 15.3 %collective-permute-start.3 = (bf16[8,2,16,384]{3,2,1,0:T(8,128)(2,1)S(1)}, bf16[8,2,16,384]{3,2,1,0:T(8,128)(2,1)S(1)}, u32[]{:S(2)}, u32[]{:S(2)}) collective-permute-start(bf16[8,2,16,384]{3,2,1,0:T(8,128)(2,1)S(1)} %all_to_all.25.received_ref.refs_0_), channel_id=1, source_target_pairs={{0,3},{1,2},{2,1},{3,0},{4,7},{5,6},{6,5},{7,4},{8,11},{9,10},{10,... | collective-permute-start | bytes 589832 | tf_op jit(solution)/shard_map/ppermute | solution.py:691
  92.7 15.3 %copy-start.2 = (bf16[8,2,16,384]{3,2,1,0:T(8,128)(2,1)}, bf16[8,2,16,384]{3,2,1,0:T(8,128)(2,1)S(1)}, u32[]{:S(2)}) copy-start(bf16[8,2,16,384]{3,2,1,0:T(8,128)(2,1)S(1)} %collective-permute-done.1.refs_1_) | copy-start | bytes 589828
  103.8 4.1 %copy-start.3 = (bf16[8,2,16,384]{3,2,1,0:T(8,128)(2,1)}, bf16[8,2,16,384]{3,2,1,0:T(8,128)(2,1)S(1)}, u32[]{:S(2)}) copy-start(bf16[8,2,16,384]{3,2,1,0:T(8,128)(2,1)S(1)} %collective-permute-done.2.refs_2_) | copy-start | bytes 589828
  107.9 0.7 copy-start.4
  115.1 23.8 %all-to-all-start.4 = ((bf16[16,160,128]{2,1,0:T(8,128)(2,1)}), bf16[16,160,128]{2,1,0:T(8,128)(2,1)S(1)}, u32[]{:S(2)}, u32[]{:S(2)}) async-start(bf16[16,160,128]{2,1,0:T(8,128)(2,1)} %add_terms.1.refs_6_), calls=%async_computation.4 | async-start | bytes 1310720 | tf_op jit(solution)/shard_map/all_to_all | solution.py:705
  138.9 2.1 %collective-permute-start.4 = (bf16[16,160,128]{2,1,0:T(8,128)(2,1)S(1)}, bf16[16,160,128]{2,1,0:T(8,128)(2,1)S(1)}, u32[]{:S(2)}, u32[]{:S(2)}) collective-permute-start(bf16[16,160,128]{2,1,0:T(8,128)(2,1)S(1)} %all-to-all-done.4.refs_1_), channel_id=1, source_target_pairs={{0,1},{1,0},{2,3},{3,2},{4,5},{5,4},{6,7},{7,6},{8,9},{9,8},{10,11... | collective-permute-start | bytes 1966088 | tf_op jit(solution)/shard_map/ppermute | solution.py:713

commit v3 on v2

v3 whole, which is shorter than its diff:
```python
import jax
import jax.numpy as jnp
from jax import lax
from jax.experimental import pallas as pl
from jax.experimental.pallas import tpu as pltpu
from jax.sharding import PartitionSpec as P

HEADS = 6
IMG_ROW = 8
LANES = 128
TILE = 256

epsilon = 1e-06
masked_fill = -1e30
score_bound = 64.0
log2_e = 1.4426950408889634
low = jnp.bfloat16
full = jnp.float32
whole_vmem = pl.BlockSpec(memory_space=pltpu.VMEM)
anywhere = pl.BlockSpec(memory_space=pl.ANY)
both_axes = ("expert", "rows")


def dot(left, right, left_dim=1, right_dim=0):
    return lax.dot_general(
        left, right, (((left_dim,), (right_dim,)), ((), ())), preferred_element_type=full
    )


def shape_of(shape, dtype):
    return jax.ShapeDtypeStruct(shape, dtype)


def kept(shape, dtype):
    return pltpu.HBM(shape, dtype)


def keep(*arrays):
    return [pltpu.with_memory_space_constraint(array, pltpu.HBM) for array in arrays]


def params(mib):
    return pltpu.CompilerParams(vmem_limit_bytes=mib << 20)


def cost(microseconds):
    return pl.CostEstimate(
        flops=0, transcendentals=0, bytes_accessed=int(microseconds * 3.6e6)
    )


def norm_parts(values):
    centred = values - jnp.mean(values, axis=-1, keepdims=True)
    factor = lax.rsqrt(jnp.mean(centred * centred, axis=-1, keepdims=True) + epsilon)
    return centred * factor, factor


def norm_back(grad_norm, normed, factor, gain):
    scaled = grad_norm * gain
    return factor * (
        scaled
        - jnp.mean(scaled, axis=-1, keepdims=True)
        - normed * jnp.mean(scaled * normed, axis=-1, keepdims=True)
    )


def member_of(ids):
    images = lax.broadcasted_iota(jnp.int32, (IMG_ROW, ids.shape[1]), 0)
    return images == ids


def gelu_parts(pre):
    cdf = 0.5 * (1.0 + lax.erf(pre * 0.7071067811865476))
    pdf = 0.3989422804014327 * jnp.exp(-0.5 * pre * pre)
    return cdf, pdf


def copies_of(sources, targets, semaphores):
    return [
        pltpu.make_async_copy(source, target, semaphores.at[index])
        for index, (source, target) in enumerate(zip(sources, targets, strict=True))
    ]


def attend_kernel(x_ref, ids_ref, gain_ref, weight_ref, proj_ref, second_gain_ref, *refs):
    outs, refs = refs[:9], refs[9:]
    probs_out, saved, refs = outs[0], refs[:8], refs[8:]
    queries_ref, keys_ref, value_rows_ref, first_ref = saved[:4]
    attn_ref, inverse_ref, resid_ref, second_ref = saved[4:]
    probs_ref, key_rows, values, mask_rows, same, bound, semaphores, probs_semaphores = refs
    pair = pl.program_id(0)
    length, width = x_ref.shape
    pairs = width // LANES
    half = LANES // 2
    saves = copies_of(saved, outs[1:], semaphores)

    def save_probs(head):
        return pltpu.make_async_copy(
            probs_ref.at[head], probs_out.at[head], probs_semaphores.at[head]
        )

    @pl.when(pair == 0)
    def _():
        normed, _ = norm_parts(x_ref[...].astype(full))
        first_in = (normed * gain_ref[...].reshape(1, width)).astype(low)
        turned = dot(weight_ref[...], first_in, 0, 1)
        scaled = (turned[:width] * (half**-0.5 * log2_e)).astype(low)
        turned = turned[width:].astype(low)
        queries_ref[...] = scaled.reshape(pairs, LANES, length)
        keys_ref[...] = turned[:width].reshape(pairs, LANES, length)
        values[...] = turned[width:].reshape(pairs, LANES, length)
        norms = []
        for part in (scaled, turned[:width]):
            square = part.astype(full).reshape(2 * pairs, half, length)
            norms.append(jnp.max(jnp.sum(square * square, axis=1), axis=1, keepdims=True))
        bound[0] = jnp.max(norms[0] * norms[1])
        rows = dot(first_in, weight_ref[:, width:]).astype(low)
        for index in range(pairs):
            key_rows[index] = rows[:, index * LANES : (index + 1) * LANES]
            value_rows_ref[index] = rows[:, width + index * LANES : width + (index + 1) * LANES]
        first_ref[...] = first_in.T
        for save in saves[:4]:
            save.start()
        images = lax.broadcasted_iota(jnp.int32, (LANES, length), 0)
        matching = images == ids_ref[...]
        same[...] = matching.astype(full).astype(low)
        other = jnp.where(jnp.logical_or(matching, images >= IMG_ROW), 0.0, masked_fill)
        mask_rows[...] = other.T.astype(low)

    def attend_pair(raise_scores):
        keys = jnp.concatenate([key_rows[pair], mask_rows[...]], axis=1)
        none = jnp.zeros((half, TILE), low)
        ones = jnp.ones((16, length), low)
        for head in range(2):
            rows = slice(head * half, (head + 1) * half)
            for start in range(0, length, TILE):
                span = slice(start, start + TILE)
                query = queries_ref[pair, rows, span]
                parts = [query, none] if head == 0 else [none, query]
                scores = dot(keys, jnp.concatenate(parts + [same[:, span]], axis=0))
                probs_ref[2 * pair + head, :, span] = raise_scores(scores).astype(low)
            save_probs(2 * pair + head).start()
        for head in range(2):
            rows = slice(head * half, (head + 1) * half)
            value = jnp.concatenate([values[pair, rows, :], ones], axis=0)
            mixed = dot(value, probs_ref[2 * pair + head])
            inverse = 1.0 / mixed[half : half + 1]
            inverse_ref[pair, head : head + 1] = inverse
            attn_ref[pair, rows] = (mixed[:half] * inverse).astype(low)

    small = bound[0] < score_bound * score_bound

    @pl.when(small)
    def _():
        attend_pair(jnp.exp2)

    @pl.when(jnp.logical_not(small))
    def _():
        attend_pair(lambda scores: jnp.exp2(scores - jnp.max(scores, axis=0, keepdims=True)))

    @pl.when(pair == pairs - 1)
    def _():
        for save in saves[4:6]:
            save.start()
        attn = attn_ref[...].reshape(width, length)
        resid = x_ref[...].astype(full) + dot(attn, proj_ref[...], 0, 0)
        resid_ref[...] = resid
        saves[6].start()
        normed, _ = norm_parts(resid)
        second_ref[...] = (normed * second_gain_ref[...].reshape(1, width)).astype(low)
        saves[7].start()
        for save in saves:
            save.wait()
        for head in range(2 * pairs):
            save_probs(head).wait()


def attend(patches, ids, gain, weight, proj, second_gain):
    length, width = patches.shape
    pairs = width // LANES
    stack = (pairs, LANES, length)
    rows = (pairs, length, LANES)
    probs = (2 * pairs, length, length)
    saved = [
        (stack, low),
        (stack, low),
        (rows, low),
        ((width, length), low),
        (stack, low),
        ((pairs, 2, length), full),
        ((length, width), full),
        ((length, width), low),
    ]
    return pl.pallas_call(
        attend_kernel,
        grid=(pairs,),
        in_specs=[whole_vmem] * 6,
        out_specs=[anywhere] * 9,
        out_shape=[kept(probs, low)] + [kept(*entry) for entry in saved],
        scratch_shapes=[pltpu.VMEM(*entry) for entry in saved]
        + [
            pltpu.VMEM(probs, low),
            pltpu.VMEM(rows, low),
            pltpu.VMEM(stack, low),
            pltpu.VMEM((length, LANES), low),
            pltpu.VMEM((LANES, length), low),
            pltpu.SMEM((1,), full),
            pltpu.SemaphoreType.DMA((8,)),
            pltpu.SemaphoreType.DMA((2 * pairs,)),
        ],
        compiler_params=params(44),
        cost_estimate=cost(17),
        name="attend",
    )(*keep(patches, ids, gain, weight, proj, second_gain))


def slot_rows(slots):
    experts = slots.shape[0]
    row = lax.broadcasted_iota(jnp.int32, (experts * IMG_ROW, experts), 0) // IMG_ROW
    column = lax.broadcasted_iota(jnp.int32, (experts * IMG_ROW, experts), 1)
    return dot((row == column).astype(full).astype(low), slots).astype(low)


def route_kernel(
    second_ref, slots_ref, ids_ref, cotangent_ref,
    dispatch_out, combine_out, send_ref,
    dispatch_ref, combine_ref, semaphores,
):
    length, width = second_ref.shape
    experts = slots_ref.shape[0]
    shape = (experts, IMG_ROW, length)
    saves = copies_of([dispatch_ref, combine_ref], [dispatch_out, combine_out], semaphores)
    second_in = second_ref[...]
    logits = dot(slot_rows(slots_ref[...]), second_in, 1, 1).reshape(shape)
    member = member_of(ids_ref[...])
    masked = jnp.where(member[None], logits, masked_fill)
    top = jnp.max(masked, axis=2, keepdims=True)
    raised = jnp.where(member[None], jnp.exp(masked - top), 0.0)
    present = jnp.max(member.astype(full), axis=1, keepdims=True)
    total = jnp.sum(raised, axis=2, keepdims=True) + (1.0 - present)[None]
    dispatch = raised * (1.0 / total)
    dispatch_ref[...] = dispatch
    saves[0].start()
    raised = jnp.exp(logits - jnp.max(logits, axis=0, keepdims=True))
    combine = raised * (1.0 / jnp.sum(raised, axis=0, keepdims=True))
    combine_ref[...] = combine
    saves[1].start()
    dispatch_low = dispatch.astype(low).reshape(-1, length)
    combine_low = jnp.where(member[None], combine, 0.0).astype(low).reshape(-1, length)
    block = (send_ref.shape[0], send_ref.shape[2], width)
    send_ref[:, 0] = dot(dispatch_low, second_in).astype(low).reshape(block)
    send_ref[:, 1] = dot(combine_low, cotangent_ref[...]).astype(low).reshape(block)
    for save in saves:
        save.wait()


def route(second_in, slots, ids, cotangent, groups):
    length, width = second_in.shape
    experts = slots.shape[0]
    own = experts // groups * IMG_ROW
    shape = (experts, IMG_ROW, length)
    return pl.pallas_call(
        route_kernel,
        in_specs=[whole_vmem] * 4,
        out_specs=[anywhere] * 2 + [whole_vmem],
        out_shape=[kept(shape, full)] * 2 + [shape_of((groups, 2, own, width), low)],
        scratch_shapes=[pltpu.VMEM(shape, full)] * 2 + [pltpu.SemaphoreType.DMA((2,))],
        compiler_params=params(14 + experts // 4),
        cost_estimate=cost(3),
        name="route",
    )(*keep(second_in), slots, *keep(ids, cotangent))


def own_rows(received, expert):
    groups, _, width = received.shape
    rows = received[:, expert * IMG_ROW : (expert + 1) * IMG_ROW]
    return rows.reshape(groups * IMG_ROW, width).astype(low)


def expert_kernel(received_ref, up_ref, down_source, back_ref, down_ref, stage, semaphores):
    groups, _, own, width = received_ref.shape
    experts = own // IMG_ROW
    loads = copies_of(
        [down_source.at[index] for index in range(experts)],
        [down_ref.at[index] for index in range(experts)],
        semaphores,
    )
    for load in loads:
        load.start()
    slots = received_ref[:, 0].astype(full)
    grads = received_ref[:, 1].astype(full)
    for index in range(experts):
        up = up_ref[index]
        pre = dot(own_rows(slots, index), up)
        cdf, pdf = gelu_parts(pre)
        loads[index].wait()
        down = down_ref[index]
        out = dot((pre * cdf).astype(low), down)
        grad_hidden = dot(own_rows(grads, index), down, 1, 1)
        grad_pre = (grad_hidden * (cdf + pre * pdf)).astype(low)
        grad_slots = dot(grad_pre, up, 1, 1)
        rows = slice(index * IMG_ROW, (index + 1) * IMG_ROW)
        stage[0, :, rows] = out.reshape(groups, IMG_ROW, width)
        stage[1, :, rows] = grad_slots.reshape(groups, IMG_ROW, width)
    back_ref[:, 0] = stage[0].astype(low)
    back_ref[:, 1] = stage[1].astype(low)


def run_experts(received, up, down):
    groups, _, own, width = received.shape
    experts, _, hidden = up.shape
    return pl.pallas_call(
        expert_kernel,
        in_specs=[whole_vmem, whole_vmem, anywhere],
        out_specs=whole_vmem,
        out_shape=shape_of(received.shape, low),
        scratch_shapes=[
            pltpu.VMEM(down.shape, low),
            pltpu.VMEM((2, groups, own, width), full),
            pltpu.SemaphoreType.DMA((experts,)),
        ],
        compiler_params=params(12 + groups // 2),
        cost_estimate=cost(3),
        name="run_experts",
    )(received, up, *keep(down))


def backward_kernel(
    back_ref, slots_ref, gain_ref, ids_ref, inverse_ref, *refs
):
    sources, probs_source, refs = refs[:11], refs[11], refs[12:]
    (output_out, grad_resid_out, grads_out, sums_ref), refs = refs[:4], refs[4:]
    targets, refs = refs[:11], refs[11:]
    probs_ref, output_ref, grad_resid_ref, grads_ref, grad_attn, delta, grad_scores = refs[:7]
    semaphores, probs_semaphores, saves_semaphores = refs[7:]
    loads = copies_of(sources, targets, semaphores)
    cotangent_ref, combine_ref, second_ref, dispatch_ref, resid_ref, attn_ref, proj_ref = targets[:7]
    values_ref, keys_ref, queries_ref, first_ref = targets[7:]
    pairs = resid_ref.shape[1] // LANES

    def load_probs(pair):
        return pltpu.make_async_copy(
            probs_source.at[pl.ds(2 * pair, 2)],
            probs_ref.at[pl.ds(2 * pair, 2)],
            probs_semaphores.at[pair],
        )

    def save_grads(pair):
        return pltpu.make_async_copy(
            grads_ref.at[pair], grads_out.at[pair], saves_semaphores.at[2 + pair]
        )

    saves = copies_of(
        [output_ref, grad_resid_ref], [output_out, grad_resid_out], saves_semaphores
    )
    for load in loads:
        load.start()
    for load in loads[:4]:
        load.wait()
    for pair in range(pairs):
        load_probs(pair).start()
    length, width = resid_ref.shape
    half = LANES // 2
    experts = slots_ref.shape[0]
    count = experts * IMG_ROW
    shape = (experts, IMG_ROW, length)
    slot_out = back_ref[:, 0].reshape(count, width)
    grad_slots = back_ref[:, 1].reshape(count, width)
    cotangent = cotangent_ref[...]
    second_in = second_ref[...]
    combine = combine_ref[...]
    dispatch = dispatch_ref[...]
    member = member_of(ids_ref[...])
    grad_combine = dot(slot_out, cotangent, 1, 1).reshape(shape)
    grad_own = jnp.sum(jnp.where(member[None], grad_combine, 0.0), axis=1, keepdims=True)
    inner = jnp.sum(combine * grad_own, axis=0, keepdims=True)
    grad_logits = combine * (grad_own - inner)
    grad_dispatch = dot(grad_slots, second_in, 1, 1).reshape(shape)
    weighted = jnp.sum(dispatch * grad_dispatch, axis=2, keepdims=True)
    routed = jnp.sum(dispatch * (grad_dispatch - weighted), axis=1, keepdims=True)
    grad_low = (grad_logits + routed).astype(low).reshape(count, length)
    row = lax.broadcasted_iota(jnp.int32, (experts, count), 0) * IMG_ROW
    column = lax.broadcasted_iota(jnp.int32, (experts, count), 1)
    grad_low = dot((row == column).astype(full).astype(low), grad_low).astype(low)
    slot_grad = dot(grad_low, second_in)
    mixing = jnp.concatenate([dispatch.astype(low).reshape(count, length), grad_low], axis=0)
    mixed = jnp.concatenate([grad_slots, slots_ref[...]], axis=0)
    grad_second = dot(mixing, mixed, 0, 0)
    for load in loads[4:7]:
        load.wait()
    resid = resid_ref[...]
    combine_low = jnp.where(member[None], combine, 0.0).astype(low).reshape(count, length)
    output_ref[...] = (resid + dot(combine_low, slot_out, 0, 0)).astype(low)
    saves[0].start()
    normed, factor = norm_parts(resid)
    second_grad = jnp.sum(grad_second * normed, axis=0, keepdims=True)
    gain = gain_ref[...].reshape(1, width)
    grad_resid = cotangent.astype(full) + norm_back(grad_second, normed, factor, gain)
    grad_resid_ref[...] = grad_resid
    saves[1].start()
    grad_branch = grad_resid.astype(low)
    attn = attn_ref[...]
    proj_grad = dot(attn.reshape(width, length), grad_branch).astype(low)
    scaled = dot(proj_ref[...], grad_branch, 1, 1).reshape(pairs, 2, half, length)
    scaled = (scaled * inverse_ref[...][:, :, None, :]).astype(low)
    product = scaled.astype(full) * attn.reshape(scaled.shape).astype(full)
    delta[...] = jnp.sum(product, axis=2)
    grad_attn[...] = scaled.reshape(grad_attn.shape)
    slot_low = slot_grad.astype(low)
    second_low = jnp.broadcast_to(second_grad, (16, width)).astype(low)
    early = pairs * (width + experts + 16)
    for index in range(pairs):
        lanes = slice(index * LANES, (index + 1) * LANES)
        sums_ref[index * width : (index + 1) * width] = proj_grad[:, lanes]
        base = width * pairs + index * experts
        sums_ref[base : base + experts] = slot_low[:, lanes]
        base = (width + experts) * pairs + index * 16
        sums_ref[base : base + 16] = second_low[:, lanes]
    used = early + pairs * 3 * width
    if used < sums_ref.shape[0]:
        sums_ref[used:] = jnp.zeros((sums_ref.shape[0] - used, LANES), low)

    for load in loads[7:]:
        load.wait()
    factor = half**-0.5
    none = jnp.zeros((half, TILE), low)

    def one_pair(pair, carry):
        load_probs(pair).wait()
        for head in range(2):
            rows = slice(head * half, (head + 1) * half)
            for start in range(0, length, TILE):
                span = slice(start, start + TILE)
                grad = grad_attn[pair, rows, span]
                parts = [grad, none] if head == 0 else [none, grad]
                grad_probs = dot(values_ref[pair], jnp.concatenate(parts, axis=0))
                probs = probs_ref[2 * pair + head, :, span].astype(full)
                grad_probs = grad_probs - delta[pair, head : head + 1, span]
                grad_scores[head, :, span] = (probs * grad_probs).astype(low)
            scores = grad_scores[head]
            probs = probs_ref[2 * pair + head]
            grads_ref[pair, 2, rows, :] = dot(grad_attn[pair, rows, :], probs, 1, 1).astype(low)
            grads_ref[pair, 0, rows, :] = (dot(keys_ref[pair, rows, :], scores) * factor).astype(low)
            grads_ref[pair, 1, rows, :] = (
                dot(queries_ref[pair, rows, :], scores, 1, 1) * (1.0 / log2_e)
            ).astype(low)
        sums = dot(first_ref[...], grads_ref[pair].reshape(3 * LANES, length), 1, 1).astype(low)

        for index in range(3):
            base = pl.multiple_of(early + (pair * 3 + index) * width, 16)
            sums_ref[pl.ds(base, width)] = sums[:, index * LANES : (index + 1) * LANES]
        save_grads(pair).start()
        return carry

    lax.fori_loop(0, pairs, one_pair, 0)
    for save in saves + [save_grads(pair) for pair in range(pairs)]:
        save.wait()


def padded(rows, devices):
    return -(-rows // (16 * devices)) * 16 * devices


def backward(back, slots, gain, ids, inverse, arrays, probs, devices):
    length, width = arrays[0].shape
    experts = slots.shape[0]
    pairs = width // LANES
    rows = padded(pairs * (4 * width + experts + 16), devices)
    saved = [((length, width), low), ((length, width), full), ((pairs, 3, LANES, length), low)]
    return pl.pallas_call(
        backward_kernel,
        in_specs=[whole_vmem] * 5 + [anywhere] * (len(arrays) + 1),
        out_specs=[anywhere] * 3 + [whole_vmem],
        out_shape=[kept(*entry) for entry in saved] + [shape_of((rows, LANES), low)],
        scratch_shapes=[pltpu.VMEM(array.shape, array.dtype) for array in (*arrays, probs)]
        + [pltpu.VMEM(*entry) for entry in saved]
        + [
            pltpu.VMEM((pairs, LANES, length), low),
            pltpu.VMEM((pairs, 2, length), full),
            pltpu.VMEM((2, length, length), low),
            pltpu.SemaphoreType.DMA((len(arrays),)),
            pltpu.SemaphoreType.DMA((pairs,)),
            pltpu.SemaphoreType.DMA((2 + pairs,)),
        ],
        compiler_params=params(44 + experts // 8),
        cost_estimate=cost(20),
        name="backward",
    )(back, *keep(slots, gain, ids, inverse, *arrays, probs))


def patch_back_kernel(x_ref, gain_ref, weight_ref, resid_ref, grads_ref, result_ref):
    length, width = x_ref.shape
    pairs = width // LANES
    grads = [grads_ref[pair, part] for part in range(3) for pair in range(pairs)]
    grad_first = dot(weight_ref[...], jnp.concatenate(grads, axis=0)).T
    normed, factor = norm_parts(x_ref[...].astype(full))
    gain = gain_ref[...].reshape(1, width)
    result_ref[...] = resid_ref[...] + norm_back(grad_first, normed, factor, gain)


def patch_back(patches, gain, weight, grad_resid, grads):
    return pl.pallas_call(
        patch_back_kernel,
        in_specs=[whole_vmem] * 5,
        out_specs=whole_vmem,
        out_shape=kept(patches.shape, full),
        compiler_params=params(20),
        cost_estimate=cost(3),
        name="patch_back",
    )(*keep(patches, gain, weight, grad_resid, grads))


def weights_kernel(copies, *refs):
    received = refs[:copies]
    up_ref, down_ref, up_grad_ref, down_grad_ref, slots, grads = refs[copies:]
    expert = pl.program_id(0)
    groups, _, own, width = received[0].shape
    count = groups * IMG_ROW
    for index in range(own // IMG_ROW):

        @pl.when(jnp.logical_and(expert == index, pl.program_id(1) == 0))
        def _():
            for copy, ref in enumerate(received):
                rows = slice(copy * count, (copy + 1) * count)
                slots[rows] = own_rows(ref[:, 0].astype(full), index)
                grads[rows] = own_rows(ref[:, 1].astype(full), index)

    pre = dot(slots[...], up_ref[0])
    cdf, pdf = gelu_parts(pre)
    down_grad_ref[0] = dot((pre * cdf).astype(low), grads[...], 0, 0)
    grad_hidden = dot(grads[...], down_ref[0], 1, 1)
    grad_pre = (grad_hidden * (cdf + pre * pdf)).astype(low)
    up_grad_ref[0] = dot(slots[...], grad_pre, 0, 0)


def weight_grads(received, up, down):
    groups, _, _, width = received[0].shape
    experts, _, hidden = up.shape
    copies = len(received)
    tile = hidden // 3
    up_spec = pl.BlockSpec((1, width, tile), lambda expert, step: (expert, 0, step))
    down_spec = pl.BlockSpec((1, tile, width), lambda expert, step: (expert, step, 0))
    rows = (copies * groups * IMG_ROW, width)

    def kernel(*refs):
        weights_kernel(copies, *refs)

    return pl.pallas_call(
        kernel,
        grid=(experts, 3),
        in_specs=[whole_vmem] * copies + [up_spec, down_spec],
        out_specs=[up_spec, down_spec],
        out_shape=[kept(up.shape, full), kept(down.shape, full)],
        scratch_shapes=[pltpu.VMEM(rows, low)] * 2,
        compiler_params=params(40),
        cost_estimate=cost(9),
        name="weight_grads",
    )(*keep(*received, up, down))


def position(place_ref):
    expert, row = place_ref[0], place_ref[1]
    return row % 2, row // 2 * 2 + expert % 2, expert // 2


def flipped(index, step):
    return jnp.bitwise_xor(index, step)


def rows_at(index, count):
    return pl.ds(pl.multiple_of(index * count, 16), count)


def small_call(kernel, out_shape, name, *arrays, scratch=(), limit=16):
    return pl.pallas_call(
        kernel,
        in_specs=[pl.BlockSpec(memory_space=pltpu.SMEM)] + [whole_vmem] * (len(arrays) - 1),
        out_specs=jax.tree.map(lambda _: whole_vmem, out_shape),
        out_shape=out_shape,
        scratch_shapes=scratch,
        compiler_params=params(limit),
        cost_estimate=cost(1),
        name=name,
    )(*arrays)


def core_kernel(place_ref, mine_ref, other_ref, *outs):
    core, quarter, _ = position(place_ref)
    count = outs[0].shape[0]
    for step, out in enumerate(outs):
        rows = rows_at(core * 4 + flipped(quarter, step), count)
        out[...] = (mine_ref[rows].astype(full) + other_ref[rows].astype(full)).astype(out.dtype)


def plane_kernel(place_ref, *refs):
    total = refs[0][...]
    for other in refs[1:-1]:
        total = total + other[...].astype(full)
    refs[-1][...] = total.astype(low)


def line_kernel(place_ref, *refs):
    _, _, layer = position(place_ref)
    pieces, out, terms = refs[:-2], refs[-2], refs[-1]
    for step, piece in enumerate(pieces):
        terms[flipped(layer, step)] = piece[...]
    out[...] = jnp.sum(terms[...].astype(full), axis=0).astype(low)


def finish_parts(place_ref, parts, whole):
    core, quarter, _ = position(place_ref)
    for index, part in enumerate(parts):
        half = flipped(core, index // 4)
        whole[rows_at(half * 4 + flipped(quarter, index % 4), part.shape[0])] = part[...]


def finish_kernel(
    total, place_ref, weight_ref, gain_ref, *refs
):
    parts = refs[:8]
    first_ref, qkv_ref, proj_ref, second_ref, slot_ref, sums = refs[8:]
    finish_parts(place_ref, parts, sums)
    width = weight_ref.shape[0]
    pairs = width // LANES
    own = slot_ref.shape[0]
    base = (width + total + 16) * pairs
    seconds = []
    for index in range(pairs):
        lanes = slice(index * LANES, (index + 1) * LANES)
        proj_ref[:, lanes] = sums[index * width : (index + 1) * width].astype(full)
        start = (width + total) * pairs + index * 16
        seconds.append(sums[start : start + 16].astype(full)[0:1])
        start = width * pairs + index * total
        row = lax.broadcasted_iota(jnp.int32, (own, total), 0) + place_ref[0] * own
        column = lax.broadcasted_iota(jnp.int32, (own, total), 1)
        chosen = (row == column).astype(full).astype(low)
        slot_ref[:, lanes] = dot(chosen, sums[start : start + total])
    second_ref[...] = jnp.concatenate(seconds, axis=1).reshape(width)
    first = jnp.zeros((width, 1), full)
    for pair in range(pairs):
        for part in range(3):
            lanes = slice(part * width + pair * LANES, part * width + (pair + 1) * LANES)
            start = base + (pair * 3 + part) * width
            grad = sums[start : start + width].astype(full)
            qkv_ref[:, lanes] = grad
            product = grad * weight_ref[:, lanes].astype(full)
            first = first + jnp.sum(product, axis=1, keepdims=True)
    row = jnp.broadcast_to(first, (width, LANES)).T[0:1]
    first_ref[...] = (row / gain_ref[...].reshape(1, width)).reshape(width)


def finish(place, parts, weight, gain, experts, own):
    width = weight.shape[0]

    def kernel(*refs):
        finish_kernel(experts, *refs)

    return pl.pallas_call(
        kernel,
        in_specs=[pl.BlockSpec(memory_space=pltpu.SMEM)] + [whole_vmem] * (2 + len(parts)),
        out_specs=[whole_vmem] * 5,
        out_shape=[
            shape_of((width,), full),
            shape_of(weight.shape, full),
            shape_of((width, width), full),
            shape_of((width,), full),
            shape_of((own, width), full),
        ],
        scratch_shapes=[pltpu.VMEM((sum(part.shape[0] for part in parts), LANES), low)],
        compiler_params=params(20),
        cost_estimate=cost(3),
        name="finish",
    )(place, *keep(weight, gain), *parts)


def per_device(
    patches,
    image_ids,
    first_gain,
    qkv_weight,
    proj_weight,
    second_gain,
    slot_params,
    up_weight,
    down_weight,
    cotangent,
):
    groups = lax.axis_size("expert")
    copies = lax.axis_size("rows")
    devices = groups * copies
    _, length, width = patches.shape
    own = slot_params.shape[1]
    experts = own * groups
    spread = jnp.broadcast_to(slot_params.T[None], (groups, own, width))
    slots = lax.all_to_all(spread, "expert", 0, 0, tiled=True).reshape(experts, width)
    patches = patches[0]
    cotangent = cotangent[0]
    probs, queries, keys, values, first_in, attn, inverse, resid, second_in = attend(
        patches, image_ids, first_gain, qkv_weight, proj_weight, second_gain
    )
    dispatch, combine, send = route(second_in, slots, image_ids, cotangent, groups)
    received = lax.all_to_all(send, "expert", 0, 0, tiled=True)
    back = run_experts(received, up_weight, down_weight)
    back = lax.all_to_all(back, "expert", 0, 0, tiled=True)
    others = [
        lax.ppermute(received, "rows", [(index, index ^ step) for index in range(copies)])
        for step in range(1, copies)
    ]
    saved = [cotangent, combine, second_in, dispatch, resid, attn, proj_weight]
    saved += [values, keys, queries, first_in]
    output, grad_resid, grads, terms = backward(
        back, slots, second_gain, image_ids, inverse, saved, probs, devices
    )
    place = jnp.stack([lax.axis_index("expert"), lax.axis_index("rows")]).astype(jnp.int32)
    layers = groups // 2

    def flip(array, expert, row):
        pairs = [
            (index, (index // copies ^ expert) * copies + (index % copies ^ row))
            for index in range(devices)
        ]
        return lax.ppermute(array, both_axes, pairs)

    terms, others = lax.optimization_barrier((terms, others))
    share = terms.shape[0] // devices
    quarter = (layers * share, LANES)
    mine, *sends = small_call(
        core_kernel, [shape_of(quarter, full)] + [shape_of(quarter, low)] * 3, "add_core",
        place, terms, flip(terms, 0, 1),
    )
    arrived = [flip(send, step % 2, step // 2 * 2) for step, send in enumerate(sends, 1)]
    grads, _ = lax.optimization_barrier((grads, mine))
    patch_grad = patch_back(patches, first_gain, qkv_weight, grad_resid, grads)
    arrived, patch_grad = lax.optimization_barrier((arrived, patch_grad))
    mine = small_call(plane_kernel, shape_of(quarter, low), "add_plane", place, mine, *arrived)
    arrived = [flip(mine, step * 2, 0) for step in range(1, layers)]
    others, _ = lax.optimization_barrier((others, mine))
    up_grad, down_grad = weight_grads([received] + others, up_weight, down_weight)
    arrived, up_grad, down_grad = lax.optimization_barrier((arrived, up_grad, down_grad))
    mine = small_call(
        line_kernel, shape_of(quarter, low), "add_line", place, mine, *arrived,
        scratch=[pltpu.VMEM((layers, *quarter), low)], limit=12 + layers,
    )
    arrived = [flip(mine, step % 2, step // 2 * 2) for step in range(1, 4)]
    parts = [mine] + arrived
    parts = parts + [flip(part, 0, 1) for part in parts]
    first_grad, qkv_grad, proj_grad, second_grad, slot_grad = finish(
        place, parts, qkv_weight, first_gain, experts, own
    )
    return (
        output[None],
        patch_grad[None],
        first_grad,
        qkv_grad,
        proj_grad,
        second_grad,
        slot_grad.T,
        up_grad,
        down_grad,
    )


def solution(mesh):
    return jax.shard_map(
        per_device,
        mesh=mesh,
        in_specs=(
            P(("expert", "rows"), None, None),
            P(("expert", "rows"), None),
            P(),
            P(),
            P(),
            P(),
            P(None, "expert"),
            P("expert", None, None),
            P("expert", None, None),
            P(("expert", "rows"), None, None),
        ),
        out_specs=(
            P(("expert", "rows"), None, None),
            P(("expert", "rows"), None, None),
            P(),
            P(),
            P(),
            P(),
            P(None, "expert"),
            P("expert", None, None),
            P("expert", None, None),
        ),
        check_vma=False,
    )
```

time: 145 us -> 120 us (0.83)
  waiting for transfers between devices: 28.7 us -> 17.6 us
  blocking collectives: 23.9 us -> 13.6 us
  Pallas kernels: 69.6 us -> 60.6 us
  starting transfers between devices: 19.2 us -> 24.4 us
    ppermute x3, waiting for transfers between devices: 15.3 us -> 0.01 us  [per_device(): lax.ppermute(received, 'rows', [(index, index ^ step) for index in range(...]
    ppermute x2 -> x14, starting transfers between devices: 0.07 us -> 11.6 us  [flip(): return lax.ppermute(array, both_axes, pairs)]
    all_to_all x1 -> x0, blocking collectives: 10.3 us -> none  [per_device(): back = lax.all_to_all(back, 'expert', 0, 0, tiled=True)]
    ppermute x2 -> x14, waiting for transfers between devices: 5.03 us -> 12 us  [flip(): return lax.ppermute(array, both_axes, pairs)]
    all_to_all x2 -> x1, starting transfers between devices: 9.77 us -> 3.58 us  [per_device(): back = lax.all_to_all(back, 'expert', 0, 0, tiled=True)]
    pallas_call x6 -> x7, Pallas kernels: 33.7 us -> 27.7 us  [the longest x1 12.5 us: attend(): pl.pallas_call(attend_kernel, grid=(pairs,), in_specs=[whole_vmem] * 6, o...]
    pallas_call x1, Pallas kernels: 23.5 us -> 20.5 us  [backward(): pl.pallas_call(backward_kernel, in_specs=[whole_vmem] * 5 + [anywhere] *...]
    all_to_all x2 -> x1, waiting for transfers between devices: 8.36 us -> 5.6 us  [per_device(): back = lax.all_to_all(back, 'expert', 0, 0, tiled=True)]
  transfers between devices with their start and end apart: 8 -> 19, of which waited for: 5 -> 8; matrix products, arithmetic and copies ran while one was open for 0% -> 0% of each run, Pallas kernels for 22% -> 40%
where the time goes in v3:
time: 120 us; the launch traced here: 119 us
  Pallas kernels  60.6 us (50%)
  starting transfers between devices  24.4 us (20%)
  waiting for transfers between devices  17.6 us (15%)
  blocking collectives  13.6 us (11%)
  local copies, waits for them, and re-layouts  1.48 us (1%)
    pallas_call x1, Pallas kernels, backward(): pl.pallas_call(backward_kernel, in_specs=[whole_vmem] * 5 + [anywhere] *...  20.5 us
    all_to_all x1, blocking collectives, per_device(): received = lax.all_to_all(send, 'expert', 0, 0, tiled=True)  13.6 us
    pallas_call x1, Pallas kernels, attend(): pl.pallas_call(attend_kernel, grid=(pairs,), in_specs=[whole_vmem] * 6, o...  12.5 us
    ppermute x14, waiting for transfers between devices, flip(): return lax.ppermute(array, both_axes, pairs)  12 us
    ppermute x14, starting transfers between devices, flip(): return lax.ppermute(array, both_axes, pairs)  11.6 us
    pallas_call x1, Pallas kernels, weight_grads(): pl.pallas_call(kernel, grid=(experts, 3), in_specs=[whole_vmem] * copies...  9.29 us
    all_to_all x1, starting transfers between devices, per_device(): lax.all_to_all(spread, 'expert', 0, 0, tiled=True).reshape(experts, width)  7.25 us
    all_to_all x1, waiting for transfers between devices, per_device(): back = lax.all_to_all(back, 'expert', 0, 0, tiled=True)  5.6 us
  transfers between devices with their start and end apart: 19, of which 8 were waited for; matrix products, arithmetic and copies ran while one was open for 0% of the time, Pallas kernels for 40%

profile of v3, /device:TPU:0, one launch (start us, length us, event | category | flops | bytes accessed | tf_op | source)
XLA Modules:
  0.0 118.6 jit_solution(829892266728841582)
XLA Ops:
  0.6 0.0 copy-start
  0.7 1.4 %broadcast_in_dim.12 = bf16[8,2,384]{2,1,0:T(2,128)(2,1)} broadcast(bf16[2,384]{1,0:T(2,128)(2,1)} %bitcast.13), dimensions={1,2} | broadcast | bytes 13824 | tf_op jit(solution)/shard_map/broadcast_in_dim | solution.py:694
  2.1 7.3 %all-to-all-start = ((bf16[8,2,384]{2,1,0:T(2,128)(2,1)}), bf16[8,2,384]{2,1,0:T(2,128)(2,1)S(1)}, u32[]{:S(2)}, u32[]{:S(2)}) async-start(bf16[8,2,384]{2,1,0:T(2,128)(2,1)} %broadcast_in_dim.12), calls=%async_computation | async-start | bytes 24576 | tf_op jit(solution)/shard_map/all_to_all | solution.py:695
  9.3 12.5 %attend.1 = (bf16[6,1024,1024]{2,1,0:T(8,128)(2,1)}, bf16[3,128,1024]{2,1,0:T(8,128)(2,1)}, bf16[3,128,1024]{2,1,0:T(8,128)(2,1)}, bf16[3,1024,128]{2,1,0:T(8,12...) custom-call(bf16[1024,384]{1,0:T(8,128)(2,1)} %bitcast.10, ...), custom_call_target="tpu_custom_call" | custom-call | bytes 61200000 | tf_op jit(solution)/shard_map/attend/pallas_call | solution.py:194
  21.9 0.0 all-to-all-done
  21.9 0.0 copy-start.2
  21.9 3.1 %route.1 = (f32[16,8,1024]{2,1,0:T(8,128)}, f32[16,8,1024]{2,1,0:T(8,128)}, bf16[8,2,16,384]{3,2,1,0:T(8,128)(2,1)S(1)}) custom-call(bf16[1024,384]{1,0:T(8,128)(2,1)} %get-tuple-element.53.second_ref.refs_2_, bf16[16,384]{1,0:T(8,128)(2,1)S(1)} %reshape.22.slots_ref, s32[1,1024]{1,0:T(1,128)} %ids_ref.5, bf16[1024,384]{1,0:T(8,128)(2,1)} %bitcast.8), custom_call_target="tpu_custom_call" | custom-call | bytes 10800000 | tf_op jit(solution)/shard_map/route/pallas_call | solution.py:262
  25.0 13.6 %all_to_all.15.received_ref.refs_0_ = bf16[8,2,16,384]{3,2,1,0:T(8,128)(2,1)S(1)} all-to-all(bf16[8,2,16,384]{3,2,1,0:T(8,128)(2,1)S(1)} %get-tuple-element.54), channel_id=1, replica_groups=mesh['expert'=8,'rows'=4] {'expert'}, dimensions={0} | all-to-all | bytes 393216 | tf_op jit(solution)/shard_map/all_to_all | solution.py:702
  38.6 0.0 copy-done
  38.6 0.0 copy-start.1
  38.6 4.5 %run_experts.1 = bf16[8,2,16,384]{3,2,1,0:T(8,128)(2,1)} custom-call(bf16[8,2,16,384]{3,2,1,0:T(8,128)(2,1)S(1)} %all_to_all.15.received_ref.refs_0_, bf16[2,384,1536]{2,1,0:T(8,128)(2,1)S(1)} %copy-done, bf16[2,1536,384]{2,1,0:T(8,128)(2,1)} %refs_5_.1), custom_call_target="tpu_custom_call" | custom-call | bytes 10800000 | tf_op jit(solution)/shard_map/run_experts/pallas_call | solution.py:312
  43.1 0.0 copy-done.2
  43.1 3.6 %all-to-all-start.2 = ((bf16[8,2,16,384]{3,2,1,0:T(8,128)(2,1)}), bf16[8,2,16,384]{3,2,1,0:T(8,128)(2,1)S(1)}, u32[]{:S(2)}, u32[]{:S(2)}) async-start(bf16[8,2,16,384]{3,2,1,0:T(8,128)(2,1)} %run_experts.1), calls=%async_computation.2 | async-start | bytes 393216 | tf_op jit(solution)/shard_map/all_to_all | solution.py:704
  46.7 0.1 collective-permute-start
  46.7 1.6 %collective-permute-start.1 = (bf16[8,2,16,384]{3,2,1,0:T(8,128)(2,1)S(1)}, bf16[8,2,16,384]{3,2,1,0:T(8,128)(2,1)S(1)}, u32[]{:S(2)}, u32[]{:S(2)}) collective-permute-start(bf16[8,2,16,384]{3,2,1,0:T(8,128)(2,1)S(1)} %all_to_all.15.received_ref.refs_0_), channel_id=1, source_target_pairs={{0,2},{1,3},{2,0},{3,1},{4,6},{5,7},{6,4},{7,5},{8,10},{9,11},{10,... | collective-permute-start | bytes 589832 | tf_op jit(solution)/shard_map/ppermute | solution.py:706
  48.3 0.0 copy-done.1
  48.3 0.3 collective-permute-start.2
  48.6 5.6 %all-to-all-done.2.back_ref = bf16[8,2,16,384]{3,2,1,0:T(8,128)(2,1)S(1)} async-done(((bf16[8,2,16,384]{3,2,1,0:T(8,128)(2,1)}), bf16[8,2,16,384]{3,2,1,0:T(8,128)(2,1)S(1)}, u32[]{:S(2)}, u32[]{:S(2)}) %all-to-all-start.2) | async-done | bytes 196640 | tf_op jit(solution)/shard_map/all_to_all | solution.py:704
  54.2 20.5 %backward.1 = (bf16[1024,384]{1,0:T(8,128)(2,1)}, f32[1024,384]{1,0:T(8,128)}, bf16[3,3,128,1024]{3,2,1,0:T(8,128)(2,1)}, bf16[5120,128]{1,0:T(8,128)(2,1)S(1)}) custom-call(bf16[8,2,16,384]{3,2,1,0:T(8,128)(2,1)S(1)} %all-to-all-done.2.back_ref, bf16[16,384]{1,0:T(8,128)(2,1)} %copy-done.2, f32[384]{0:T(512)} %gain_ref.4, s32[1,1024]{1,0:T(1,128)} %ids_ref.5, ...), custom_call_target="tpu_custom_call" | custom-call | bytes 72000000 | tf_op jit(solution)/shard_map/backward/pallas_call | solution.py:470
  74.8 0.0 collective-permute-done.refs_1_
  74.8 0.0 copy-start.3
  74.8 0.0 collective-permute-done.1.refs_2_
  74.8 0.0 copy-start.4
  74.8 0.0 collective-permute-done.2.refs_3_
  74.8 0.0 copy-start.5
  74.8 0.1 collective-permute-start.3
  74.9 0.1 pad_add_fusion.place_ref.refs_0_
  75.0 2.9 %collective-permute-done.3.other_ref = bf16[5120,128]{1,0:T(8,128)(2,1)S(1)} collective-permute-done((bf16[5120,128]{1,0:T(8,128)(2,1)S(1)}, bf16[5120,128]{1,0:T(8,128)(2,1)S(1)}, u32[]{:S(2)}, u32[]{:S(2)}) %collective-permute-start.3) | collective-permute-done | bytes 1310752 | tf_op jit(solution)/shard_map/ppermute | solution.py:722
  77.9 0.7 add_core.1
  78.6 0.1 collective-permute-start.4
  78.7 1.5 %collective-permute-start.5 = (bf16[640,128]{1,0:T(8,128)(2,1)S(1)}, bf16[640,128]{1,0:T(8,128)(2,1)S(1)}, u32[]{:S(2)}, u32[]{:S(2)}) collective-permute-start(bf16[640,128]{1,0:T(8,128)(2,1)S(1)} %get-tuple-element.69), channel_id=1, source_target_pairs={{0,2},{1,3},{2,0},{3,1},{4,6},{5,7},{6,4},{7,5},{8,10},{9,11},{10,... | collective-permute-start | bytes 491528 | tf_op jit(solution)/shard_map/ppermute | solution.py:722
  80.3 1.9 %collective-permute-start.6 = (bf16[640,128]{1,0:T(8,128)(2,1)S(1)}, bf16[640,128]{1,0:T(8,128)(2,1)S(1)}, u32[]{:S(2)}, u32[]{:S(2)}) collective-permute-start(bf16[640,128]{1,0:T(8,128)(2,1)S(1)} %get-tuple-element.70), channel_id=1, source_target_pairs={{0,6},{1,7},{2,4},{3,5},{4,2},{5,3},{6,0},{7,1},{8,14},{9,15},{10,... | collective-permute-start | bytes 491528 | tf_op jit(solution)/shard_map/ppermute | solution.py:722
  82.2 5.6 %patch_back.1 = f32[1024,384]{1,0:T(8,128)} custom-call(bf16[1024,384]{1,0:T(8,128)(2,1)} %bitcast.11, f32[384]{0:T(512)} %refs_2_.1, bf16[384,1152]{1,0:T(8,128)(2,1)} %refs_1_.1, f32[1024,384]{1,0:T(8,128)} %get-tuple-element.71.resid_ref, bf16[3,3,128,1024]{3,2,1,0:T(8,128)(2,1)} %get-tuple-element.74.grads_ref), custom_call_target="tpu_custom_call" | custom-call | bytes 10800000 | tf_op jit(solution)/shard_map/patch_back/pallas_call | solution.py:502
  87.8 0.0 copy-done.3
  87.8 0.0 copy-done.4
  87.8 0.0 copy-done.5
  87.8 0.0 collective-permute-done.4.refs_1_
  87.8 0.0 collective-permute-done.5.refs_2_
  87.8 1.6 %collective-permute-done.6.refs_3_ = bf16[640,128]{1,0:T(8,128)(2,1)S(1)} collective-permute-done((bf16[640,128]{1,0:T(8,128)(2,1)S(1)}, bf16[640,128]{1,0:T(8,128)(2,1)S(1)}, u32[]{:S(2)}, u32[]{:S(2)}) %collective-permute-start.6) | collective-permute-done | bytes 163872 | tf_op jit(solution)/shard_map/ppermute | solution.py:722
  89.4 0.6 add_plane.1.refs_0_
  90.0 0.2 collective-permute-start.7
  90.2 1.1 collective-permute-start.8
  91.3 3.2 %collective-permute-start.9 = (bf16[640,128]{1,0:T(8,128)(2,1)S(1)}, bf16[640,128]{1,0:T(8,128)(2,1)S(1)}, u32[]{:S(2)}, u32[]{:S(2)}) collective-permute-start(bf16[640,128]{1,0:T(8,128)(2,1)S(1)} %add_plane.1.refs_0_), channel_id=1, source_target_pairs={{0,24},{1,25},{2,26},{3,27},{4,28},{5,29},{6,30},{7,31},{8,16},{9,... | collective-permute-start | bytes 491528 | tf_op jit(solution)/shard_map/ppermute | solution.py:722
  94.5 9.3 %weight_grads.1 = (f32[2,384,1536]{2,1,0:T(8,128)}, f32[2,1536,384]{2,1,0:T(8,128)}) custom-call(bf16[8,2,16,384]{3,2,1,0:T(8,128)(2,1)} %copy-done.1, bf16[8,2,16,384]{3,2,1,0:T(8,128)(2,1)} %copy-done.3, bf16[8,2,16,384]{3,2,1,0:T(8,128)(2,1)} %copy-done.4, bf16[8,2,16,384]{3,2,1,0:T(8,128)(2,1)} %copy-done.5, bf16[2,384,1536]{2,1,0:T(8,128)(2,1)} %refs_4_.1, ...), custom_call_target="tpu_custom_call" | custom-call | bytes 32400000 | tf_op jit(solution)/shard_map/weight_grads/pallas_call | solution.py:548
  103.8 0.0 collective-permute-done.7.refs_1_
  103.8 1.2 collective-permute-done.8.refs_2_
  105.0 0.0 collective-permute-done.9.refs_3_
  105.0 0.7 add_line.1.refs_3_
  105.7 1.0 collective-permute-start.10
  106.7 1.2 %collective-permute-start.11 = (bf16[640,128]{1,0:T(8,128)(2,1)S(1)}, bf16[640,128]{1,0:T(8,128)(2,1)S(1)}, u32[]{:S(2)}, u32[]{:S(2)}) collective-permute-start(bf16[640,128]{1,0:T(8,128)(2,1)S(1)} %add_line.1.refs_3_), channel_id=1, source_target_pairs={{0,2},{1,3},{2,0},{3,1},{4,6},{5,7},{6,4},{7,5},{8,10},{9,11},{10,... | collective-permute-start | bytes 491528 | tf_op jit(solution)/shard_map/ppermute | solution.py:722
  107.9 1.3 %collective-permute-start.12 = (bf16[640,128]{1,0:T(8,128)(2,1)S(1)}, bf16[640,128]{1,0:T(8,128)(2,1)S(1)}, u32[]{:S(2)}, u32[]{:S(2)}) collective-permute-start(bf16[640,128]{1,0:T(8,128)(2,1)S(1)} %add_line.1.refs_3_), channel_id=1, source_target_pairs={{0,6},{1,7},{2,4},{3,5},{4,2},{5,3},{6,0},{7,1},{8,14},{9,15},{10,... | collective-permute-start | bytes 491528 | tf_op jit(solution)/shard_map/ppermute | solution.py:722
  109.2 0.0 collective-permute-start.13
  109.3 1.9 %collective-permute-done.10.refs_4_ = bf16[640,128]{1,0:T(8,128)(2,1)S(1)} collective-permute-done((bf16[640,128]{1,0:T(8,128)(2,1)S(1)}, bf16[640,128]{1,0:T(8,128)(2,1)S(1)}, u32[]{:S(2)}, u32[]{:S(2)}) %collective-permute-start.10) | collective-permute-done | bytes 163872 | tf_op jit(solution)/shard_map/ppermute | solution.py:722
  111.1 0.0 collective-permute-start.14
  111.1 0.8 collective-permute-done.11.refs_5_
  112.0 0.0 collective-permute-start.15
  112.0 2.1 %collective-permute-done.12.refs_6_ = bf16[640,128]{1,0:T(8,128)(2,1)S(1)} collective-permute-done((bf16[640,128]{1,0:T(8,128)(2,1)S(1)}, bf16[640,128]{1,0:T(8,128)(2,1)S(1)}, u32[]{:S(2)}, u32[]{:S(2)}) %collective-permute-start.12) | collective-permute-done | bytes 163872 | tf_op jit(solution)/shard_map/ppermute | solution.py:722
  114.1 0.0 collective-permute-start.16
  114.1 0.0 collective-permute-done.13.refs_7_
  114.1 0.0 collective-permute-done.14.refs_8_
  114.1 0.0 collective-permute-done.15.refs_9_
  114.1 1.4 %collective-permute-done.16.refs_10_ = bf16[640,128]{1,0:T(8,128)(2,1)S(1)} collective-permute-done((bf16[640,128]{1,0:T(8,128)(2,1)S(1)}, bf16[640,128]{1,0:T(8,128)(2,1)S(1)}, u32[]{:S(2)}, u32[]{:S(2)}) %collective-permute-start.16) | collective-permute-done | bytes 163872 | tf_op jit(solution)/shard_map/ppermute | solution.py:722
  115.5 3.1 %finish.1 = (f32[384]{0:T(512)}, f32[384,1152]{1,0:T(8,128)}, f32[384,384]{1,0:T(8,128)}, f32[384]{0:T(512)}, f32[2,384]{1,0:T(2,128)}) custom-call(s32[2]{0:T(128)S(1)} %pad_add_fusion.place_ref.refs_0_, bf16[384,1152]{1,0:T(8,128)(2,1)} %refs_1_.1, f32[384]{0:T(512)} %refs_2_.1, bf16[640,128]{1,0:T(8,128)(2,1)S(1)} %add_line.1.refs_3_, ...), custom_call_target="tpu_custom_call" | custom-call | bytes 10800000 | tf_op jit(solution)/shard_map/finish/pallas_call | solution.py:658
  (1 shorter events, 0.0 us)
Async XLA Ops:
  0.6 37.9 %copy-start = (bf16[2,384,1536]{2,1,0:T(8,128)(2,1)S(1)}, bf16[2,384,1536]{2,1,0:T(8,128)(2,1)}, u32[]{:S(2)}) copy-start(bf16[2,384,1536]{2,1,0:T(8,128)(2,1)} %refs_4_.1) | copy-start | bytes 7077892
  2.1 19.8 %all-to-all-start = ((bf16[8,2,384]{2,1,0:T(2,128)(2,1)}), bf16[8,2,384]{2,1,0:T(2,128)(2,1)S(1)}, u32[]{:S(2)}, u32[]{:S(2)}) async-start(bf16[8,2,384]{2,1,0:T(2,128)(2,1)} %broadcast_in_dim.12), calls=%async_computation | async-start | bytes 24576 | tf_op jit(solution)/shard_map/all_to_all | solution.py:695
  21.9 21.2 %copy-start.2 = (bf16[16,384]{1,0:T(8,128)(2,1)}, bf16[16,384]{1,0:T(8,128)(2,1)S(1)}, u32[]{:S(2)}) copy-start(bf16[16,384]{1,0:T(8,128)(2,1)S(1)} %reshape.22.slots_ref) | copy-start | bytes 36868
  38.6 9.7 %copy-start.1 = (bf16[8,2,16,384]{3,2,1,0:T(8,128)(2,1)}, bf16[8,2,16,384]{3,2,1,0:T(8,128)(2,1)S(1)}, u32[]{:S(2)}) copy-start(bf16[8,2,16,384]{3,2,1,0:T(8,128)(2,1)S(1)} %all_to_all.15.received_ref.refs_0_) | copy-start | bytes 589828
  43.1 11.1 %all-to-all-start.2 = ((bf16[8,2,16,384]{3,2,1,0:T(8,128)(2,1)}), bf16[8,2,16,384]{3,2,1,0:T(8,128)(2,1)S(1)}, u32[]{:S(2)}, u32[]{:S(2)}) async-start(bf16[8,2,16,384]{3,2,1,0:T(8,128)(2,1)} %run_experts.1), calls=%async_computation.2 | async-start | bytes 393216 | tf_op jit(solution)/shard_map/all_to_all | solution.py:704
  46.7 28.1 %collective-permute-start = (bf16[8,2,16,384]{3,2,1,0:T(8,128)(2,1)S(1)}, bf16[8,2,16,384]{3,2,1,0:T(8,128)(2,1)S(1)}, u32[]{:S(2)}, u32[]{:S(2)}) collective-permute-start(bf16[8,2,16,384]{3,2,1,0:T(8,128)(2,1)S(1)} %all_to_all.15.received_ref.refs_0_), channel_id=1, source_target_pairs={{0,1},{1,0},{2,3},{3,2},{4,5},{5,4},{6,7},{7,6},{8,9},{9,8},{10,11... | collective-permute-start | bytes 589832 | tf_op jit(solution)/shard_map/ppermute | solution.py:706
  46.7 28.0 %collective-permute-start.1 = (bf16[8,2,16,384]{3,2,1,0:T(8,128)(2,1)S(1)}, bf16[8,2,16,384]{3,2,1,0:T(8,128)(2,1)S(1)}, u32[]{:S(2)}, u32[]{:S(2)}) collective-permute-start(bf16[8,2,16,384]{3,2,1,0:T(8,128)(2,1)S(1)} %all_to_all.15.received_ref.refs_0_), channel_id=1, source_target_pairs={{0,2},{1,3},{2,0},{3,1},{4,6},{5,7},{6,4},{7,5},{8,10},{9,11},{10,... | collective-permute-start | bytes 589832 | tf_op jit(solution)/shard_map/ppermute | solution.py:706
  48.3 26.5 %collective-permute-start.2 = (bf16[8,2,16,384]{3,2,1,0:T(8,128)(2,1)S(1)}, bf16[8,2,16,384]{3,2,1,0:T(8,128)(2,1)S(1)}, u32[]{:S(2)}, u32[]{:S(2)}) collective-permute-start(bf16[8,2,16,384]{3,2,1,0:T(8,128)(2,1)S(1)} %all_to_all.15.received_ref.refs_0_), channel_id=1, source_target_pairs={{0,3},{1,2},{2,1},{3,0},{4,7},{5,6},{6,5},{7,4},{8,11},{9,10},{10,... | collective-permute-start | bytes 589832 | tf_op jit(solution)/shard_map/ppermute | solution.py:706
  74.8 13.0 %copy-start.3 = (bf16[8,2,16,384]{3,2,1,0:T(8,128)(2,1)}, bf16[8,2,16,384]{3,2,1,0:T(8,128)(2,1)S(1)}, u32[]{:S(2)}) copy-start(bf16[8,2,16,384]{3,2,1,0:T(8,128)(2,1)S(1)} %collective-permute-done.refs_1_) | copy-start | bytes 589828
  74.8 13.0 %copy-start.4 = (bf16[8,2,16,384]{3,2,1,0:T(8,128)(2,1)}, bf16[8,2,16,384]{3,2,1,0:T(8,128)(2,1)S(1)}, u32[]{:S(2)}) copy-start(bf16[8,2,16,384]{3,2,1,0:T(8,128)(2,1)S(1)} %collective-permute-done.1.refs_2_) | copy-start | bytes 589828
  74.8 13.0 %copy-start.5 = (bf16[8,2,16,384]{3,2,1,0:T(8,128)(2,1)}, bf16[8,2,16,384]{3,2,1,0:T(8,128)(2,1)S(1)}, u32[]{:S(2)}) copy-start(bf16[8,2,16,384]{3,2,1,0:T(8,128)(2,1)S(1)} %collective-permute-done.2.refs_3_) | copy-start | bytes 589828
  74.8 3.1 %collective-permute-start.3 = (bf16[5120,128]{1,0:T(8,128)(2,1)S(1)}, bf16[5120,128]{1,0:T(8,128)(2,1)S(1)}, u32[]{:S(2)}, u32[]{:S(2)}) collective-permute-start(bf16[5120,128]{1,0:T(8,128)(2,1)S(1)} %get-tuple-element.67.mine_ref), channel_id=1, source_target_pairs={{0,1},{1,0},{2,3},{3,2},{4,5},{5,4},{6,7},{7,6},{8,9},{9,8},{10,11... | collective-permute-start | bytes 3932168 | tf_op jit(solution)/shard_map/ppermute | solution.py:722
  78.6 9.1 %collective-permute-start.4 = (bf16[640,128]{1,0:T(8,128)(2,1)S(1)}, bf16[640,128]{1,0:T(8,128)(2,1)S(1)}, u32[]{:S(2)}, u32[]{:S(2)}) collective-permute-start(bf16[640,128]{1,0:T(8,128)(2,1)S(1)} %get-tuple-element.68), channel_id=1, source_target_pairs={{0,4},{1,5},{2,6},{3,7},{4,0},{5,1},{6,2},{7,3},{8,12},{9,13},{10,... | collective-permute-start | bytes 491528 | tf_op jit(solution)/shard_map/ppermute | solution.py:722
  78.7 9.0 %collective-permute-start.5 = (bf16[640,128]{1,0:T(8,128)(2,1)S(1)}, bf16[640,128]{1,0:T(8,128)(2,1)S(1)}, u32[]{:S(2)}, u32[]{:S(2)}) collective-permute-start(bf16[640,128]{1,0:T(8,128)(2,1)S(1)} %get-tuple-element.69), channel_id=1, source_target_pairs={{0,2},{1,3},{2,0},{3,1},{4,6},{5,7},{6,4},{7,5},{8,10},{9,11},{10,... | collective-permute-start | bytes 491528 | tf_op jit(solution)/shard_map/ppermute | solution.py:722
  80.3 9.1 %collective-permute-start.6 = (bf16[640,128]{1,0:T(8,128)(2,1)S(1)}, bf16[640,128]{1,0:T(8,128)(2,1)S(1)}, u32[]{:S(2)}, u32[]{:S(2)}) collective-permute-start(bf16[640,128]{1,0:T(8,128)(2,1)S(1)} %get-tuple-element.70), channel_id=1, source_target_pairs={{0,6},{1,7},{2,4},{3,5},{4,2},{5,3},{6,0},{7,1},{8,14},{9,15},{10,... | collective-permute-start | bytes 491528 | tf_op jit(solution)/shard_map/ppermute | solution.py:722
  90.0 13.7 %collective-permute-start.7 = (bf16[640,128]{1,0:T(8,128)(2,1)S(1)}, bf16[640,128]{1,0:T(8,128)(2,1)S(1)}, u32[]{:S(2)}, u32[]{:S(2)}) collective-permute-start(bf16[640,128]{1,0:T(8,128)(2,1)S(1)} %add_plane.1.refs_0_), channel_id=1, source_target_pairs={{0,8},{1,9},{2,10},{3,11},{4,12},{5,13},{6,14},{7,15},{8,0},{9,1},... | collective-permute-start | bytes 491528 | tf_op jit(solution)/shard_map/ppermute | solution.py:722
  90.2 14.7 %collective-permute-start.8 = (bf16[640,128]{1,0:T(8,128)(2,1)S(1)}, bf16[640,128]{1,0:T(8,128)(2,1)S(1)}, u32[]{:S(2)}, u32[]{:S(2)}) collective-permute-start(bf16[640,128]{1,0:T(8,128)(2,1)S(1)} %add_plane.1.refs_0_), channel_id=1, source_target_pairs={{0,16},{1,17},{2,18},{3,19},{4,20},{5,21},{6,22},{7,23},{8,24},{9,... | collective-permute-start | bytes 491528 | tf_op jit(solution)/shard_map/ppermute | solution.py:722
  91.3 13.7 %collective-permute-start.9 = (bf16[640,128]{1,0:T(8,128)(2,1)S(1)}, bf16[640,128]{1,0:T(8,128)(2,1)S(1)}, u32[]{:S(2)}, u32[]{:S(2)}) collective-permute-start(bf16[640,128]{1,0:T(8,128)(2,1)S(1)} %add_plane.1.refs_0_), channel_id=1, source_target_pairs={{0,24},{1,25},{2,26},{3,27},{4,28},{5,29},{6,30},{7,31},{8,16},{9,... | collective-permute-start | bytes 491528 | tf_op jit(solution)/shard_map/ppermute | solution.py:722
  105.7 5.4 %collective-permute-start.10 = (bf16[640,128]{1,0:T(8,128)(2,1)S(1)}, bf16[640,128]{1,0:T(8,128)(2,1)S(1)}, u32[]{:S(2)}, u32[]{:S(2)}) collective-permute-start(bf16[640,128]{1,0:T(8,128)(2,1)S(1)} %add_line.1.refs_3_), channel_id=1, source_target_pairs={{0,4},{1,5},{2,6},{3,7},{4,0},{5,1},{6,2},{7,3},{8,12},{9,13},{10,... | collective-permute-start | bytes 491528 | tf_op jit(solution)/shard_map/ppermute | solution.py:722
  106.7 5.3 %collective-permute-start.11 = (bf16[640,128]{1,0:T(8,128)(2,1)S(1)}, bf16[640,128]{1,0:T(8,128)(2,1)S(1)}, u32[]{:S(2)}, u32[]{:S(2)}) collective-permute-start(bf16[640,128]{1,0:T(8,128)(2,1)S(1)} %add_line.1.refs_3_), channel_id=1, source_target_pairs={{0,2},{1,3},{2,0},{3,1},{4,6},{5,7},{6,4},{7,5},{8,10},{9,11},{10,... | collective-permute-start | bytes 491528 | tf_op jit(solution)/shard_map/ppermute | solution.py:722
  107.9 6.2 %collective-permute-start.12 = (bf16[640,128]{1,0:T(8,128)(2,1)S(1)}, bf16[640,128]{1,0:T(8,128)(2,1)S(1)}, u32[]{:S(2)}, u32[]{:S(2)}) collective-permute-start(bf16[640,128]{1,0:T(8,128)(2,1)S(1)} %add_line.1.refs_3_), channel_id=1, source_target_pairs={{0,6},{1,7},{2,4},{3,5},{4,2},{5,3},{6,0},{7,1},{8,14},{9,15},{10,... | collective-permute-start | bytes 491528 | tf_op jit(solution)/shard_map/ppermute | solution.py:722
  109.2 4.9 %collective-permute-start.13 = (bf16[640,128]{1,0:T(8,128)(2,1)S(1)}, bf16[640,128]{1,0:T(8,128)(2,1)S(1)}, u32[]{:S(2)}, u32[]{:S(2)}) collective-permute-start(bf16[640,128]{1,0:T(8,128)(2,1)S(1)} %add_line.1.refs_3_), channel_id=1, source_target_pairs={{0,1},{1,0},{2,3},{3,2},{4,5},{5,4},{6,7},{7,6},{8,9},{9,8},{10,11... | collective-permute-start | bytes 491528 | tf_op jit(solution)/shard_map/ppermute | solution.py:722
  111.1 3.0 %collective-permute-start.14 = (bf16[640,128]{1,0:T(8,128)(2,1)S(1)}, bf16[640,128]{1,0:T(8,128)(2,1)S(1)}, u32[]{:S(2)}, u32[]{:S(2)}) collective-permute-start(bf16[640,128]{1,0:T(8,128)(2,1)S(1)} %collective-permute-done.10.refs_4_), channel_id=1, source_target_pairs={{0,1},{1,0},{2,3},{3,2},{4,5},{5,4},{6,7},{7,6},{8,9},{9,8},{10,11... | collective-permute-start | bytes 491528 | tf_op jit(solution)/shard_map/ppermute | solution.py:722
  112.0 2.2 %collective-permute-start.15 = (bf16[640,128]{1,0:T(8,128)(2,1)S(1)}, bf16[640,128]{1,0:T(8,128)(2,1)S(1)}, u32[]{:S(2)}, u32[]{:S(2)}) collective-permute-start(bf16[640,128]{1,0:T(8,128)(2,1)S(1)} %collective-permute-done.11.refs_5_), channel_id=1, source_target_pairs={{0,1},{1,0},{2,3},{3,2},{4,5},{5,4},{6,7},{7,6},{8,9},{9,8},{10,11... | collective-permute-start | bytes 491528 | tf_op jit(solution)/shard_map/ppermute | solution.py:722
  114.1 1.4 %collective-permute-start.16 = (bf16[640,128]{1,0:T(8,128)(2,1)S(1)}, bf16[640,128]{1,0:T(8,128)(2,1)S(1)}, u32[]{:S(2)}, u32[]{:S(2)}) collective-permute-start(bf16[640,128]{1,0:T(8,128)(2,1)S(1)} %collective-permute-done.12.refs_6_), channel_id=1, source_target_pairs={{0,1},{1,0},{2,3},{3,2},{4,5},{5,4},{6,7},{7,6},{8,9},{9,8},{10,11... | collective-permute-start | bytes 491528 | tf_op jit(solution)/shard_map/ppermute | solution.py:722

commit v4 on v3

--- a/solution.py
+++ b/solution.py
@@ -82,13 +82,17 @@
     ]
 
 
-def attend_kernel(x_ref, ids_ref, gain_ref, weight_ref, proj_ref, second_gain_ref, *refs):
-    outs, refs = refs[:9], refs[9:]
-    probs_out, saved, refs = outs[0], refs[:8], refs[8:]
+def attend_kernel(*refs):
+    sources, refs = refs[:6], refs[6:]
+    outs, second_ref, same, refs = refs[:8], refs[8], refs[9], refs[10:]
+    probs_out, saved, refs = outs[0], refs[:7], refs[7:]
     queries_ref, keys_ref, value_rows_ref, first_ref = saved[:4]
-    attn_ref, inverse_ref, resid_ref, second_ref = saved[4:]
-    probs_ref, key_rows, values, mask_rows, same, bound, semaphores, probs_semaphores = refs
-    pair = pl.program_id(0)
+    attn_ref, inverse_ref, resid_ref = saved[4:]
+    probs_ref, key_rows, values, mask_rows, bound, semaphores, probs_semaphores = refs[:7]
+    x_ref, gain_ref, weight_ref, ids_ref, proj_ref, second_gain_ref = refs[7:13]
+    loads = copies_of(sources, refs[7:13], refs[13])
+    for load in loads:
+        load.start()
     length, width = x_ref.shape
     pairs = width // LANES
     half = LANES // 2
@@ -99,35 +103,37 @@
             probs_ref.at[head], probs_out.at[head], probs_semaphores.at[head]
         )
 
-    @pl.when(pair == 0)
-    def _():
-        normed, _ = norm_parts(x_ref[...].astype(full))
-        first_in = (normed * gain_ref[...].reshape(1, width)).astype(low)
-        turned = dot(weight_ref[...], first_in, 0, 1)
-        scaled = (turned[:width] * (half**-0.5 * log2_e)).astype(low)
-        turned = turned[width:].astype(low)
-        queries_ref[...] = scaled.reshape(pairs, LANES, length)
-        keys_ref[...] = turned[:width].reshape(pairs, LANES, length)
-        values[...] = turned[width:].reshape(pairs, LANES, length)
-        norms = []
-        for part in (scaled, turned[:width]):
-            square = part.astype(full).reshape(2 * pairs, half, length)
-            norms.append(jnp.max(jnp.sum(square * square, axis=1), axis=1, keepdims=True))
-        bound[0] = jnp.max(norms[0] * norms[1])
-        rows = dot(first_in, weight_ref[:, width:]).astype(low)
-        for index in range(pairs):
-            key_rows[index] = rows[:, index * LANES : (index + 1) * LANES]
-            value_rows_ref[index] = rows[:, width + index * LANES : width + (index + 1) * LANES]
-        first_ref[...] = first_in.T
-        for save in saves[:4]:
-            save.start()
-        images = lax.broadcasted_iota(jnp.int32, (LANES, length), 0)
-        matching = images == ids_ref[...]
-        same[...] = matching.astype(full).astype(low)
-        other = jnp.where(jnp.logical_or(matching, images >= IMG_ROW), 0.0, masked_fill)
-        mask_rows[...] = other.T.astype(low)
-
-    def attend_pair(raise_scores):
+    for load in loads[:2]:
+        load.wait()
+    normed, _ = norm_parts(x_ref[...].astype(full))
+    first_in = (normed * gain_ref[...].reshape(1, width)).astype(low)
+    loads[2].wait()
+    turned = dot(weight_ref[...], first_in, 0, 1)
+    scaled = (turned[:width] * (half**-0.5 * log2_e)).astype(low)
+    turned = turned[width:].astype(low)
+    queries_ref[...] = scaled.reshape(pairs, LANES, length)
+    keys_ref[...] = turned[:width].reshape(pairs, LANES, length)
+    values[...] = turned[width:].reshape(pairs, LANES, length)
+    norms = []
+    for part in (scaled, turned[:width]):
+        square = part.astype(full).reshape(2 * pairs, half, length)
+        norms.append(jnp.max(jnp.sum(square * square, axis=1), axis=1, keepdims=True))
+    bound[0] = jnp.max(norms[0] * norms[1])
+    rows = dot(first_in, weight_ref[:, width:]).astype(low)
+    for index in range(pairs):
+        key_rows[index] = rows[:, index * LANES : (index + 1) * LANES]
+        value_rows_ref[index] = rows[:, width + index * LANES : width + (index + 1) * LANES]
+    first_ref[...] = first_in.T
+    for save in saves[:4]:
+        save.start()
+    loads[3].wait()
+    images = lax.broadcasted_iota(jnp.int32, (LANES, length), 0)
+    matching = images == ids_ref[...]
+    same[...] = matching.astype(full).astype(low)
+    other = jnp.where(jnp.logical_or(matching, images >= IMG_ROW), 0.0, masked_fill)
+    mask_rows[...] = other.T.astype(low)
+
+    def attend_pair(pair, raise_scores):
         keys = jnp.concatenate([key_rows[pair], mask_rows[...]], axis=1)
         none = jnp.zeros((half, TILE), low)
         ones = jnp.ones((16, length), low)
@@ -150,32 +156,39 @@
 
     small = bound[0] < score_bound * score_bound
 
-    @pl.when(small)
-    def _():
-        attend_pair(jnp.exp2)
-
-    @pl.when(jnp.logical_not(small))
-    def _():
-        attend_pair(lambda scores: jnp.exp2(scores - jnp.max(scores, axis=0, keepdims=True)))
-
-    @pl.when(pair == pairs - 1)
-    def _():
-        for save in saves[4:6]:
-            save.start()
-        attn = attn_ref[...].reshape(width, length)
-        resid = x_ref[...].astype(full) + dot(attn, proj_ref[...], 0, 0)
-        resid_ref[...] = resid
-        saves[6].start()
-        normed, _ = norm_parts(resid)
-        second_ref[...] = (normed * second_gain_ref[...].reshape(1, width)).astype(low)
-        saves[7].start()
-        for save in saves:
-            save.wait()
-        for head in range(2 * pairs):
-            save_probs(head).wait()
+    def one_pair(pair, carry):
+        @pl.when(small)
+        def _():
+            attend_pair(pair, jnp.exp2)
+
+        @pl.when(jnp.logical_not(small))
+        def _():
+            attend_pair(
+                pair,
+                lambda scores: jnp.exp2(scores - jnp.max(scores, axis=0, keepdims=True)),
+            )
+
+        return carry
+
+    lax.fori_loop(0, pairs, one_pair, 0)
+    for save in saves[4:6]:
+        save.start()
+    for load in loads[4:]:
+        load.wait()
+    attn = attn_ref[...].reshape(width, length)
+    resid = x_ref[...].astype(full) + dot(attn, proj_ref[...], 0, 0)
+    resid_ref[...] = resid
+    saves[6].start()
+    normed, _ = norm_parts(resid)
+    second_ref[...] = (normed * second_gain_ref[...].reshape(1, width)).astype(low)
+    for save in saves:
+        save.wait()
+    for head in range(2 * pairs):
+        save_probs(head).wait()
 
 
 def attend(patches, ids, gain, weight, proj, second_gain):
+    inputs = patches, gain, weight, ids, proj, second_gain
     length, width = patches.shape
     pairs = width // LANES
     stack = (pairs, LANES, length)
@@ -189,29 +202,30 @@
         (stack, low),
         ((pairs, 2, length), full),
         ((length, width), full),
-        ((length, width), low),
     ]
     return pl.pallas_call(
         attend_kernel,
-        grid=(pairs,),
-        in_specs=[whole_vmem] * 6,
-        out_specs=[anywhere] * 9,
-        out_shape=[kept(probs, low)] + [kept(*entry) for entry in saved],
+        in_specs=[anywhere] * 6,
+        out_specs=[anywhere] * 8 + [whole_vmem] * 2,
+        out_shape=[kept(probs, low)]
+        + [kept(*entry) for entry in saved]
+        + [shape_of((length, width), low), shape_of((LANES, length), low)],
         scratch_shapes=[pltpu.VMEM(*entry) for entry in saved]
         + [
             pltpu.VMEM(probs, low),
             pltpu.VMEM(rows, low),
             pltpu.VMEM(stack, low),
             pltpu.VMEM((length, LANES), low),
-            pltpu.VMEM((LANES, length), low),
             pltpu.SMEM((1,), full),
-            pltpu.SemaphoreType.DMA((8,)),
+            pltpu.SemaphoreType.DMA((7,)),
             pltpu.SemaphoreType.DMA((2 * pairs,)),
-        ],
-        compiler_params=params(44),
-        cost_estimate=cost(17),
+        ]
+        + [pltpu.VMEM(array.shape, array.dtype) for array in inputs]
+        + [pltpu.SemaphoreType.DMA((6,))],
+        compiler_params=params(30),
+        cost_estimate=cost(12),
         name="attend",
-    )(*keep(patches, ids, gain, weight, proj, second_gain))
+    )(*keep(*inputs))
 
 
 def slot_rows(slots):
@@ -222,53 +236,65 @@
 
 
 def route_kernel(
-    second_ref, slots_ref, ids_ref, cotangent_ref,
-    dispatch_out, combine_out, send_ref,
-    dispatch_ref, combine_ref, semaphores,
+    second_ref, slots_ref, same_ref, cotangent_source,
+    second_out, dispatch_out, combine_out, send_ref,
+    cotangent_ref, dispatch_ref, combine_ref, semaphores,
 ):
     length, width = second_ref.shape
     experts = slots_ref.shape[0]
     shape = (experts, IMG_ROW, length)
-    saves = copies_of([dispatch_ref, combine_ref], [dispatch_out, combine_out], semaphores)
+    load, *saves = copies_of(
+        [cotangent_source, second_ref, dispatch_ref, combine_ref],
+        [cotangent_ref, second_out, dispatch_out, combine_out],
+        semaphores,
+    )
+    load.start()
+    saves[0].start()
     second_in = second_ref[...]
     logits = dot(slot_rows(slots_ref[...]), second_in, 1, 1).reshape(shape)
-    member = member_of(ids_ref[...])
+    present = same_ref[...].astype(full)[:IMG_ROW]
+    member = present > 0.0
     masked = jnp.where(member[None], logits, masked_fill)
     top = jnp.max(masked, axis=2, keepdims=True)
     raised = jnp.where(member[None], jnp.exp(masked - top), 0.0)
-    present = jnp.max(member.astype(full), axis=1, keepdims=True)
-    total = jnp.sum(raised, axis=2, keepdims=True) + (1.0 - present)[None]
+    absent = 1.0 - jnp.max(present, axis=1, keepdims=True)
+    total = jnp.sum(raised, axis=2, keepdims=True) + absent[None]
     dispatch = raised * (1.0 / total)
     dispatch_ref[...] = dispatch
-    saves[0].start()
+    saves[1].start()
     raised = jnp.exp(logits - jnp.max(logits, axis=0, keepdims=True))
     combine = raised * (1.0 / jnp.sum(raised, axis=0, keepdims=True))
     combine_ref[...] = combine
-    saves[1].start()
+    saves[2].start()
     dispatch_low = dispatch.astype(low).reshape(-1, length)
     combine_low = jnp.where(member[None], combine, 0.0).astype(low).reshape(-1, length)
     block = (send_ref.shape[0], send_ref.shape[2], width)
     send_ref[:, 0] = dot(dispatch_low, second_in).astype(low).reshape(block)
+    load.wait()
     send_ref[:, 1] = dot(combine_low, cotangent_ref[...]).astype(low).reshape(block)
     for save in saves:
         save.wait()
 
 
-def route(second_in, slots, ids, cotangent, groups):
+def route(second_in, slots, same, cotangent, groups):
     length, width = second_in.shape
     experts = slots.shape[0]
     own = experts // groups * IMG_ROW
     shape = (experts, IMG_ROW, length)
     return pl.pallas_call(
         route_kernel,
-        in_specs=[whole_vmem] * 4,
-        out_specs=[anywhere] * 2 + [whole_vmem],
-        out_shape=[kept(shape, full)] * 2 + [shape_of((groups, 2, own, width), low)],
-        scratch_shapes=[pltpu.VMEM(shape, full)] * 2 + [pltpu.SemaphoreType.DMA((2,))],
+        in_specs=[whole_vmem] * 3 + [anywhere],
+        out_specs=[anywhere] * 3 + [whole_vmem],
+        out_shape=[kept((length, width), low)]
+        + [kept(shape, full)] * 2
+        + [shape_of((groups, 2, own, width), low)],
+        scratch_shapes=[pltpu.VMEM((length, width), low)]
+        + [pltpu.VMEM(shape, full)] * 2
+        + [pltpu.SemaphoreType.DMA((4,))],
         compiler_params=params(14 + experts // 4),
         cost_estimate=cost(3),
         name="route",
-    )(*keep(second_in), slots, *keep(ids, cotangent))
+    )(second_in, slots, same, *keep(cotangent))
 
 
 def own_rows(received, expert):
@@ -325,17 +351,16 @@
     )(received, up, *keep(down))
 
 
-def backward_kernel(
-    back_ref, slots_ref, gain_ref, ids_ref, inverse_ref, *refs
-):
-    sources, probs_source, refs = refs[:11], refs[11], refs[12:]
+def backward_kernel(back_ref, *refs):
+    sources, probs_source, refs = refs[:15], refs[15], refs[16:]
     (output_out, grad_resid_out, grads_out, sums_ref), refs = refs[:4], refs[4:]
-    targets, refs = refs[:11], refs[11:]
+    targets, refs = refs[:15], refs[15:]
     probs_ref, output_ref, grad_resid_ref, grads_ref, grad_attn, delta, grad_scores = refs[:7]
     semaphores, probs_semaphores, saves_semaphores = refs[7:]
     loads = copies_of(sources, targets, semaphores)
-    cotangent_ref, combine_ref, second_ref, dispatch_ref, resid_ref, attn_ref, proj_ref = targets[:7]
-    values_ref, keys_ref, queries_ref, first_ref = targets[7:]
+    ids_ref, cotangent_ref, combine_ref, second_ref, dispatch_ref, slots_ref = targets[:6]
+    resid_ref, gain_ref, attn_ref, proj_ref, inverse_ref = targets[6:11]
+    values_ref, keys_ref, queries_ref, first_ref = targets[11:]
     pairs = resid_ref.shape[1] // LANES
 
     def load_probs(pair):
@@ -353,12 +378,13 @@
     saves = copies_of(
         [output_ref, grad_resid_ref], [output_out, grad_resid_out], saves_semaphores
     )
-    for load in loads:
+    for load in loads[:11]:
         load.start()
-    for load in loads[:4]:
+    for load in loads[:6]:
         load.wait()
-    for pair in range(pairs):
-        load_probs(pair).start()
+    for load in loads[11:]:
+        load.start()
+    load_probs(0).start()
     length, width = resid_ref.shape
     half = LANES // 2
     experts = slots_ref.shape[0]
@@ -386,7 +412,7 @@
     mixing = jnp.concatenate([dispatch.astype(low).reshape(count, length), grad_low], axis=0)
     mixed = jnp.concatenate([grad_slots, slots_ref[...]], axis=0)
     grad_second = dot(mixing, mixed, 0, 0)
-    for load in loads[4:7]:
+    for load in loads[6:11]:
         load.wait()
     resid = resid_ref[...]
     combine_low = jnp.where(member[None], combine, 0.0).astype(low).reshape(count, length)
@@ -420,13 +446,18 @@
     if used < sums_ref.shape[0]:
         sums_ref[used:] = jnp.zeros((sums_ref.shape[0] - used, LANES), low)
 
-    for load in loads[7:]:
+    for load in loads[11:]:
         load.wait()
     factor = half**-0.5
     none = jnp.zeros((half, TILE), low)
 
     def one_pair(pair, carry):
         load_probs(pair).wait()
+
+        @pl.when(pair < pairs - 1)
+        def _():
+            load_probs(pair + 1).start()
+
         for head in range(2):
             rows = slice(head * half, (head + 1) * half)
             for start in range(0, length, TILE):
@@ -457,19 +488,19 @@
         save.wait()
 
 
-def padded(rows, devices):
-    return -(-rows // (16 * devices)) * 16 * devices
-
-
-def backward(back, slots, gain, ids, inverse, arrays, probs, devices):
-    length, width = arrays[0].shape
-    experts = slots.shape[0]
+def padded(rows, parts):
+    return -(-rows // (16 * parts)) * 16 * parts
+
+
+def backward(back, arrays, probs):
+    length, width = arrays[1].shape
+    experts = arrays[5].shape[0]
     pairs = width // LANES
-    rows = padded(pairs * (4 * width + experts + 16), devices)
+    rows = padded(pairs * (4 * width + experts + 16), 8)
     saved = [((length, width), low), ((length, width), full), ((pairs, 3, LANES, length), low)]
     return pl.pallas_call(
         backward_kernel,
-        in_specs=[whole_vmem] * 5 + [anywhere] * (len(arrays) + 1),
+        in_specs=[whole_vmem] + [anywhere] * (len(arrays) + 1),
         out_specs=[anywhere] * 3 + [whole_vmem],
         out_shape=[kept(*entry) for entry in saved] + [shape_of((rows, LANES), low)],
         scratch_shapes=[pltpu.VMEM(array.shape, array.dtype) for array in (*arrays, probs)]
@@ -482,10 +513,10 @@
             pltpu.SemaphoreType.DMA((pairs,)),
             pltpu.SemaphoreType.DMA((2 + pairs,)),
         ],
-        compiler_params=params(44 + experts // 8),
+        compiler_params=params(38 + experts // 8),
         cost_estimate=cost(20),
         name="backward",
-    )(back, *keep(slots, gain, ids, inverse, *arrays, probs))
+    )(back, *keep(*arrays, probs))
 
 
 def patch_back_kernel(x_ref, gain_ref, weight_ref, resid_ref, grads_ref, result_ref):
@@ -537,7 +568,8 @@
     groups, _, _, width = received[0].shape
     experts, _, hidden = up.shape
     copies = len(received)
-    tile = hidden // 3
+    steps = 1 if copies * groups <= 64 else 3
+    tile = hidden // steps
     up_spec = pl.BlockSpec((1, width, tile), lambda expert, step: (expert, 0, step))
     down_spec = pl.BlockSpec((1, tile, width), lambda expert, step: (expert, step, 0))
     rows = (copies * groups * IMG_ROW, width)
@@ -547,7 +579,7 @@
 
     return pl.pallas_call(
         kernel,
-        grid=(experts, 3),
+        grid=(experts, steps),
         in_specs=[whole_vmem] * copies + [up_spec, down_spec],
         out_specs=[up_spec, down_spec],
         out_shape=[kept(up.shape, full), kept(down.shape, full)],
@@ -571,14 +603,13 @@
     return pl.ds(pl.multiple_of(index * count, 16), count)
 
 
-def small_call(kernel, out_shape, name, *arrays, scratch=(), limit=16):
+def small_call(kernel, out_shape, name, *arrays):
     return pl.pallas_call(
         kernel,
         in_specs=[pl.BlockSpec(memory_space=pltpu.SMEM)] + [whole_vmem] * (len(arrays) - 1),
         out_specs=jax.tree.map(lambda _: whole_vmem, out_shape),
         out_shape=out_shape,
-        scratch_shapes=scratch,
-        compiler_params=params(limit),
+        compiler_params=params(16),
         cost_estimate=cost(1),
         name=name,
     )(*arrays)
@@ -599,12 +630,8 @@
     refs[-1][...] = total.astype(low)
 
 
-def line_kernel(place_ref, *refs):
-    _, _, layer = position(place_ref)
-    pieces, out, terms = refs[:-2], refs[-2], refs[-1]
-    for step, piece in enumerate(pieces):
-        terms[flipped(layer, step)] = piece[...]
-    out[...] = jnp.sum(terms[...].astype(full), axis=0).astype(low)
+def line_kernel(place_ref, mine_ref, other_ref, out_ref):
+    out_ref[...] = (mine_ref[...].astype(full) + other_ref[...].astype(full)).astype(low)
 
 
 def finish_parts(place_ref, parts, whole):
@@ -636,16 +663,15 @@
         chosen = (row == column).astype(full).astype(low)
         slot_ref[:, lanes] = dot(chosen, sums[start : start + total])
     second_ref[...] = jnp.concatenate(seconds, axis=1).reshape(width)
-    first = jnp.zeros((width, 1), full)
+    first = jnp.zeros((width, LANES), full)
     for pair in range(pairs):
         for part in range(3):
             lanes = slice(part * width + pair * LANES, part * width + (pair + 1) * LANES)
             start = base + (pair * 3 + part) * width
             grad = sums[start : start + width].astype(full)
             qkv_ref[:, lanes] = grad
-            product = grad * weight_ref[:, lanes].astype(full)
-            first = first + jnp.sum(product, axis=1, keepdims=True)
-    row = jnp.broadcast_to(first, (width, LANES)).T[0:1]
+            first = first + grad * weight_ref[:, lanes].astype(full)
+    row = jnp.sum(first.T, axis=0, keepdims=True)
     first_ref[...] = (row / gain_ref[...].reshape(1, width)).reshape(width)
 
 
@@ -670,7 +696,7 @@
         compiler_params=params(20),
         cost_estimate=cost(3),
         name="finish",
-    )(place, *keep(weight, gain), *parts)
+    )(place, weight, gain, *parts)
 
 
 def per_device(
@@ -695,10 +721,10 @@
     slots = lax.all_to_all(spread, "expert", 0, 0, tiled=True).reshape(experts, width)
     patches = patches[0]
     cotangent = cotangent[0]
-    probs, queries, keys, values, first_in, attn, inverse, resid, second_in = attend(
+    probs, queries, keys, values, first_in, attn, inverse, resid, second_in, same = attend(
         patches, image_ids, first_gain, qkv_weight, proj_weight, second_gain
     )
-    dispatch, combine, send = route(second_in, slots, image_ids, cotangent, groups)
+    second_in, dispatch, combine, send = route(second_in, slots, same, cotangent, groups)
     received = lax.all_to_all(send, "expert", 0, 0, tiled=True)
     back = run_experts(received, up_weight, down_weight)
     back = lax.all_to_all(back, "expert", 0, 0, tiled=True)
@@ -706,11 +732,9 @@
         lax.ppermute(received, "rows", [(index, index ^ step) for index in range(copies)])
         for step in range(1, copies)
     ]
-    saved = [cotangent, combine, second_in, dispatch, resid, attn, proj_weight]
-    saved += [values, keys, queries, first_in]
-    output, grad_resid, grads, terms = backward(
-        back, slots, second_gain, image_ids, inverse, saved, probs, devices
-    )
+    saved = [image_ids, cotangent, combine, second_in, dispatch, slots]
+    saved += [resid, second_gain, attn, proj_weight, inverse, values, keys, queries, first_in]
+    output, grad_resid, grads, terms = backward(back, saved, probs)
     place = jnp.stack([lax.axis_index("expert"), lax.axis_index("rows")]).astype(jnp.int32)
     layers = groups // 2
 
@@ -722,8 +746,7 @@
         return lax.ppermute(array, both_axes, pairs)
 
     terms, others = lax.optimization_barrier((terms, others))
-    share = terms.shape[0] // devices
-    quarter = (layers * share, LANES)
+    quarter = (terms.shape[0] // 8, LANES)
     mine, *sends = small_call(
         core_kernel, [shape_of(quarter, full)] + [shape_of(quarter, low)] * 3, "add_core",
         place, terms, flip(terms, 0, 1),
@@ -733,14 +756,17 @@
     patch_grad = patch_back(patches, first_gain, qkv_weight, grad_resid, grads)
     arrived, patch_grad = lax.optimization_barrier((arrived, patch_grad))
     mine = small_call(plane_kernel, shape_of(quarter, low), "add_plane", place, mine, *arrived)
-    arrived = [flip(mine, step * 2, 0) for step in range(1, layers)]
-    others, _ = lax.optimization_barrier((others, mine))
-    up_grad, down_grad = weight_grads([received] + others, up_weight, down_weight)
-    arrived, up_grad, down_grad = lax.optimization_barrier((arrived, up_grad, down_grad))
-    mine = small_call(
-        line_kernel, shape_of(quarter, low), "add_line", place, mine, *arrived,
-        scratch=[pltpu.VMEM((layers, *quarter), low)], limit=12 + layers,
-    )
+    step = 1
+    while step < layers:
+        arrived = flip(mine, step * 2, 0)
+        if step * 2 >= layers:
+            others, _ = lax.optimization_barrier((others, mine))
+            up_grad, down_grad = weight_grads([received] + others, up_weight, down_weight)
+            arrived, up_grad, down_grad = lax.optimization_barrier((arrived, up_grad, down_grad))
+        mine = small_call(
+            line_kernel, shape_of(quarter, low), f"add_line_{step}", place, mine, arrived
+        )
+        step *= 2
     arrived = [flip(mine, step % 2, step // 2 * 2) for step in range(1, 4)]
     parts = [mine] + arrived
     parts = parts + [flip(part, 0, 1) for part in parts]

time: 120 us -> 114 us (0.950); the launches traced: 119 us -> 114 us
  Pallas kernels: 60.6 us -> 55.4 us
  waiting for transfers between devices: 17.6 us -> 21.4 us
  starting transfers between devices: 24.4 us -> 21.2 us
    pallas_call x4, Pallas kernels: 45.5 us -> 40.7 us  [the longest x1 19.9 us: backward(): pl.pallas_call(backward_kernel, in_specs=[whole_vmem] + [anywhere] * (len...]
    ppermute x14 -> x13, waiting for transfers between devices: 12 us -> 15.8 us  [flip(): return lax.ppermute(array, both_axes, pairs)]
    ppermute x14 -> x13, starting transfers between devices: 11.6 us -> 8.44 us  [flip(): return lax.ppermute(array, both_axes, pairs)]
    pallas_call x3 -> x4, Pallas kernels: 2.05 us -> 2.46 us  [small_call(): pl.pallas_call(kernel, in_specs=[pl.BlockSpec(memory_space=pltpu.SMEM)] +...]
  transfers between devices with their start and end apart: 19 -> 18, of which waited for: 8 -> 9; matrix products, arithmetic and copies ran while one was open for 0% -> 0% of each run, Pallas kernels for 40% -> 39%
where the time goes in v4:
time: 114 us
  Pallas kernels  55.4 us (49%)
  waiting for transfers between devices  21.4 us (19%)
  starting transfers between devices  21.2 us (19%)
  blocking collectives  13.6 us (12%)
  local copies, waits for them, and re-layouts  1.49 us (1%)
    pallas_call x1, Pallas kernels, backward(): pl.pallas_call(backward_kernel, in_specs=[whole_vmem] + [anywhere] * (len...  19.9 us
    ppermute x13, waiting for transfers between devices, flip(): return lax.ppermute(array, both_axes, pairs)  15.8 us
    all_to_all x1, blocking collectives, per_device(): received = lax.all_to_all(send, 'expert', 0, 0, tiled=True)  13.6 us
    pallas_call x1, Pallas kernels, attend(): pl.pallas_call(attend_kernel, in_specs=[anywhere] * 6, out_specs=[anywher...  12.1 us
    ppermute x13, starting transfers between devices, flip(): return lax.ppermute(array, both_axes, pairs)  8.44 us
    all_to_all x1, starting transfers between devices, per_device(): lax.all_to_all(spread, 'expert', 0, 0, tiled=True).reshape(experts, width)  7.25 us
    pallas_call x1, Pallas kernels, weight_grads(): pl.pallas_call(kernel, grid=(experts, steps), in_specs=[whole_vmem] * cop...  6.89 us
    all_to_all x1, waiting for transfers between devices, per_device(): back = lax.all_to_all(back, 'expert', 0, 0, tiled=True)  5.6 us
  transfers between devices with their start and end apart: 18, of which 9 were waited for; matrix products, arithmetic and copies ran while one was open for 0% of the time, Pallas kernels for 39%

profile of v4, /device:TPU:0, one launch (start us, length us, event | category | flops | bytes accessed | tf_op | source)
XLA Modules:
  0.0 114.1 jit_solution(11037430518133735458)
XLA Ops:
  0.6 0.0 copy-start
  0.7 1.4 %broadcast_in_dim.12 = bf16[8,2,384]{2,1,0:T(2,128)(2,1)} broadcast(bf16[2,384]{1,0:T(2,128)(2,1)} %bitcast.13), dimensions={1,2} | broadcast | bytes 13824 | tf_op jit(solution)/shard_map/broadcast_in_dim | solution.py:720
  2.1 7.3 %all-to-all-start = ((bf16[8,2,384]{2,1,0:T(2,128)(2,1)}), bf16[8,2,384]{2,1,0:T(2,128)(2,1)S(1)}, u32[]{:S(2)}, u32[]{:S(2)}) async-start(bf16[8,2,384]{2,1,0:T(2,128)(2,1)} %broadcast_in_dim.12), calls=%async_computation | async-start | bytes 24576 | tf_op jit(solution)/shard_map/all_to_all | solution.py:721
  9.3 12.1 %attend.1 = (bf16[6,1024,1024]{2,1,0:T(8,128)(2,1)}, bf16[3,128,1024]{2,1,0:T(8,128)(2,1)}, bf16[3,128,1024]{2,1,0:T(8,128)(2,1)}, bf16[3,1024,128]{2,1,0:T(8,12...) custom-call(bf16[1024,384]{1,0:T(8,128)(2,1)} %bitcast.10, ...), custom_call_target="tpu_custom_call" | custom-call | bytes 43200000 | tf_op jit(solution)/shard_map/attend/pallas_call | solution.py:206
  21.4 0.0 all-to-all-done
  21.5 0.0 copy-start.3
  21.5 1.8 %route.1 = (bf16[1024,384]{1,0:T(8,128)(2,1)}, f32[16,8,1024]{2,1,0:T(8,128)}, f32[16,8,1024]{2,1,0:T(8,128)}, bf16[8,2,16,384]{3,2,1,0:T(8,128)(2,1)S(1)}) custom-call(bf16[1024,384]{1,0:T(8,128)(2,1)S(1)} %get-tuple-element.53.second_ref, bf16[16,384]{1,0:T(8,128)(2,1)S(1)} %reshape.22.slots_ref.refs_5_, bf16[128,1024]{1,0:T(8,128)(2,1)S(1)} %get-tuple-element.54.same_ref, ...), custom_call_target="tpu_custom_call" | custom-call | bytes 10800000 | tf_op jit(solution)/shard_map/route/pallas_call | solution.py:284
  23.3 13.6 %all_to_all.15.received_ref.refs_0_ = bf16[8,2,16,384]{3,2,1,0:T(8,128)(2,1)S(1)} all-to-all(bf16[8,2,16,384]{3,2,1,0:T(8,128)(2,1)S(1)} %get-tuple-element.55), channel_id=1, replica_groups=mesh['expert'=8,'rows'=4] {'expert'}, dimensions={0} | all-to-all | bytes 393216 | tf_op jit(solution)/shard_map/all_to_all | solution.py:728
  36.9 0.0 copy-done
  36.9 4.5 %run_experts.1 = bf16[8,2,16,384]{3,2,1,0:T(8,128)(2,1)} custom-call(bf16[8,2,16,384]{3,2,1,0:T(8,128)(2,1)S(1)} %all_to_all.15.received_ref.refs_0_, bf16[2,384,1536]{2,1,0:T(8,128)(2,1)S(1)} %copy-done, bf16[2,1536,384]{2,1,0:T(8,128)(2,1)} %refs_5_.3), custom_call_target="tpu_custom_call" | custom-call | bytes 10800000 | tf_op jit(solution)/shard_map/run_experts/pallas_call | solution.py:338
  41.4 0.0 copy-done.3
  41.4 3.6 %all-to-all-start.2 = ((bf16[8,2,16,384]{3,2,1,0:T(8,128)(2,1)}), bf16[8,2,16,384]{3,2,1,0:T(8,128)(2,1)S(1)}, u32[]{:S(2)}, u32[]{:S(2)}) async-start(bf16[8,2,16,384]{3,2,1,0:T(8,128)(2,1)} %run_experts.1), calls=%async_computation.2 | async-start | bytes 393216 | tf_op jit(solution)/shard_map/all_to_all | solution.py:730
  45.0 0.1 collective-permute-start
  45.1 1.6 %collective-permute-start.1 = (bf16[8,2,16,384]{3,2,1,0:T(8,128)(2,1)S(1)}, bf16[8,2,16,384]{3,2,1,0:T(8,128)(2,1)S(1)}, u32[]{:S(2)}, u32[]{:S(2)}) collective-permute-start(bf16[8,2,16,384]{3,2,1,0:T(8,128)(2,1)S(1)} %all_to_all.15.received_ref.refs_0_), channel_id=1, source_target_pairs={{0,2},{1,3},{2,0},{3,1},{4,6},{5,7},{6,4},{7,5},{8,10},{9,11},{10,... | collective-permute-start | bytes 589832 | tf_op jit(solution)/shard_map/ppermute | solution.py:732
  46.6 0.0 copy-done.2
  46.6 0.3 collective-permute-start.2
  46.9 5.6 %all-to-all-done.2.back_ref = bf16[8,2,16,384]{3,2,1,0:T(8,128)(2,1)S(1)} async-done(((bf16[8,2,16,384]{3,2,1,0:T(8,128)(2,1)}), bf16[8,2,16,384]{3,2,1,0:T(8,128)(2,1)S(1)}, u32[]{:S(2)}, u32[]{:S(2)}) %all-to-all-start.2) | async-done | bytes 196640 | tf_op jit(solution)/shard_map/all_to_all | solution.py:730
  52.5 19.9 %backward.1 = (bf16[1024,384]{1,0:T(8,128)(2,1)}, f32[1024,384]{1,0:T(8,128)}, bf16[3,3,128,1024]{3,2,1,0:T(8,128)(2,1)}, bf16[4736,128]{1,0:T(8,128)(2,1)S(1)}) custom-call(bf16[8,2,16,384]{3,2,1,0:T(8,128)(2,1)S(1)} %all-to-all-done.2.back_ref, s32[1,1024]{1,0:T(1,128)} %refs_0_.1, bf16[1024,384]{1,0:T(8,128)(2,1)} %bitcast.9, ...), custom_call_target="tpu_custom_call" | custom-call | bytes 72000000 | tf_op jit(solution)/shard_map/backward/pallas_call | solution.py:501
  72.4 0.0 collective-permute-done.refs_1_
  72.4 0.0 copy-start.5
  72.4 0.0 collective-permute-done.1.refs_2_
  72.4 0.0 copy-start.6
  72.4 0.0 collective-permute-done.2.refs_3_
  72.5 0.0 copy-start.7
  72.5 0.1 collective-permute-start.3
  72.5 0.1 pad_add_fusion.place_ref.refs_0_
  72.6 2.8 %collective-permute-done.3.other_ref = bf16[4736,128]{1,0:T(8,128)(2,1)S(1)} collective-permute-done((bf16[4736,128]{1,0:T(8,128)(2,1)S(1)}, bf16[4736,128]{1,0:T(8,128)(2,1)S(1)}, u32[]{:S(2)}, u32[]{:S(2)}) %collective-permute-start.3) | collective-permute-done | bytes 1212448 | tf_op jit(solution)/shard_map/ppermute | solution.py:746
  75.4 0.7 add_core.1
  76.1 0.1 collective-permute-start.4
  76.2 1.5 %collective-permute-start.5 = (bf16[592,128]{1,0:T(8,128)(2,1)S(1)}, bf16[592,128]{1,0:T(8,128)(2,1)S(1)}, u32[]{:S(2)}, u32[]{:S(2)}) collective-permute-start(bf16[592,128]{1,0:T(8,128)(2,1)S(1)} %get-tuple-element.71), channel_id=1, source_target_pairs={{0,2},{1,3},{2,0},{3,1},{4,6},{5,7},{6,4},{7,5},{8,10},{9,11},{10,... | collective-permute-start | bytes 454664 | tf_op jit(solution)/shard_map/ppermute | solution.py:746
  77.8 1.9 %collective-permute-start.6 = (bf16[592,128]{1,0:T(8,128)(2,1)S(1)}, bf16[592,128]{1,0:T(8,128)(2,1)S(1)}, u32[]{:S(2)}, u32[]{:S(2)}) collective-permute-start(bf16[592,128]{1,0:T(8,128)(2,1)S(1)} %get-tuple-element.72), channel_id=1, source_target_pairs={{0,6},{1,7},{2,4},{3,5},{4,2},{5,3},{6,0},{7,1},{8,14},{9,15},{10,... | collective-permute-start | bytes 454664 | tf_op jit(solution)/shard_map/ppermute | solution.py:746
  79.7 5.6 %patch_back.1 = f32[1024,384]{1,0:T(8,128)} custom-call(bf16[1024,384]{1,0:T(8,128)(2,1)} %bitcast.11, f32[384]{0:T(512)} %refs_2_.3, bf16[384,1152]{1,0:T(8,128)(2,1)} %refs_1_.3, f32[1024,384]{1,0:T(8,128)} %get-tuple-element.73.resid_ref, bf16[3,3,128,1024]{3,2,1,0:T(8,128)(2,1)} %get-tuple-element.76.grads_ref), custom_call_target="tpu_custom_call" | custom-call | bytes 10800000 | tf_op jit(solution)/shard_map/patch_back/pallas_call | solution.py:533
  85.3 0.0 copy-done.5
  85.3 0.0 copy-done.6
  85.3 0.0 copy-done.7
  85.3 0.0 collective-permute-done.4.refs_1_
  85.3 0.0 collective-permute-done.5.refs_2_
  85.3 1.1 collective-permute-done.6.refs_3_
  86.3 0.6 add_plane.1.mine_ref
  87.0 0.3 collective-permute-start.7
  87.2 5.0 %collective-permute-done.7.other_ref = bf16[592,128]{1,0:T(8,128)(2,1)S(1)} collective-permute-done((bf16[592,128]{1,0:T(8,128)(2,1)S(1)}, bf16[592,128]{1,0:T(8,128)(2,1)S(1)}, u32[]{:S(2)}, u32[]{:S(2)}) %collective-permute-start.7) | collective-permute-done | bytes 151584 | tf_op jit(solution)/shard_map/ppermute | solution.py:746
  92.2 0.6 add_line_1.1.mine_ref
  92.8 0.0 copy-start.1
  92.8 0.0 copy-start.4
  92.8 0.5 collective-permute-start.8
  93.3 6.9 %weight_grads.1 = (f32[2,384,1536]{2,1,0:T(8,128)}, f32[2,1536,384]{2,1,0:T(8,128)}) custom-call(bf16[8,2,16,384]{3,2,1,0:T(8,128)(2,1)} %copy-done.2, bf16[8,2,16,384]{3,2,1,0:T(8,128)(2,1)} %copy-done.5, bf16[8,2,16,384]{3,2,1,0:T(8,128)(2,1)} %copy-done.6, bf16[8,2,16,384]{3,2,1,0:T(8,128)(2,1)} %copy-done.7, bf16[2,384,1536]{2,1,0:T(8,128)(2,1)} %refs_4_.3, ...), custom_call_target="tpu_custom_call" | custom-call | bytes 32400000 | tf_op jit(solution)/shard_map/weight_grads/pallas_call | solution.py:580
  100.2 0.6 collective-permute-done.8.other_ref
  100.8 0.6 add_line_2.1.refs_3_
  101.3 0.7 collective-permute-start.9
  102.1 1.3 %collective-permute-start.10 = (bf16[592,128]{1,0:T(8,128)(2,1)S(1)}, bf16[592,128]{1,0:T(8,128)(2,1)S(1)}, u32[]{:S(2)}, u32[]{:S(2)}) collective-permute-start(bf16[592,128]{1,0:T(8,128)(2,1)S(1)} %add_line_2.1.refs_3_), channel_id=1, source_target_pairs={{0,2},{1,3},{2,0},{3,1},{4,6},{5,7},{6,4},{7,5},{8,10},{9,11},{10,... | collective-permute-start | bytes 454664 | tf_op jit(solution)/shard_map/ppermute | solution.py:746
  103.4 1.5 %collective-permute-start.11 = (bf16[592,128]{1,0:T(8,128)(2,1)S(1)}, bf16[592,128]{1,0:T(8,128)(2,1)S(1)}, u32[]{:S(2)}, u32[]{:S(2)}) collective-permute-start(bf16[592,128]{1,0:T(8,128)(2,1)S(1)} %add_line_2.1.refs_3_), channel_id=1, source_target_pairs={{0,6},{1,7},{2,4},{3,5},{4,2},{5,3},{6,0},{7,1},{8,14},{9,15},{10,... | collective-permute-start | bytes 454664 | tf_op jit(solution)/shard_map/ppermute | solution.py:746
  104.9 0.0 collective-permute-start.12
  104.9 2.8 %collective-permute-done.9.refs_4_ = bf16[592,128]{1,0:T(8,128)(2,1)S(1)} collective-permute-done((bf16[592,128]{1,0:T(8,128)(2,1)S(1)}, bf16[592,128]{1,0:T(8,128)(2,1)S(1)}, u32[]{:S(2)}, u32[]{:S(2)}) %collective-permute-start.9) | collective-permute-done | bytes 151584 | tf_op jit(solution)/shard_map/ppermute | solution.py:746
  107.7 0.0 collective-permute-start.13
  107.7 2.5 %collective-permute-done.10.refs_5_ = bf16[592,128]{1,0:T(8,128)(2,1)S(1)} collective-permute-done((bf16[592,128]{1,0:T(8,128)(2,1)S(1)}, bf16[592,128]{1,0:T(8,128)(2,1)S(1)}, u32[]{:S(2)}, u32[]{:S(2)}) %collective-permute-start.10) | collective-permute-done | bytes 151584 | tf_op jit(solution)/shard_map/ppermute | solution.py:746
  110.2 0.0 collective-permute-start.14
  110.2 0.0 collective-permute-done.11.refs_6_
  110.2 0.5 collective-permute-start.15
  110.7 0.0 collective-permute-done.12.refs_7_
  110.7 0.0 collective-permute-done.13.refs_8_
  110.7 0.9 collective-permute-done.14.refs_9_
  111.6 0.2 collective-permute-done.15.refs_10_
  111.8 0.0 copy-done.4
  111.8 2.3 %finish.1 = (f32[384]{0:T(512)}, f32[384,1152]{1,0:T(8,128)}, f32[384,384]{1,0:T(8,128)}, f32[384]{0:T(512)}, f32[2,384]{1,0:T(2,128)}) custom-call(s32[2]{0:T(128)S(1)} %pad_add_fusion.place_ref.refs_0_, bf16[384,1152]{1,0:T(8,128)(2,1)S(1)} %copy-done.1, f32[384]{0:T(512)S(1)} %copy-done.4, bf16[592,128]{1,0:T(8,128)(2,1)S(1)} %add_line_2.1.refs_3_, ...), custom_call_target="tpu_custom_call" | custom-call | bytes 10800000 | tf_op jit(solution)/shard_map/finish/pallas_call | solution.py:684
  (3 shorter events, 0.0 us)
Async XLA Ops:
  0.6 36.3 %copy-start = (bf16[2,384,1536]{2,1,0:T(8,128)(2,1)S(1)}, bf16[2,384,1536]{2,1,0:T(8,128)(2,1)}, u32[]{:S(2)}) copy-start(bf16[2,384,1536]{2,1,0:T(8,128)(2,1)} %refs_4_.3) | copy-start | bytes 7077892
  2.1 19.3 %all-to-all-start = ((bf16[8,2,384]{2,1,0:T(2,128)(2,1)}), bf16[8,2,384]{2,1,0:T(2,128)(2,1)S(1)}, u32[]{:S(2)}, u32[]{:S(2)}) async-start(bf16[8,2,384]{2,1,0:T(2,128)(2,1)} %broadcast_in_dim.12), calls=%async_computation | async-start | bytes 24576 | tf_op jit(solution)/shard_map/all_to_all | solution.py:721
  21.5 19.9 %copy-start.3 = (bf16[16,384]{1,0:T(8,128)(2,1)}, bf16[16,384]{1,0:T(8,128)(2,1)S(1)}, u32[]{:S(2)}) copy-start(bf16[16,384]{1,0:T(8,128)(2,1)S(1)} %reshape.22.slots_ref.refs_5_) | copy-start | bytes 36868
  36.9 9.7 %copy-start.2 = (bf16[8,2,16,384]{3,2,1,0:T(8,128)(2,1)}, bf16[8,2,16,384]{3,2,1,0:T(8,128)(2,1)S(1)}, u32[]{:S(2)}) copy-start(bf16[8,2,16,384]{3,2,1,0:T(8,128)(2,1)S(1)} %all_to_all.15.received_ref.refs_0_) | copy-start | bytes 589828
  41.4 11.1 %all-to-all-start.2 = ((bf16[8,2,16,384]{3,2,1,0:T(8,128)(2,1)}), bf16[8,2,16,384]{3,2,1,0:T(8,128)(2,1)S(1)}, u32[]{:S(2)}, u32[]{:S(2)}) async-start(bf16[8,2,16,384]{3,2,1,0:T(8,128)(2,1)} %run_experts.1), calls=%async_computation.2 | async-start | bytes 393216 | tf_op jit(solution)/shard_map/all_to_all | solution.py:730
  45.0 27.4 %collective-permute-start = (bf16[8,2,16,384]{3,2,1,0:T(8,128)(2,1)S(1)}, bf16[8,2,16,384]{3,2,1,0:T(8,128)(2,1)S(1)}, u32[]{:S(2)}, u32[]{:S(2)}) collective-permute-start(bf16[8,2,16,384]{3,2,1,0:T(8,128)(2,1)S(1)} %all_to_all.15.received_ref.refs_0_), channel_id=1, source_target_pairs={{0,1},{1,0},{2,3},{3,2},{4,5},{5,4},{6,7},{7,6},{8,9},{9,8},{10,11... | collective-permute-start | bytes 589832 | tf_op jit(solution)/shard_map/ppermute | solution.py:732
  45.1 27.4 %collective-permute-start.1 = (bf16[8,2,16,384]{3,2,1,0:T(8,128)(2,1)S(1)}, bf16[8,2,16,384]{3,2,1,0:T(8,128)(2,1)S(1)}, u32[]{:S(2)}, u32[]{:S(2)}) collective-permute-start(bf16[8,2,16,384]{3,2,1,0:T(8,128)(2,1)S(1)} %all_to_all.15.received_ref.refs_0_), channel_id=1, source_target_pairs={{0,2},{1,3},{2,0},{3,1},{4,6},{5,7},{6,4},{7,5},{8,10},{9,11},{10,... | collective-permute-start | bytes 589832 | tf_op jit(solution)/shard_map/ppermute | solution.py:732
  46.6 25.8 %collective-permute-start.2 = (bf16[8,2,16,384]{3,2,1,0:T(8,128)(2,1)S(1)}, bf16[8,2,16,384]{3,2,1,0:T(8,128)(2,1)S(1)}, u32[]{:S(2)}, u32[]{:S(2)}) collective-permute-start(bf16[8,2,16,384]{3,2,1,0:T(8,128)(2,1)S(1)} %all_to_all.15.received_ref.refs_0_), channel_id=1, source_target_pairs={{0,3},{1,2},{2,1},{3,0},{4,7},{5,6},{6,5},{7,4},{8,11},{9,10},{10,... | collective-permute-start | bytes 589832 | tf_op jit(solution)/shard_map/ppermute | solution.py:732
  72.4 12.8 %copy-start.5 = (bf16[8,2,16,384]{3,2,1,0:T(8,128)(2,1)}, bf16[8,2,16,384]{3,2,1,0:T(8,128)(2,1)S(1)}, u32[]{:S(2)}) copy-start(bf16[8,2,16,384]{3,2,1,0:T(8,128)(2,1)S(1)} %collective-permute-done.refs_1_) | copy-start | bytes 589828
  72.4 12.8 %copy-start.6 = (bf16[8,2,16,384]{3,2,1,0:T(8,128)(2,1)}, bf16[8,2,16,384]{3,2,1,0:T(8,128)(2,1)S(1)}, u32[]{:S(2)}) copy-start(bf16[8,2,16,384]{3,2,1,0:T(8,128)(2,1)S(1)} %collective-permute-done.1.refs_2_) | copy-start | bytes 589828
  72.5 12.8 %copy-start.7 = (bf16[8,2,16,384]{3,2,1,0:T(8,128)(2,1)}, bf16[8,2,16,384]{3,2,1,0:T(8,128)(2,1)S(1)}, u32[]{:S(2)}) copy-start(bf16[8,2,16,384]{3,2,1,0:T(8,128)(2,1)S(1)} %collective-permute-done.2.refs_3_) | copy-start | bytes 589828
  72.5 3.0 %collective-permute-start.3 = (bf16[4736,128]{1,0:T(8,128)(2,1)S(1)}, bf16[4736,128]{1,0:T(8,128)(2,1)S(1)}, u32[]{:S(2)}, u32[]{:S(2)}) collective-permute-start(bf16[4736,128]{1,0:T(8,128)(2,1)S(1)} %get-tuple-element.69.mine_ref), channel_id=1, source_target_pairs={{0,1},{1,0},{2,3},{3,2},{4,5},{5,4},{6,7},{7,6},{8,9},{9,8},{10,11... | collective-permute-start | bytes 3637256 | tf_op jit(solution)/shard_map/ppermute | solution.py:746
  76.1 9.1 %collective-permute-start.4 = (bf16[592,128]{1,0:T(8,128)(2,1)S(1)}, bf16[592,128]{1,0:T(8,128)(2,1)S(1)}, u32[]{:S(2)}, u32[]{:S(2)}) collective-permute-start(bf16[592,128]{1,0:T(8,128)(2,1)S(1)} %get-tuple-element.70), channel_id=1, source_target_pairs={{0,4},{1,5},{2,6},{3,7},{4,0},{5,1},{6,2},{7,3},{8,12},{9,13},{10,... | collective-permute-start | bytes 454664 | tf_op jit(solution)/shard_map/ppermute | solution.py:746
  76.2 9.1 %collective-permute-start.5 = (bf16[592,128]{1,0:T(8,128)(2,1)S(1)}, bf16[592,128]{1,0:T(8,128)(2,1)S(1)}, u32[]{:S(2)}, u32[]{:S(2)}) collective-permute-start(bf16[592,128]{1,0:T(8,128)(2,1)S(1)} %get-tuple-element.71), channel_id=1, source_target_pairs={{0,2},{1,3},{2,0},{3,1},{4,6},{5,7},{6,4},{7,5},{8,10},{9,11},{10,... | collective-permute-start | bytes 454664 | tf_op jit(solution)/shard_map/ppermute | solution.py:746
  77.8 8.6 %collective-permute-start.6 = (bf16[592,128]{1,0:T(8,128)(2,1)S(1)}, bf16[592,128]{1,0:T(8,128)(2,1)S(1)}, u32[]{:S(2)}, u32[]{:S(2)}) collective-permute-start(bf16[592,128]{1,0:T(8,128)(2,1)S(1)} %get-tuple-element.72), channel_id=1, source_target_pairs={{0,6},{1,7},{2,4},{3,5},{4,2},{5,3},{6,0},{7,1},{8,14},{9,15},{10,... | collective-permute-start | bytes 454664 | tf_op jit(solution)/shard_map/ppermute | solution.py:746
  87.0 5.3 %collective-permute-start.7 = (bf16[592,128]{1,0:T(8,128)(2,1)S(1)}, bf16[592,128]{1,0:T(8,128)(2,1)S(1)}, u32[]{:S(2)}, u32[]{:S(2)}) collective-permute-start(bf16[592,128]{1,0:T(8,128)(2,1)S(1)} %add_plane.1.mine_ref), channel_id=1, source_target_pairs={{0,8},{1,9},{2,10},{3,11},{4,12},{5,13},{6,14},{7,15},{8,0},{9,1},... | collective-permute-start | bytes 454664 | tf_op jit(solution)/shard_map/ppermute | solution.py:746
  92.8 19.0 %copy-start.1 = (bf16[384,1152]{1,0:T(8,128)(2,1)S(1)}, bf16[384,1152]{1,0:T(8,128)(2,1)}, u32[]{:S(2)}) copy-start(bf16[384,1152]{1,0:T(8,128)(2,1)} %refs_1_.3) | copy-start | bytes 2654212
  92.8 19.0 %copy-start.4 = (f32[384]{0:T(512)S(1)}, f32[384]{0:T(512)}, u32[]{:S(2)}) copy-start(f32[384]{0:T(512)} %refs_2_.3) | copy-start | bytes 4612
  92.8 7.9 %collective-permute-start.8 = (bf16[592,128]{1,0:T(8,128)(2,1)S(1)}, bf16[592,128]{1,0:T(8,128)(2,1)S(1)}, u32[]{:S(2)}, u32[]{:S(2)}) collective-permute-start(bf16[592,128]{1,0:T(8,128)(2,1)S(1)} %add_line_1.1.mine_ref), channel_id=1, source_target_pairs={{0,16},{1,17},{2,18},{3,19},{4,20},{5,21},{6,22},{7,23},{8,24},{9,... | collective-permute-start | bytes 454664 | tf_op jit(solution)/shard_map/ppermute | solution.py:746
  101.3 6.3 %collective-permute-start.9 = (bf16[592,128]{1,0:T(8,128)(2,1)S(1)}, bf16[592,128]{1,0:T(8,128)(2,1)S(1)}, u32[]{:S(2)}, u32[]{:S(2)}) collective-permute-start(bf16[592,128]{1,0:T(8,128)(2,1)S(1)} %add_line_2.1.refs_3_), channel_id=1, source_target_pairs={{0,4},{1,5},{2,6},{3,7},{4,0},{5,1},{6,2},{7,3},{8,12},{9,13},{10,... | collective-permute-start | bytes 454664 | tf_op jit(solution)/shard_map/ppermute | solution.py:746
  102.1 8.1 %collective-permute-start.10 = (bf16[592,128]{1,0:T(8,128)(2,1)S(1)}, bf16[592,128]{1,0:T(8,128)(2,1)S(1)}, u32[]{:S(2)}, u32[]{:S(2)}) collective-permute-start(bf16[592,128]{1,0:T(8,128)(2,1)S(1)} %add_line_2.1.refs_3_), channel_id=1, source_target_pairs={{0,2},{1,3},{2,0},{3,1},{4,6},{5,7},{6,4},{7,5},{8,10},{9,11},{10,... | collective-permute-start | bytes 454664 | tf_op jit(solution)/shard_map/ppermute | solution.py:746
  103.4 6.8 %collective-permute-start.11 = (bf16[592,128]{1,0:T(8,128)(2,1)S(1)}, bf16[592,128]{1,0:T(8,128)(2,1)S(1)}, u32[]{:S(2)}, u32[]{:S(2)}) collective-permute-start(bf16[592,128]{1,0:T(8,128)(2,1)S(1)} %add_line_2.1.refs_3_), channel_id=1, source_target_pairs={{0,6},{1,7},{2,4},{3,5},{4,2},{5,3},{6,0},{7,1},{8,14},{9,15},{10,... | collective-permute-start | bytes 454664 | tf_op jit(solution)/shard_map/ppermute | solution.py:746
  104.9 5.8 %collective-permute-start.12 = (bf16[592,128]{1,0:T(8,128)(2,1)S(1)}, bf16[592,128]{1,0:T(8,128)(2,1)S(1)}, u32[]{:S(2)}, u32[]{:S(2)}) collective-permute-start(bf16[592,128]{1,0:T(8,128)(2,1)S(1)} %add_line_2.1.refs_3_), channel_id=1, source_target_pairs={{0,1},{1,0},{2,3},{3,2},{4,5},{5,4},{6,7},{7,6},{8,9},{9,8},{10,11... | collective-permute-start | bytes 454664 | tf_op jit(solution)/shard_map/ppermute | solution.py:746
  107.7 3.1 %collective-permute-start.13 = (bf16[592,128]{1,0:T(8,128)(2,1)S(1)}, bf16[592,128]{1,0:T(8,128)(2,1)S(1)}, u32[]{:S(2)}, u32[]{:S(2)}) collective-permute-start(bf16[592,128]{1,0:T(8,128)(2,1)S(1)} %collective-permute-done.9.refs_4_), channel_id=1, source_target_pairs={{0,1},{1,0},{2,3},{3,2},{4,5},{5,4},{6,7},{7,6},{8,9},{9,8},{10,11... | collective-permute-start | bytes 454664 | tf_op jit(solution)/shard_map/ppermute | solution.py:746
  110.2 1.4 %collective-permute-start.14 = (bf16[592,128]{1,0:T(8,128)(2,1)S(1)}, bf16[592,128]{1,0:T(8,128)(2,1)S(1)}, u32[]{:S(2)}, u32[]{:S(2)}) collective-permute-start(bf16[592,128]{1,0:T(8,128)(2,1)S(1)} %collective-permute-done.10.refs_5_), channel_id=1, source_target_pairs={{0,1},{1,0},{2,3},{3,2},{4,5},{5,4},{6,7},{7,6},{8,9},{9,8},{10,11... | collective-permute-start | bytes 454664 | tf_op jit(solution)/shard_map/ppermute | solution.py:746
  110.2 1.6 %collective-permute-start.15 = (bf16[592,128]{1,0:T(8,128)(2,1)S(1)}, bf16[592,128]{1,0:T(8,128)(2,1)S(1)}, u32[]{:S(2)}, u32[]{:S(2)}) collective-permute-start(bf16[592,128]{1,0:T(8,128)(2,1)S(1)} %collective-permute-done.11.refs_6_), channel_id=1, source_target_pairs={{0,1},{1,0},{2,3},{3,2},{4,5},{5,4},{6,7},{7,6},{8,9},{9,8},{10,11... | collective-permute-start | bytes 454664 | tf_op jit(solution)/shard_map/ppermute | solution.py:746

commit v5 on v4

--- a/solution.py
+++ b/solution.py
@@ -119,10 +119,9 @@
         square = part.astype(full).reshape(2 * pairs, half, length)
         norms.append(jnp.max(jnp.sum(square * square, axis=1), axis=1, keepdims=True))
     bound[0] = jnp.max(norms[0] * norms[1])
-    rows = dot(first_in, weight_ref[:, width:]).astype(low)
     for index in range(pairs):
-        key_rows[index] = rows[:, index * LANES : (index + 1) * LANES]
-        value_rows_ref[index] = rows[:, width + index * LANES : width + (index + 1) * LANES]
+        key_rows[index] = keys_ref[index].T
+        value_rows_ref[index] = values[index].T
     first_ref[...] = first_in.T
     for save in saves[:4]:
         save.start()
@@ -356,7 +355,7 @@
     (output_out, grad_resid_out, grads_out, sums_ref), refs = refs[:4], refs[4:]
     targets, refs = refs[:15], refs[15:]
     probs_ref, output_ref, grad_resid_ref, grads_ref, grad_attn, delta, grad_scores = refs[:7]
-    semaphores, probs_semaphores, saves_semaphores = refs[7:]
+    turned_scores, turned_probs, semaphores, probs_semaphores, saves_semaphores = refs[7:]
     loads = copies_of(sources, targets, semaphores)
     ids_ref, cotangent_ref, combine_ref, second_ref, dispatch_ref, slots_ref = targets[:6]
     resid_ref, gain_ref, attn_ref, proj_ref, inverse_ref = targets[6:11]
@@ -458,22 +457,30 @@
         def _():
             load_probs(pair + 1).start()
 
-        for head in range(2):
-            rows = slice(head * half, (head + 1) * half)
+        heads = [slice(head * half, (head + 1) * half) for head in range(2)]
+        for head, rows in enumerate(heads):
             for start in range(0, length, TILE):
                 span = slice(start, start + TILE)
                 grad = grad_attn[pair, rows, span]
                 parts = [grad, none] if head == 0 else [none, grad]
                 grad_probs = dot(values_ref[pair], jnp.concatenate(parts, axis=0))
+                grad_probs = grad_probs - delta[pair, head : head + 1, span]
                 probs = probs_ref[2 * pair + head, :, span].astype(full)
-                grad_probs = grad_probs - delta[pair, head : head + 1, span]
-                grad_scores[head, :, span] = (probs * grad_probs).astype(low)
-            scores = grad_scores[head]
-            probs = probs_ref[2 * pair + head]
-            grads_ref[pair, 2, rows, :] = dot(grad_attn[pair, rows, :], probs, 1, 1).astype(low)
-            grads_ref[pair, 0, rows, :] = (dot(keys_ref[pair, rows, :], scores) * factor).astype(low)
+                scores = (probs * grad_probs).astype(low)
+                grad_scores[head, :, span] = scores
+                turned_scores[head, span, :] = scores.T
+            turned_probs[head] = probs_ref[2 * pair + head].T
+        for head, rows in enumerate(heads):
             grads_ref[pair, 1, rows, :] = (
-                dot(queries_ref[pair, rows, :], scores, 1, 1) * (1.0 / log2_e)
+                dot(queries_ref[pair, rows, :], turned_scores[head]) * (1.0 / log2_e)
+            ).astype(low)
+        for head, rows in enumerate(heads):
+            grads_ref[pair, 2, rows, :] = dot(
+                grad_attn[pair, rows, :], turned_probs[head]
+            ).astype(low)
+        for head, rows in enumerate(heads):
+            grads_ref[pair, 0, rows, :] = (
+                dot(keys_ref[pair, rows, :], grad_scores[head]) * factor
             ).astype(low)
         sums = dot(first_ref[...], grads_ref[pair].reshape(3 * LANES, length), 1, 1).astype(low)
 
@@ -509,11 +516,13 @@
             pltpu.VMEM((pairs, LANES, length), low),
             pltpu.VMEM((pairs, 2, length), full),
             pltpu.VMEM((2, length, length), low),
+            pltpu.VMEM((2, length, length), low),
+            pltpu.VMEM((2, length, length), low),
             pltpu.SemaphoreType.DMA((len(arrays),)),
             pltpu.SemaphoreType.DMA((pairs,)),
             pltpu.SemaphoreType.DMA((2 + pairs,)),
         ],
-        compiler_params=params(38 + experts // 8),
+        compiler_params=params(44 + experts // 8),
         cost_estimate=cost(20),
         name="backward",
     )(back, *keep(*arrays, probs))

time: 114 us -> 112 us (0.982)
  Pallas kernels: 55.4 us -> 52.9 us
    pallas_call x1, Pallas kernels: 19.9 us -> 17.8 us  [backward(): pl.pallas_call(backward_kernel, in_specs=[whole_vmem] + [anywhere] * (len...]
  transfers between devices with their start and end apart: 18 -> 18, of which waited for: 9 -> 9; matrix products, arithmetic and copies ran while one was open for 0% -> 0% of each run, Pallas kernels for 39% -> 38%
where the time goes in v5:
time: 112 us; the launch traced here: 111 us
  Pallas kernels  52.9 us (47%)
  waiting for transfers between devices  21.4 us (19%)
  starting transfers between devices  21.2 us (19%)
  blocking collectives  13.6 us (12%)
  local copies, waits for them, and re-layouts  1.49 us (1%)
    pallas_call x1, Pallas kernels, backward(): pl.pallas_call(backward_kernel, in_specs=[whole_vmem] + [anywhere] * (len...  17.8 us
    ppermute x13, waiting for transfers between devices, flip(): return lax.ppermute(array, both_axes, pairs)  15.8 us
    all_to_all x1, blocking collectives, per_device(): received = lax.all_to_all(send, 'expert', 0, 0, tiled=True)  13.6 us
    pallas_call x1, Pallas kernels, attend(): pl.pallas_call(attend_kernel, in_specs=[anywhere] * 6, out_specs=[anywher...  11.6 us
    ppermute x13, starting transfers between devices, flip(): return lax.ppermute(array, both_axes, pairs)  8.4 us
    all_to_all x1, starting transfers between devices, per_device(): lax.all_to_all(spread, 'expert', 0, 0, tiled=True).reshape(experts, width)  7.25 us
    pallas_call x1, Pallas kernels, weight_grads(): pl.pallas_call(kernel, grid=(experts, steps), in_specs=[whole_vmem] * cop...  6.89 us
    all_to_all x1, waiting for transfers between devices, per_device(): back = lax.all_to_all(back, 'expert', 0, 0, tiled=True)  5.6 us
  transfers between devices with their start and end apart: 18, of which 9 were waited for; matrix products, arithmetic and copies ran while one was open for 0% of the time, Pallas kernels for 38%

profile of v5, /device:TPU:0, one launch (start us, length us, event | category | flops | bytes accessed | tf_op | source)
XLA Modules:
  0.0 111.5 jit_solution(478537467005614435)
XLA Ops:
  0.6 0.0 copy-start
  0.7 1.4 %broadcast_in_dim.12 = bf16[8,2,384]{2,1,0:T(2,128)(2,1)} broadcast(bf16[2,384]{1,0:T(2,128)(2,1)} %bitcast.13), dimensions={1,2} | broadcast | bytes 13824 | tf_op jit(solution)/shard_map/broadcast_in_dim | solution.py:729
  2.1 7.3 %all-to-all-start = ((bf16[8,2,384]{2,1,0:T(2,128)(2,1)}), bf16[8,2,384]{2,1,0:T(2,128)(2,1)S(1)}, u32[]{:S(2)}, u32[]{:S(2)}) async-start(bf16[8,2,384]{2,1,0:T(2,128)(2,1)} %broadcast_in_dim.12), calls=%async_computation | async-start | bytes 24576 | tf_op jit(solution)/shard_map/all_to_all | solution.py:730
  9.3 11.6 %attend.1 = (bf16[6,1024,1024]{2,1,0:T(8,128)(2,1)}, bf16[3,128,1024]{2,1,0:T(8,128)(2,1)}, bf16[3,128,1024]{2,1,0:T(8,128)(2,1)}, bf16[3,1024,128]{2,1,0:T(8,12...) custom-call(bf16[1024,384]{1,0:T(8,128)(2,1)} %bitcast.10, ...), custom_call_target="tpu_custom_call" | custom-call | bytes 43200000 | tf_op jit(solution)/shard_map/attend/pallas_call | solution.py:205
  21.0 0.0 all-to-all-done
  21.0 0.0 copy-start.3
  21.0 1.8 %route.1 = (bf16[1024,384]{1,0:T(8,128)(2,1)}, f32[16,8,1024]{2,1,0:T(8,128)}, f32[16,8,1024]{2,1,0:T(8,128)}, bf16[8,2,16,384]{3,2,1,0:T(8,128)(2,1)S(1)}) custom-call(bf16[1024,384]{1,0:T(8,128)(2,1)S(1)} %get-tuple-element.53.second_ref, bf16[16,384]{1,0:T(8,128)(2,1)S(1)} %reshape.22.slots_ref.refs_5_, bf16[128,1024]{1,0:T(8,128)(2,1)S(1)} %get-tuple-element.54.same_ref, ...), custom_call_target="tpu_custom_call" | custom-call | bytes 10800000 | tf_op jit(solution)/shard_map/route/pallas_call | solution.py:283
  22.9 13.6 %all_to_all.15.received_ref.refs_0_ = bf16[8,2,16,384]{3,2,1,0:T(8,128)(2,1)S(1)} all-to-all(bf16[8,2,16,384]{3,2,1,0:T(8,128)(2,1)S(1)} %get-tuple-element.55), channel_id=1, replica_groups=mesh['expert'=8,'rows'=4] {'expert'}, dimensions={0} | all-to-all | bytes 393216 | tf_op jit(solution)/shard_map/all_to_all | solution.py:737
  36.4 0.0 copy-done
  36.4 4.5 %run_experts.1 = bf16[8,2,16,384]{3,2,1,0:T(8,128)(2,1)} custom-call(bf16[8,2,16,384]{3,2,1,0:T(8,128)(2,1)S(1)} %all_to_all.15.received_ref.refs_0_, bf16[2,384,1536]{2,1,0:T(8,128)(2,1)S(1)} %copy-done, bf16[2,1536,384]{2,1,0:T(8,128)(2,1)} %refs_5_.3), custom_call_target="tpu_custom_call" | custom-call | bytes 10800000 | tf_op jit(solution)/shard_map/run_experts/pallas_call | solution.py:337
  40.9 0.0 copy-done.3
  40.9 3.6 %all-to-all-start.2 = ((bf16[8,2,16,384]{3,2,1,0:T(8,128)(2,1)}), bf16[8,2,16,384]{3,2,1,0:T(8,128)(2,1)S(1)}, u32[]{:S(2)}, u32[]{:S(2)}) async-start(bf16[8,2,16,384]{3,2,1,0:T(8,128)(2,1)} %run_experts.1), calls=%async_computation.2 | async-start | bytes 393216 | tf_op jit(solution)/shard_map/all_to_all | solution.py:739
  44.5 0.1 collective-permute-start
  44.6 1.6 %collective-permute-start.1 = (bf16[8,2,16,384]{3,2,1,0:T(8,128)(2,1)S(1)}, bf16[8,2,16,384]{3,2,1,0:T(8,128)(2,1)S(1)}, u32[]{:S(2)}, u32[]{:S(2)}) collective-permute-start(bf16[8,2,16,384]{3,2,1,0:T(8,128)(2,1)S(1)} %all_to_all.15.received_ref.refs_0_), channel_id=1, source_target_pairs={{0,2},{1,3},{2,0},{3,1},{4,6},{5,7},{6,4},{7,5},{8,10},{9,11},{10,... | collective-permute-start | bytes 589832 | tf_op jit(solution)/shard_map/ppermute | solution.py:741
  46.2 0.0 copy-done.2
  46.2 0.3 collective-permute-start.2
  46.5 5.6 %all-to-all-done.2.back_ref = bf16[8,2,16,384]{3,2,1,0:T(8,128)(2,1)S(1)} async-done(((bf16[8,2,16,384]{3,2,1,0:T(8,128)(2,1)}), bf16[8,2,16,384]{3,2,1,0:T(8,128)(2,1)S(1)}, u32[]{:S(2)}, u32[]{:S(2)}) %all-to-all-start.2) | async-done | bytes 196640 | tf_op jit(solution)/shard_map/all_to_all | solution.py:739
  52.1 17.8 %backward.1 = (bf16[1024,384]{1,0:T(8,128)(2,1)}, f32[1024,384]{1,0:T(8,128)}, bf16[3,3,128,1024]{3,2,1,0:T(8,128)(2,1)}, bf16[4736,128]{1,0:T(8,128)(2,1)S(1)}) custom-call(bf16[8,2,16,384]{3,2,1,0:T(8,128)(2,1)S(1)} %all-to-all-done.2.back_ref, s32[1,1024]{1,0:T(1,128)} %refs_0_.1, bf16[1024,384]{1,0:T(8,128)(2,1)} %bitcast.9, ...), custom_call_target="tpu_custom_call" | custom-call | bytes 72000000 | tf_op jit(solution)/shard_map/backward/pallas_call | solution.py:508
  69.9 0.0 collective-permute-done.refs_1_
  69.9 0.0 copy-start.5
  69.9 0.0 collective-permute-done.1.refs_2_
  69.9 0.0 copy-start.6
  69.9 0.0 collective-permute-done.2.refs_3_
  69.9 0.0 copy-start.7
  69.9 0.1 collective-permute-start.3
  70.0 0.1 pad_add_fusion.place_ref.refs_0_
  70.1 2.8 %collective-permute-done.3.other_ref = bf16[4736,128]{1,0:T(8,128)(2,1)S(1)} collective-permute-done((bf16[4736,128]{1,0:T(8,128)(2,1)S(1)}, bf16[4736,128]{1,0:T(8,128)(2,1)S(1)}, u32[]{:S(2)}, u32[]{:S(2)}) %collective-permute-start.3) | collective-permute-done | bytes 1212448 | tf_op jit(solution)/shard_map/ppermute | solution.py:755
  72.9 0.7 add_core.1
  73.6 0.1 collective-permute-start.4
  73.7 1.6 %collective-permute-start.5 = (bf16[592,128]{1,0:T(8,128)(2,1)S(1)}, bf16[592,128]{1,0:T(8,128)(2,1)S(1)}, u32[]{:S(2)}, u32[]{:S(2)}) collective-permute-start(bf16[592,128]{1,0:T(8,128)(2,1)S(1)} %get-tuple-element.71), channel_id=1, source_target_pairs={{0,2},{1,3},{2,0},{3,1},{4,6},{5,7},{6,4},{7,5},{8,10},{9,11},{10,... | collective-permute-start | bytes 454664 | tf_op jit(solution)/shard_map/ppermute | solution.py:755
  75.3 1.9 %collective-permute-start.6 = (bf16[592,128]{1,0:T(8,128)(2,1)S(1)}, bf16[592,128]{1,0:T(8,128)(2,1)S(1)}, u32[]{:S(2)}, u32[]{:S(2)}) collective-permute-start(bf16[592,128]{1,0:T(8,128)(2,1)S(1)} %get-tuple-element.72), channel_id=1, source_target_pairs={{0,6},{1,7},{2,4},{3,5},{4,2},{5,3},{6,0},{7,1},{8,14},{9,15},{10,... | collective-permute-start | bytes 454664 | tf_op jit(solution)/shard_map/ppermute | solution.py:755
  77.2 5.6 %patch_back.1 = f32[1024,384]{1,0:T(8,128)} custom-call(bf16[1024,384]{1,0:T(8,128)(2,1)} %bitcast.11, f32[384]{0:T(512)} %refs_2_.3, bf16[384,1152]{1,0:T(8,128)(2,1)} %refs_1_.3, f32[1024,384]{1,0:T(8,128)} %get-tuple-element.73.resid_ref, bf16[3,3,128,1024]{3,2,1,0:T(8,128)(2,1)} %get-tuple-element.76.grads_ref), custom_call_target="tpu_custom_call" | custom-call | bytes 10800000 | tf_op jit(solution)/shard_map/patch_back/pallas_call | solution.py:542
  82.7 0.0 copy-done.5
  82.7 0.0 copy-done.6
  82.7 0.0 copy-done.7
  82.7 0.0 collective-permute-done.4.refs_1_
  82.8 0.0 collective-permute-done.5.refs_2_
  82.8 1.1 collective-permute-done.6.refs_3_
  83.8 0.6 add_plane.1.mine_ref
  84.5 0.2 collective-permute-start.7
  84.7 5.0 %collective-permute-done.7.other_ref = bf16[592,128]{1,0:T(8,128)(2,1)S(1)} collective-permute-done((bf16[592,128]{1,0:T(8,128)(2,1)S(1)}, bf16[592,128]{1,0:T(8,128)(2,1)S(1)}, u32[]{:S(2)}, u32[]{:S(2)}) %collective-permute-start.7) | collective-permute-done | bytes 151584 | tf_op jit(solution)/shard_map/ppermute | solution.py:755
  89.7 0.6 add_line_1.1.mine_ref
  90.3 0.0 copy-start.1
  90.3 0.0 copy-start.4
  90.3 0.5 collective-permute-start.8
  90.8 6.9 %weight_grads.1 = (f32[2,384,1536]{2,1,0:T(8,128)}, f32[2,1536,384]{2,1,0:T(8,128)}) custom-call(bf16[8,2,16,384]{3,2,1,0:T(8,128)(2,1)} %copy-done.2, bf16[8,2,16,384]{3,2,1,0:T(8,128)(2,1)} %copy-done.5, bf16[8,2,16,384]{3,2,1,0:T(8,128)(2,1)} %copy-done.6, bf16[8,2,16,384]{3,2,1,0:T(8,128)(2,1)} %copy-done.7, bf16[2,384,1536]{2,1,0:T(8,128)(2,1)} %refs_4_.3, ...), custom_call_target="tpu_custom_call" | custom-call | bytes 32400000 | tf_op jit(solution)/shard_map/weight_grads/pallas_call | solution.py:589
  97.7 0.8 collective-permute-done.8.other_ref
  98.5 0.6 add_line_2.1.refs_3_
  99.1 0.4 collective-permute-start.9
  99.5 1.4 %collective-permute-start.10 = (bf16[592,128]{1,0:T(8,128)(2,1)S(1)}, bf16[592,128]{1,0:T(8,128)(2,1)S(1)}, u32[]{:S(2)}, u32[]{:S(2)}) collective-permute-start(bf16[592,128]{1,0:T(8,128)(2,1)S(1)} %add_line_2.1.refs_3_), channel_id=1, source_target_pairs={{0,2},{1,3},{2,0},{3,1},{4,6},{5,7},{6,4},{7,5},{8,10},{9,11},{10,... | collective-permute-start | bytes 454664 | tf_op jit(solution)/shard_map/ppermute | solution.py:755
  100.9 1.8 %collective-permute-start.11 = (bf16[592,128]{1,0:T(8,128)(2,1)S(1)}, bf16[592,128]{1,0:T(8,128)(2,1)S(1)}, u32[]{:S(2)}, u32[]{:S(2)}) collective-permute-start(bf16[592,128]{1,0:T(8,128)(2,1)S(1)} %add_line_2.1.refs_3_), channel_id=1, source_target_pairs={{0,6},{1,7},{2,4},{3,5},{4,2},{5,3},{6,0},{7,1},{8,14},{9,15},{10,... | collective-permute-start | bytes 454664 | tf_op jit(solution)/shard_map/ppermute | solution.py:755
  102.7 0.0 collective-permute-start.12
  102.7 3.1 %collective-permute-done.9.refs_4_ = bf16[592,128]{1,0:T(8,128)(2,1)S(1)} collective-permute-done((bf16[592,128]{1,0:T(8,128)(2,1)S(1)}, bf16[592,128]{1,0:T(8,128)(2,1)S(1)}, u32[]{:S(2)}, u32[]{:S(2)}) %collective-permute-start.9) | collective-permute-done | bytes 151584 | tf_op jit(solution)/shard_map/ppermute | solution.py:755
  105.7 0.0 collective-permute-start.13
  105.7 1.9 %collective-permute-done.10.refs_5_ = bf16[592,128]{1,0:T(8,128)(2,1)S(1)} collective-permute-done((bf16[592,128]{1,0:T(8,128)(2,1)S(1)}, bf16[592,128]{1,0:T(8,128)(2,1)S(1)}, u32[]{:S(2)}, u32[]{:S(2)}) %collective-permute-start.10) | collective-permute-done | bytes 151584 | tf_op jit(solution)/shard_map/ppermute | solution.py:755
  107.6 0.0 collective-permute-start.14
  107.6 0.0 collective-permute-done.11.refs_6_
  107.6 0.5 collective-permute-start.15
  108.1 0.0 collective-permute-done.12.refs_7_
  108.1 0.0 collective-permute-done.13.refs_8_
  108.1 0.9 collective-permute-done.14.refs_9_
  109.0 0.2 collective-permute-done.15.refs_10_
  109.2 0.0 copy-done.4
  109.2 2.3 %finish.1 = (f32[384]{0:T(512)}, f32[384,1152]{1,0:T(8,128)}, f32[384,384]{1,0:T(8,128)}, f32[384]{0:T(512)}, f32[2,384]{1,0:T(2,128)}) custom-call(s32[2]{0:T(128)S(1)} %pad_add_fusion.place_ref.refs_0_, bf16[384,1152]{1,0:T(8,128)(2,1)S(1)} %copy-done.1, f32[384]{0:T(512)S(1)} %copy-done.4, bf16[592,128]{1,0:T(8,128)(2,1)S(1)} %add_line_2.1.refs_3_, ...), custom_call_target="tpu_custom_call" | custom-call | bytes 10800000 | tf_op jit(solution)/shard_map/finish/pallas_call | solution.py:693
  (3 shorter events, 0.0 us)
Async XLA Ops:
  0.6 35.8 %copy-start = (bf16[2,384,1536]{2,1,0:T(8,128)(2,1)S(1)}, bf16[2,384,1536]{2,1,0:T(8,128)(2,1)}, u32[]{:S(2)}) copy-start(bf16[2,384,1536]{2,1,0:T(8,128)(2,1)} %refs_4_.3) | copy-start | bytes 7077892
  2.1 18.9 %all-to-all-start = ((bf16[8,2,384]{2,1,0:T(2,128)(2,1)}), bf16[8,2,384]{2,1,0:T(2,128)(2,1)S(1)}, u32[]{:S(2)}, u32[]{:S(2)}) async-start(bf16[8,2,384]{2,1,0:T(2,128)(2,1)} %broadcast_in_dim.12), calls=%async_computation | async-start | bytes 24576 | tf_op jit(solution)/shard_map/all_to_all | solution.py:730
  21.0 19.9 %copy-start.3 = (bf16[16,384]{1,0:T(8,128)(2,1)}, bf16[16,384]{1,0:T(8,128)(2,1)S(1)}, u32[]{:S(2)}) copy-start(bf16[16,384]{1,0:T(8,128)(2,1)S(1)} %reshape.22.slots_ref.refs_5_) | copy-start | bytes 36868
  36.4 9.7 %copy-start.2 = (bf16[8,2,16,384]{3,2,1,0:T(8,128)(2,1)}, bf16[8,2,16,384]{3,2,1,0:T(8,128)(2,1)S(1)}, u32[]{:S(2)}) copy-start(bf16[8,2,16,384]{3,2,1,0:T(8,128)(2,1)S(1)} %all_to_all.15.received_ref.refs_0_) | copy-start | bytes 589828
  40.9 11.1 %all-to-all-start.2 = ((bf16[8,2,16,384]{3,2,1,0:T(8,128)(2,1)}), bf16[8,2,16,384]{3,2,1,0:T(8,128)(2,1)S(1)}, u32[]{:S(2)}, u32[]{:S(2)}) async-start(bf16[8,2,16,384]{3,2,1,0:T(8,128)(2,1)} %run_experts.1), calls=%async_computation.2 | async-start | bytes 393216 | tf_op jit(solution)/shard_map/all_to_all | solution.py:739
  44.5 25.4 %collective-permute-start = (bf16[8,2,16,384]{3,2,1,0:T(8,128)(2,1)S(1)}, bf16[8,2,16,384]{3,2,1,0:T(8,128)(2,1)S(1)}, u32[]{:S(2)}, u32[]{:S(2)}) collective-permute-start(bf16[8,2,16,384]{3,2,1,0:T(8,128)(2,1)S(1)} %all_to_all.15.received_ref.refs_0_), channel_id=1, source_target_pairs={{0,1},{1,0},{2,3},{3,2},{4,5},{5,4},{6,7},{7,6},{8,9},{9,8},{10,11... | collective-permute-start | bytes 589832 | tf_op jit(solution)/shard_map/ppermute | solution.py:741
  44.6 25.3 %collective-permute-start.1 = (bf16[8,2,16,384]{3,2,1,0:T(8,128)(2,1)S(1)}, bf16[8,2,16,384]{3,2,1,0:T(8,128)(2,1)S(1)}, u32[]{:S(2)}, u32[]{:S(2)}) collective-permute-start(bf16[8,2,16,384]{3,2,1,0:T(8,128)(2,1)S(1)} %all_to_all.15.received_ref.refs_0_), channel_id=1, source_target_pairs={{0,2},{1,3},{2,0},{3,1},{4,6},{5,7},{6,4},{7,5},{8,10},{9,11},{10,... | collective-permute-start | bytes 589832 | tf_op jit(solution)/shard_map/ppermute | solution.py:741
  46.2 23.7 %collective-permute-start.2 = (bf16[8,2,16,384]{3,2,1,0:T(8,128)(2,1)S(1)}, bf16[8,2,16,384]{3,2,1,0:T(8,128)(2,1)S(1)}, u32[]{:S(2)}, u32[]{:S(2)}) collective-permute-start(bf16[8,2,16,384]{3,2,1,0:T(8,128)(2,1)S(1)} %all_to_all.15.received_ref.refs_0_), channel_id=1, source_target_pairs={{0,3},{1,2},{2,1},{3,0},{4,7},{5,6},{6,5},{7,4},{8,11},{9,10},{10,... | collective-permute-start | bytes 589832 | tf_op jit(solution)/shard_map/ppermute | solution.py:741
  69.9 12.8 %copy-start.5 = (bf16[8,2,16,384]{3,2,1,0:T(8,128)(2,1)}, bf16[8,2,16,384]{3,2,1,0:T(8,128)(2,1)S(1)}, u32[]{:S(2)}) copy-start(bf16[8,2,16,384]{3,2,1,0:T(8,128)(2,1)S(1)} %collective-permute-done.refs_1_) | copy-start | bytes 589828
  69.9 12.8 %copy-start.6 = (bf16[8,2,16,384]{3,2,1,0:T(8,128)(2,1)}, bf16[8,2,16,384]{3,2,1,0:T(8,128)(2,1)S(1)}, u32[]{:S(2)}) copy-start(bf16[8,2,16,384]{3,2,1,0:T(8,128)(2,1)S(1)} %collective-permute-done.1.refs_2_) | copy-start | bytes 589828
  69.9 12.8 %copy-start.7 = (bf16[8,2,16,384]{3,2,1,0:T(8,128)(2,1)}, bf16[8,2,16,384]{3,2,1,0:T(8,128)(2,1)S(1)}, u32[]{:S(2)}) copy-start(bf16[8,2,16,384]{3,2,1,0:T(8,128)(2,1)S(1)} %collective-permute-done.2.refs_3_) | copy-start | bytes 589828
  69.9 3.0 %collective-permute-start.3 = (bf16[4736,128]{1,0:T(8,128)(2,1)S(1)}, bf16[4736,128]{1,0:T(8,128)(2,1)S(1)}, u32[]{:S(2)}, u32[]{:S(2)}) collective-permute-start(bf16[4736,128]{1,0:T(8,128)(2,1)S(1)} %get-tuple-element.69.mine_ref), channel_id=1, source_target_pairs={{0,1},{1,0},{2,3},{3,2},{4,5},{5,4},{6,7},{7,6},{8,9},{9,8},{10,11... | collective-permute-start | bytes 3637256 | tf_op jit(solution)/shard_map/ppermute | solution.py:755
  73.6 9.1 %collective-permute-start.4 = (bf16[592,128]{1,0:T(8,128)(2,1)S(1)}, bf16[592,128]{1,0:T(8,128)(2,1)S(1)}, u32[]{:S(2)}, u32[]{:S(2)}) collective-permute-start(bf16[592,128]{1,0:T(8,128)(2,1)S(1)} %get-tuple-element.70), channel_id=1, source_target_pairs={{0,4},{1,5},{2,6},{3,7},{4,0},{5,1},{6,2},{7,3},{8,12},{9,13},{10,... | collective-permute-start | bytes 454664 | tf_op jit(solution)/shard_map/ppermute | solution.py:755
  73.7 9.1 %collective-permute-start.5 = (bf16[592,128]{1,0:T(8,128)(2,1)S(1)}, bf16[592,128]{1,0:T(8,128)(2,1)S(1)}, u32[]{:S(2)}, u32[]{:S(2)}) collective-permute-start(bf16[592,128]{1,0:T(8,128)(2,1)S(1)} %get-tuple-element.71), channel_id=1, source_target_pairs={{0,2},{1,3},{2,0},{3,1},{4,6},{5,7},{6,4},{7,5},{8,10},{9,11},{10,... | collective-permute-start | bytes 454664 | tf_op jit(solution)/shard_map/ppermute | solution.py:755
  75.3 8.6 %collective-permute-start.6 = (bf16[592,128]{1,0:T(8,128)(2,1)S(1)}, bf16[592,128]{1,0:T(8,128)(2,1)S(1)}, u32[]{:S(2)}, u32[]{:S(2)}) collective-permute-start(bf16[592,128]{1,0:T(8,128)(2,1)S(1)} %get-tuple-element.72), channel_id=1, source_target_pairs={{0,6},{1,7},{2,4},{3,5},{4,2},{5,3},{6,0},{7,1},{8,14},{9,15},{10,... | collective-permute-start | bytes 454664 | tf_op jit(solution)/shard_map/ppermute | solution.py:755
  84.5 5.3 %collective-permute-start.7 = (bf16[592,128]{1,0:T(8,128)(2,1)S(1)}, bf16[592,128]{1,0:T(8,128)(2,1)S(1)}, u32[]{:S(2)}, u32[]{:S(2)}) collective-permute-start(bf16[592,128]{1,0:T(8,128)(2,1)S(1)} %add_plane.1.mine_ref), channel_id=1, source_target_pairs={{0,8},{1,9},{2,10},{3,11},{4,12},{5,13},{6,14},{7,15},{8,0},{9,1},... | collective-permute-start | bytes 454664 | tf_op jit(solution)/shard_map/ppermute | solution.py:755
  90.3 18.9 %copy-start.1 = (bf16[384,1152]{1,0:T(8,128)(2,1)S(1)}, bf16[384,1152]{1,0:T(8,128)(2,1)}, u32[]{:S(2)}) copy-start(bf16[384,1152]{1,0:T(8,128)(2,1)} %refs_1_.3) | copy-start | bytes 2654212
  90.3 18.9 %copy-start.4 = (f32[384]{0:T(512)S(1)}, f32[384]{0:T(512)}, u32[]{:S(2)}) copy-start(f32[384]{0:T(512)} %refs_2_.3) | copy-start | bytes 4612
  90.3 8.2 %collective-permute-start.8 = (bf16[592,128]{1,0:T(8,128)(2,1)S(1)}, bf16[592,128]{1,0:T(8,128)(2,1)S(1)}, u32[]{:S(2)}, u32[]{:S(2)}) collective-permute-start(bf16[592,128]{1,0:T(8,128)(2,1)S(1)} %add_line_1.1.mine_ref), channel_id=1, source_target_pairs={{0,16},{1,17},{2,18},{3,19},{4,20},{5,21},{6,22},{7,23},{8,24},{9,... | collective-permute-start | bytes 454664 | tf_op jit(solution)/shard_map/ppermute | solution.py:755
  99.1 6.6 %collective-permute-start.9 = (bf16[592,128]{1,0:T(8,128)(2,1)S(1)}, bf16[592,128]{1,0:T(8,128)(2,1)S(1)}, u32[]{:S(2)}, u32[]{:S(2)}) collective-permute-start(bf16[592,128]{1,0:T(8,128)(2,1)S(1)} %add_line_2.1.refs_3_), channel_id=1, source_target_pairs={{0,4},{1,5},{2,6},{3,7},{4,0},{5,1},{6,2},{7,3},{8,12},{9,13},{10,... | collective-permute-start | bytes 454664 | tf_op jit(solution)/shard_map/ppermute | solution.py:755
  99.5 8.1 %collective-permute-start.10 = (bf16[592,128]{1,0:T(8,128)(2,1)S(1)}, bf16[592,128]{1,0:T(8,128)(2,1)S(1)}, u32[]{:S(2)}, u32[]{:S(2)}) collective-permute-start(bf16[592,128]{1,0:T(8,128)(2,1)S(1)} %add_line_2.1.refs_3_), channel_id=1, source_target_pairs={{0,2},{1,3},{2,0},{3,1},{4,6},{5,7},{6,4},{7,5},{8,10},{9,11},{10,... | collective-permute-start | bytes 454664 | tf_op jit(solution)/shard_map/ppermute | solution.py:755
  100.9 6.7 %collective-permute-start.11 = (bf16[592,128]{1,0:T(8,128)(2,1)S(1)}, bf16[592,128]{1,0:T(8,128)(2,1)S(1)}, u32[]{:S(2)}, u32[]{:S(2)}) collective-permute-start(bf16[592,128]{1,0:T(8,128)(2,1)S(1)} %add_line_2.1.refs_3_), channel_id=1, source_target_pairs={{0,6},{1,7},{2,4},{3,5},{4,2},{5,3},{6,0},{7,1},{8,14},{9,15},{10,... | collective-permute-start | bytes 454664 | tf_op jit(solution)/shard_map/ppermute | solution.py:755
  102.7 5.4 %collective-permute-start.12 = (bf16[592,128]{1,0:T(8,128)(2,1)S(1)}, bf16[592,128]{1,0:T(8,128)(2,1)S(1)}, u32[]{:S(2)}, u32[]{:S(2)}) collective-permute-start(bf16[592,128]{1,0:T(8,128)(2,1)S(1)} %add_line_2.1.refs_3_), channel_id=1, source_target_pairs={{0,1},{1,0},{2,3},{3,2},{4,5},{5,4},{6,7},{7,6},{8,9},{9,8},{10,11... | collective-permute-start | bytes 454664 | tf_op jit(solution)/shard_map/ppermute | solution.py:755
  105.7 2.4 %collective-permute-start.13 = (bf16[592,128]{1,0:T(8,128)(2,1)S(1)}, bf16[592,128]{1,0:T(8,128)(2,1)S(1)}, u32[]{:S(2)}, u32[]{:S(2)}) collective-permute-start(bf16[592,128]{1,0:T(8,128)(2,1)S(1)} %collective-permute-done.9.refs_4_), channel_id=1, source_target_pairs={{0,1},{1,0},{2,3},{3,2},{4,5},{5,4},{6,7},{7,6},{8,9},{9,8},{10,11... | collective-permute-start | bytes 454664 | tf_op jit(solution)/shard_map/ppermute | solution.py:755
  107.6 1.4 %collective-permute-start.14 = (bf16[592,128]{1,0:T(8,128)(2,1)S(1)}, bf16[592,128]{1,0:T(8,128)(2,1)S(1)}, u32[]{:S(2)}, u32[]{:S(2)}) collective-permute-start(bf16[592,128]{1,0:T(8,128)(2,1)S(1)} %collective-permute-done.10.refs_5_), channel_id=1, source_target_pairs={{0,1},{1,0},{2,3},{3,2},{4,5},{5,4},{6,7},{7,6},{8,9},{9,8},{10,11... | collective-permute-start | bytes 454664 | tf_op jit(solution)/shard_map/ppermute | solution.py:755
  107.6 1.6 %collective-permute-start.15 = (bf16[592,128]{1,0:T(8,128)(2,1)S(1)}, bf16[592,128]{1,0:T(8,128)(2,1)S(1)}, u32[]{:S(2)}, u32[]{:S(2)}) collective-permute-start(bf16[592,128]{1,0:T(8,128)(2,1)S(1)} %collective-permute-done.11.refs_6_), channel_id=1, source_target_pairs={{0,1},{1,0},{2,3},{3,2},{4,5},{5,4},{6,7},{7,6},{8,9},{9,8},{10,11... | collective-permute-start | bytes 454664 | tf_op jit(solution)/shard_map/ppermute | solution.py:755

commit v6 on v5

--- a/solution.py
+++ b/solution.py
@@ -12,8 +12,7 @@
 
 epsilon = 1e-06
 masked_fill = -1e30
-score_bound = 64.0
-log2_e = 1.4426950408889634
+score_bound = 44.0
 low = jnp.bfloat16
 full = jnp.float32
 whole_vmem = pl.BlockSpec(memory_space=pltpu.VMEM)
@@ -84,10 +83,10 @@
 
 def attend_kernel(*refs):
     sources, refs = refs[:6], refs[6:]
-    outs, second_ref, same, refs = refs[:8], refs[8], refs[9], refs[10:]
-    probs_out, saved, refs = outs[0], refs[:7], refs[7:]
+    outs, second_ref, same, refs = refs[:9], refs[9], refs[10], refs[11:]
+    probs_out, saved, refs = outs[0], refs[:8], refs[8:]
     queries_ref, keys_ref, value_rows_ref, first_ref = saved[:4]
-    attn_ref, inverse_ref, resid_ref = saved[4:]
+    attn_ref, rest_ref, inverse_ref, resid_ref = saved[4:]
     probs_ref, key_rows, values, mask_rows, bound, semaphores, probs_semaphores = refs[:7]
     x_ref, gain_ref, weight_ref, ids_ref, proj_ref, second_gain_ref = refs[7:13]
     loads = copies_of(sources, refs[7:13], refs[13])
@@ -109,8 +108,9 @@
     first_in = (normed * gain_ref[...].reshape(1, width)).astype(low)
     loads[2].wait()
     turned = dot(weight_ref[...], first_in, 0, 1)
-    scaled = (turned[:width] * (half**-0.5 * log2_e)).astype(low)
-    turned = turned[width:].astype(low)
+    turned = turned.astype(low)
+    scaled = turned[:width] * jnp.asarray(half**-0.5, low)
+    turned = turned[width:]
     queries_ref[...] = scaled.reshape(pairs, LANES, length)
     keys_ref[...] = turned[:width].reshape(pairs, LANES, length)
     values[...] = turned[width:].reshape(pairs, LANES, length)
@@ -151,33 +151,36 @@
             mixed = dot(value, probs_ref[2 * pair + head])
             inverse = 1.0 / mixed[half : half + 1]
             inverse_ref[pair, head : head + 1] = inverse
-            attn_ref[pair, rows] = (mixed[:half] * inverse).astype(low)
+            mixed = mixed[:half] * inverse
+            attn = mixed.astype(low)
+            attn_ref[pair, rows] = attn
+            rest_ref[pair, rows] = (mixed - attn.astype(full)).astype(low)
 
     small = bound[0] < score_bound * score_bound
 
     def one_pair(pair, carry):
         @pl.when(small)
         def _():
-            attend_pair(pair, jnp.exp2)
+            attend_pair(pair, jnp.exp)
 
         @pl.when(jnp.logical_not(small))
         def _():
             attend_pair(
                 pair,
-                lambda scores: jnp.exp2(scores - jnp.max(scores, axis=0, keepdims=True)),
+                lambda scores: jnp.exp(scores - jnp.max(scores, axis=0, keepdims=True)),
             )
 
         return carry
 
     lax.fori_loop(0, pairs, one_pair, 0)
-    for save in saves[4:6]:
+    for save in saves[4:7]:
         save.start()
     for load in loads[4:]:
         load.wait()
     attn = attn_ref[...].reshape(width, length)
     resid = x_ref[...].astype(full) + dot(attn, proj_ref[...], 0, 0)
     resid_ref[...] = resid
-    saves[6].start()
+    saves[7].start()
     normed, _ = norm_parts(resid)
     second_ref[...] = (normed * second_gain_ref[...].reshape(1, width)).astype(low)
     for save in saves:
@@ -199,13 +202,14 @@
         (rows, low),
         ((width, length), low),
         (stack, low),
+        (stack, low),
         ((pairs, 2, length), full),
         ((length, width), full),
     ]
     return pl.pallas_call(
         attend_kernel,
         in_specs=[anywhere] * 6,
-        out_specs=[anywhere] * 8 + [whole_vmem] * 2,
+        out_specs=[anywhere] * 9 + [whole_vmem] * 2,
         out_shape=[kept(probs, low)]
         + [kept(*entry) for entry in saved]
         + [shape_of((length, width), low), shape_of((LANES, length), low)],
@@ -216,7 +220,7 @@
             pltpu.VMEM(stack, low),
             pltpu.VMEM((length, LANES), low),
             pltpu.SMEM((1,), full),
-            pltpu.SemaphoreType.DMA((7,)),
+            pltpu.SemaphoreType.DMA((8,)),
             pltpu.SemaphoreType.DMA((2 * pairs,)),
         ]
         + [pltpu.VMEM(array.shape, array.dtype) for array in inputs]
@@ -351,15 +355,15 @@
 
 
 def backward_kernel(back_ref, *refs):
-    sources, probs_source, refs = refs[:15], refs[15], refs[16:]
+    sources, probs_source, refs = refs[:16], refs[16], refs[17:]
     (output_out, grad_resid_out, grads_out, sums_ref), refs = refs[:4], refs[4:]
-    targets, refs = refs[:15], refs[15:]
+    targets, refs = refs[:16], refs[16:]
     probs_ref, output_ref, grad_resid_ref, grads_ref, grad_attn, delta, grad_scores = refs[:7]
     turned_scores, turned_probs, semaphores, probs_semaphores, saves_semaphores = refs[7:]
     loads = copies_of(sources, targets, semaphores)
     ids_ref, cotangent_ref, combine_ref, second_ref, dispatch_ref, slots_ref = targets[:6]
-    resid_ref, gain_ref, attn_ref, proj_ref, inverse_ref = targets[6:11]
-    values_ref, keys_ref, queries_ref, first_ref = targets[11:]
+    resid_ref, gain_ref, attn_ref, rest_ref, proj_ref, inverse_ref = targets[6:12]
+    values_ref, keys_ref, queries_ref, first_ref = targets[12:]
     pairs = resid_ref.shape[1] // LANES
 
     def load_probs(pair):
@@ -377,11 +381,11 @@
     saves = copies_of(
         [output_ref, grad_resid_ref], [output_out, grad_resid_out], saves_semaphores
     )
-    for load in loads[:11]:
+    for load in loads[:12]:
         load.start()
     for load in loads[:6]:
         load.wait()
-    for load in loads[11:]:
+    for load in loads[12:]:
         load.start()
     load_probs(0).start()
     length, width = resid_ref.shape
@@ -411,7 +415,7 @@
     mixing = jnp.concatenate([dispatch.astype(low).reshape(count, length), grad_low], axis=0)
     mixed = jnp.concatenate([grad_slots, slots_ref[...]], axis=0)
     grad_second = dot(mixing, mixed, 0, 0)
-    for load in loads[6:11]:
+    for load in loads[6:12]:
         load.wait()
     resid = resid_ref[...]
     combine_low = jnp.where(member[None], combine, 0.0).astype(low).reshape(count, length)
@@ -428,8 +432,8 @@
     proj_grad = dot(attn.reshape(width, length), grad_branch).astype(low)
     scaled = dot(proj_ref[...], grad_branch, 1, 1).reshape(pairs, 2, half, length)
     scaled = (scaled * inverse_ref[...][:, :, None, :]).astype(low)
-    product = scaled.astype(full) * attn.reshape(scaled.shape).astype(full)
-    delta[...] = jnp.sum(product, axis=2)
+    exact = attn.astype(full) + rest_ref[...].astype(full)
+    delta[...] = jnp.sum(scaled.astype(full) * exact.reshape(scaled.shape), axis=2)
     grad_attn[...] = scaled.reshape(grad_attn.shape)
     slot_low = slot_grad.astype(low)
     second_low = jnp.broadcast_to(second_grad, (16, width)).astype(low)
@@ -445,7 +449,7 @@
     if used < sums_ref.shape[0]:
         sums_ref[used:] = jnp.zeros((sums_ref.shape[0] - used, LANES), low)
 
-    for load in loads[11:]:
+    for load in loads[12:]:
         load.wait()
     factor = half**-0.5
     none = jnp.zeros((half, TILE), low)
@@ -471,8 +475,8 @@
                 turned_scores[head, span, :] = scores.T
             turned_probs[head] = probs_ref[2 * pair + head].T
         for head, rows in enumerate(heads):
-            grads_ref[pair, 1, rows, :] = (
-                dot(queries_ref[pair, rows, :], turned_scores[head]) * (1.0 / log2_e)
+            grads_ref[pair, 1, rows, :] = dot(
+                queries_ref[pair, rows, :], turned_scores[head]
             ).astype(low)
         for head, rows in enumerate(heads):
             grads_ref[pair, 2, rows, :] = dot(
@@ -730,7 +734,7 @@
     slots = lax.all_to_all(spread, "expert", 0, 0, tiled=True).reshape(experts, width)
     patches = patches[0]
     cotangent = cotangent[0]
-    probs, queries, keys, values, first_in, attn, inverse, resid, second_in, same = attend(
+    probs, queries, keys, values, first_in, attn, rest, inverse, resid, second_in, same = attend(
         patches, image_ids, first_gain, qkv_weight, proj_weight, second_gain
     )
     second_in, dispatch, combine, send = route(second_in, slots, same, cotangent, groups)
@@ -742,7 +746,8 @@
         for step in range(1, copies)
     ]
     saved = [image_ids, cotangent, combine, second_in, dispatch, slots]
-    saved += [resid, second_gain, attn, proj_weight, inverse, values, keys, queries, first_in]
+    saved += [resid, second_gain, attn, rest, proj_weight, inverse]
+    saved += [values, keys, queries, first_in]
     output, grad_resid, grads, terms = backward(back, saved, probs)
     place = jnp.stack([lax.axis_index("expert"), lax.axis_index("rows")]).astype(jnp.int32)
     layers = groups // 2

time: 112 us -> 112 us (level)
  no operation moved by 1% of the time
where the time goes in v6:
time: 112 us
  Pallas kernels  53.1 us (47%)
  waiting for transfers between devices  21.4 us (19%)
  starting transfers between devices  21.1 us (19%)
  blocking collectives  13.6 us (12%)
  local copies, waits for them, and re-layouts  1.49 us (1%)
    pallas_call x1, Pallas kernels, backward(): pl.pallas_call(backward_kernel, in_specs=[whole_vmem] + [anywhere] * (len...  18 us
    ppermute x13, waiting for transfers between devices, flip(): return lax.ppermute(array, both_axes, pairs)  15.8 us
    all_to_all x1, blocking collectives, per_device(): received = lax.all_to_all(send, 'expert', 0, 0, tiled=True)  13.6 us
    pallas_call x1, Pallas kernels, attend(): pl.pallas_call(attend_kernel, in_specs=[anywhere] * 6, out_specs=[anywher...  11.7 us
    ppermute x13, starting transfers between devices, flip(): return lax.ppermute(array, both_axes, pairs)  8.36 us
    all_to_all x1, starting transfers between devices, per_device(): lax.all_to_all(spread, 'expert', 0, 0, tiled=True).reshape(experts, width)  7.25 us
    pallas_call x1, Pallas kernels, weight_grads(): pl.pallas_call(kernel, grid=(experts, steps), in_specs=[whole_vmem] * cop...  6.89 us
    all_to_all x1, waiting for transfers between devices, per_device(): back = lax.all_to_all(back, 'expert', 0, 0, tiled=True)  5.6 us
  transfers between devices with their start and end apart: 18, of which 9 were waited for; matrix products, arithmetic and copies ran while one was open for 0% of the time, Pallas kernels for 38%

profile of v6, /device:TPU:0, one launch (start us, length us, event | category | flops | bytes accessed | tf_op | source)
XLA Modules:
  0.0 111.7 jit_solution(10959751384213533309)
XLA Ops:
  0.6 0.0 copy-start
  0.7 1.4 %broadcast_in_dim.12 = bf16[8,2,384]{2,1,0:T(2,128)(2,1)} broadcast(bf16[2,384]{1,0:T(2,128)(2,1)} %bitcast.13), dimensions={1,2} | broadcast | bytes 13824 | tf_op jit(solution)/shard_map/broadcast_in_dim | solution.py:733
  2.1 7.3 %all-to-all-start = ((bf16[8,2,384]{2,1,0:T(2,128)(2,1)}), bf16[8,2,384]{2,1,0:T(2,128)(2,1)S(1)}, u32[]{:S(2)}, u32[]{:S(2)}) async-start(bf16[8,2,384]{2,1,0:T(2,128)(2,1)} %broadcast_in_dim.12), calls=%async_computation | async-start | bytes 24576 | tf_op jit(solution)/shard_map/all_to_all | solution.py:734
  9.3 11.7 %attend.1 = (bf16[6,1024,1024]{2,1,0:T(8,128)(2,1)}, bf16[3,128,1024]{2,1,0:T(8,128)(2,1)}, bf16[3,128,1024]{2,1,0:T(8,128)(2,1)}, bf16[3,1024,128]{2,1,0:T(8,12...) custom-call(bf16[1024,384]{1,0:T(8,128)(2,1)} %bitcast.8, ...), custom_call_target="tpu_custom_call" | custom-call | bytes 43200000 | tf_op jit(solution)/shard_map/attend/pallas_call | solution.py:209
  21.0 0.0 all-to-all-done
  21.1 0.0 copy-start.3
  21.1 1.8 %route.1 = (bf16[1024,384]{1,0:T(8,128)(2,1)}, f32[16,8,1024]{2,1,0:T(8,128)}, f32[16,8,1024]{2,1,0:T(8,128)}, bf16[8,2,16,384]{3,2,1,0:T(8,128)(2,1)S(1)}) custom-call(bf16[1024,384]{1,0:T(8,128)(2,1)S(1)} %get-tuple-element.54.second_ref, bf16[16,384]{1,0:T(8,128)(2,1)S(1)} %reshape.22.slots_ref.refs_5_, bf16[128,1024]{1,0:T(8,128)(2,1)S(1)} %get-tuple-element.55.same_ref, ...), custom_call_target="tpu_custom_call" | custom-call | bytes 10800000 | tf_op jit(solution)/shard_map/route/pallas_call | solution.py:287
  22.9 13.6 %all_to_all.15.received_ref.refs_0_ = bf16[8,2,16,384]{3,2,1,0:T(8,128)(2,1)S(1)} all-to-all(bf16[8,2,16,384]{3,2,1,0:T(8,128)(2,1)S(1)} %get-tuple-element.56), channel_id=1, replica_groups=mesh['expert'=8,'rows'=4] {'expert'}, dimensions={0} | all-to-all | bytes 393216 | tf_op jit(solution)/shard_map/all_to_all | solution.py:741
  36.5 0.0 copy-done
  36.5 4.5 %run_experts.1 = bf16[8,2,16,384]{3,2,1,0:T(8,128)(2,1)} custom-call(bf16[8,2,16,384]{3,2,1,0:T(8,128)(2,1)S(1)} %all_to_all.15.received_ref.refs_0_, bf16[2,384,1536]{2,1,0:T(8,128)(2,1)S(1)} %copy-done, bf16[2,1536,384]{2,1,0:T(8,128)(2,1)} %refs_5_.3), custom_call_target="tpu_custom_call" | custom-call | bytes 10800000 | tf_op jit(solution)/shard_map/run_experts/pallas_call | solution.py:341
  41.0 0.0 copy-done.3
  41.0 3.6 %all-to-all-start.2 = ((bf16[8,2,16,384]{3,2,1,0:T(8,128)(2,1)}), bf16[8,2,16,384]{3,2,1,0:T(8,128)(2,1)S(1)}, u32[]{:S(2)}, u32[]{:S(2)}) async-start(bf16[8,2,16,384]{3,2,1,0:T(8,128)(2,1)} %run_experts.1), calls=%async_computation.2 | async-start | bytes 393216 | tf_op jit(solution)/shard_map/all_to_all | solution.py:743
  44.6 0.1 collective-permute-start
  44.7 1.6 %collective-permute-start.1 = (bf16[8,2,16,384]{3,2,1,0:T(8,128)(2,1)S(1)}, bf16[8,2,16,384]{3,2,1,0:T(8,128)(2,1)S(1)}, u32[]{:S(2)}, u32[]{:S(2)}) collective-permute-start(bf16[8,2,16,384]{3,2,1,0:T(8,128)(2,1)S(1)} %all_to_all.15.received_ref.refs_0_), channel_id=1, source_target_pairs={{0,2},{1,3},{2,0},{3,1},{4,6},{5,7},{6,4},{7,5},{8,10},{9,11},{10,... | collective-permute-start | bytes 589832 | tf_op jit(solution)/shard_map/ppermute | solution.py:745
  46.3 0.0 copy-done.2
  46.3 0.3 collective-permute-start.2
  46.5 5.6 %all-to-all-done.2.back_ref = bf16[8,2,16,384]{3,2,1,0:T(8,128)(2,1)S(1)} async-done(((bf16[8,2,16,384]{3,2,1,0:T(8,128)(2,1)}), bf16[8,2,16,384]{3,2,1,0:T(8,128)(2,1)S(1)}, u32[]{:S(2)}, u32[]{:S(2)}) %all-to-all-start.2) | async-done | bytes 196640 | tf_op jit(solution)/shard_map/all_to_all | solution.py:743
  52.1 18.0 %backward.1 = (bf16[1024,384]{1,0:T(8,128)(2,1)}, f32[1024,384]{1,0:T(8,128)}, bf16[3,3,128,1024]{3,2,1,0:T(8,128)(2,1)}, bf16[4736,128]{1,0:T(8,128)(2,1)S(1)}) custom-call(bf16[8,2,16,384]{3,2,1,0:T(8,128)(2,1)S(1)} %all-to-all-done.2.back_ref, s32[1,1024]{1,0:T(1,128)} %refs_0_.1, bf16[1024,384]{1,0:T(8,128)(2,1)} %bitcast.11, ...), custom_call_target="tpu_custom_call" | custom-call | bytes 72000000 | tf_op jit(solution)/shard_map/backward/pallas_call | solution.py:512
  70.1 0.0 collective-permute-done.refs_1_
  70.1 0.0 copy-start.5
  70.1 0.0 collective-permute-done.1.refs_2_
  70.1 0.0 copy-start.6
  70.1 0.0 collective-permute-done.2.refs_3_
  70.1 0.0 copy-start.7
  70.2 0.1 collective-permute-start.3
  70.2 0.1 pad_add_fusion.place_ref.refs_0_
  70.3 2.8 %collective-permute-done.3.other_ref = bf16[4736,128]{1,0:T(8,128)(2,1)S(1)} collective-permute-done((bf16[4736,128]{1,0:T(8,128)(2,1)S(1)}, bf16[4736,128]{1,0:T(8,128)(2,1)S(1)}, u32[]{:S(2)}, u32[]{:S(2)}) %collective-permute-start.3) | collective-permute-done | bytes 1212448 | tf_op jit(solution)/shard_map/ppermute | solution.py:760
  73.1 0.7 add_core.1
  73.8 0.1 collective-permute-start.4
  73.9 1.6 %collective-permute-start.5 = (bf16[592,128]{1,0:T(8,128)(2,1)S(1)}, bf16[592,128]{1,0:T(8,128)(2,1)S(1)}, u32[]{:S(2)}, u32[]{:S(2)}) collective-permute-start(bf16[592,128]{1,0:T(8,128)(2,1)S(1)} %get-tuple-element.73), channel_id=1, source_target_pairs={{0,2},{1,3},{2,0},{3,1},{4,6},{5,7},{6,4},{7,5},{8,10},{9,11},{10,... | collective-permute-start | bytes 454664 | tf_op jit(solution)/shard_map/ppermute | solution.py:760
  75.5 1.9 %collective-permute-start.6 = (bf16[592,128]{1,0:T(8,128)(2,1)S(1)}, bf16[592,128]{1,0:T(8,128)(2,1)S(1)}, u32[]{:S(2)}, u32[]{:S(2)}) collective-permute-start(bf16[592,128]{1,0:T(8,128)(2,1)S(1)} %get-tuple-element.74), channel_id=1, source_target_pairs={{0,6},{1,7},{2,4},{3,5},{4,2},{5,3},{6,0},{7,1},{8,14},{9,15},{10,... | collective-permute-start | bytes 454664 | tf_op jit(solution)/shard_map/ppermute | solution.py:760
  77.4 5.6 %patch_back.1 = f32[1024,384]{1,0:T(8,128)} custom-call(bf16[1024,384]{1,0:T(8,128)(2,1)} %bitcast.9, f32[384]{0:T(512)} %refs_2_.3, bf16[384,1152]{1,0:T(8,128)(2,1)} %refs_1_.3, f32[1024,384]{1,0:T(8,128)} %get-tuple-element.75.resid_ref, bf16[3,3,128,1024]{3,2,1,0:T(8,128)(2,1)} %get-tuple-element.78.grads_ref), custom_call_target="tpu_custom_call" | custom-call | bytes 10800000 | tf_op jit(solution)/shard_map/patch_back/pallas_call | solution.py:546
  82.9 0.0 copy-done.5
  82.9 0.0 copy-done.6
  83.0 0.0 copy-done.7
  83.0 0.0 collective-permute-done.4.refs_1_
  83.0 0.0 collective-permute-done.5.refs_2_
  83.0 1.1 collective-permute-done.6.refs_3_
  84.1 0.6 add_plane.1.mine_ref
  84.7 0.2 collective-permute-start.7
  84.9 5.0 %collective-permute-done.7.other_ref = bf16[592,128]{1,0:T(8,128)(2,1)S(1)} collective-permute-done((bf16[592,128]{1,0:T(8,128)(2,1)S(1)}, bf16[592,128]{1,0:T(8,128)(2,1)S(1)}, u32[]{:S(2)}, u32[]{:S(2)}) %collective-permute-start.7) | collective-permute-done | bytes 151584 | tf_op jit(solution)/shard_map/ppermute | solution.py:760
  89.9 0.6 add_line_1.1.mine_ref
  90.5 0.0 copy-start.1
  90.5 0.0 copy-start.4
  90.5 0.4 collective-permute-start.8
  91.0 6.9 %weight_grads.1 = (f32[2,384,1536]{2,1,0:T(8,128)}, f32[2,1536,384]{2,1,0:T(8,128)}) custom-call(bf16[8,2,16,384]{3,2,1,0:T(8,128)(2,1)} %copy-done.2, bf16[8,2,16,384]{3,2,1,0:T(8,128)(2,1)} %copy-done.5, bf16[8,2,16,384]{3,2,1,0:T(8,128)(2,1)} %copy-done.6, bf16[8,2,16,384]{3,2,1,0:T(8,128)(2,1)} %copy-done.7, bf16[2,384,1536]{2,1,0:T(8,128)(2,1)} %refs_4_.3, ...), custom_call_target="tpu_custom_call" | custom-call | bytes 32400000 | tf_op jit(solution)/shard_map/weight_grads/pallas_call | solution.py:593
  97.9 0.9 collective-permute-done.8.other_ref
  98.8 0.6 add_line_2.1.refs_3_
  99.3 0.4 collective-permute-start.9
  99.8 1.4 %collective-permute-start.10 = (bf16[592,128]{1,0:T(8,128)(2,1)S(1)}, bf16[592,128]{1,0:T(8,128)(2,1)S(1)}, u32[]{:S(2)}, u32[]{:S(2)}) collective-permute-start(bf16[592,128]{1,0:T(8,128)(2,1)S(1)} %add_line_2.1.refs_3_), channel_id=1, source_target_pairs={{0,2},{1,3},{2,0},{3,1},{4,6},{5,7},{6,4},{7,5},{8,10},{9,11},{10,... | collective-permute-start | bytes 454664 | tf_op jit(solution)/shard_map/ppermute | solution.py:760
  101.1 1.8 %collective-permute-start.11 = (bf16[592,128]{1,0:T(8,128)(2,1)S(1)}, bf16[592,128]{1,0:T(8,128)(2,1)S(1)}, u32[]{:S(2)}, u32[]{:S(2)}) collective-permute-start(bf16[592,128]{1,0:T(8,128)(2,1)S(1)} %add_line_2.1.refs_3_), channel_id=1, source_target_pairs={{0,6},{1,7},{2,4},{3,5},{4,2},{5,3},{6,0},{7,1},{8,14},{9,15},{10,... | collective-permute-start | bytes 454664 | tf_op jit(solution)/shard_map/ppermute | solution.py:760
  102.9 0.0 collective-permute-start.12
  102.9 3.1 %collective-permute-done.9.refs_4_ = bf16[592,128]{1,0:T(8,128)(2,1)S(1)} collective-permute-done((bf16[592,128]{1,0:T(8,128)(2,1)S(1)}, bf16[592,128]{1,0:T(8,128)(2,1)S(1)}, u32[]{:S(2)}, u32[]{:S(2)}) %collective-permute-start.9) | collective-permute-done | bytes 151584 | tf_op jit(solution)/shard_map/ppermute | solution.py:760
  105.9 0.0 collective-permute-start.13
  106.0 1.9 %collective-permute-done.10.refs_5_ = bf16[592,128]{1,0:T(8,128)(2,1)S(1)} collective-permute-done((bf16[592,128]{1,0:T(8,128)(2,1)S(1)}, bf16[592,128]{1,0:T(8,128)(2,1)S(1)}, u32[]{:S(2)}, u32[]{:S(2)}) %collective-permute-start.10) | collective-permute-done | bytes 151584 | tf_op jit(solution)/shard_map/ppermute | solution.py:760
  107.8 0.0 collective-permute-start.14
  107.8 0.0 collective-permute-done.11.refs_6_
  107.8 0.5 collective-permute-start.15
  108.3 0.0 collective-permute-done.12.refs_7_
  108.3 0.0 collective-permute-done.13.refs_8_
  108.3 0.9 collective-permute-done.14.refs_9_
  109.2 0.2 collective-permute-done.15.refs_10_
  109.4 0.0 copy-done.1
  109.4 2.3 %finish.1 = (f32[384]{0:T(512)}, f32[384,1152]{1,0:T(8,128)}, f32[384,384]{1,0:T(8,128)}, f32[384]{0:T(512)}, f32[2,384]{1,0:T(2,128)}) custom-call(s32[2]{0:T(128)S(1)} %pad_add_fusion.place_ref.refs_0_, bf16[384,1152]{1,0:T(8,128)(2,1)S(1)} %copy-done.1, f32[384]{0:T(512)S(1)} %copy-done.4, bf16[592,128]{1,0:T(8,128)(2,1)S(1)} %add_line_2.1.refs_3_, ...), custom_call_target="tpu_custom_call" | custom-call | bytes 10800000 | tf_op jit(solution)/shard_map/finish/pallas_call | solution.py:697
  (3 shorter events, 0.0 us)
Async XLA Ops:
  0.6 35.9 %copy-start = (bf16[2,384,1536]{2,1,0:T(8,128)(2,1)S(1)}, bf16[2,384,1536]{2,1,0:T(8,128)(2,1)}, u32[]{:S(2)}) copy-start(bf16[2,384,1536]{2,1,0:T(8,128)(2,1)} %refs_4_.3) | copy-start | bytes 7077892
  2.1 18.9 %all-to-all-start = ((bf16[8,2,384]{2,1,0:T(2,128)(2,1)}), bf16[8,2,384]{2,1,0:T(2,128)(2,1)S(1)}, u32[]{:S(2)}, u32[]{:S(2)}) async-start(bf16[8,2,384]{2,1,0:T(2,128)(2,1)} %broadcast_in_dim.12), calls=%async_computation | async-start | bytes 24576 | tf_op jit(solution)/shard_map/all_to_all | solution.py:734
  21.1 19.9 %copy-start.3 = (bf16[16,384]{1,0:T(8,128)(2,1)}, bf16[16,384]{1,0:T(8,128)(2,1)S(1)}, u32[]{:S(2)}) copy-start(bf16[16,384]{1,0:T(8,128)(2,1)S(1)} %reshape.22.slots_ref.refs_5_) | copy-start | bytes 36868
  36.5 9.7 %copy-start.2 = (bf16[8,2,16,384]{3,2,1,0:T(8,128)(2,1)}, bf16[8,2,16,384]{3,2,1,0:T(8,128)(2,1)S(1)}, u32[]{:S(2)}) copy-start(bf16[8,2,16,384]{3,2,1,0:T(8,128)(2,1)S(1)} %all_to_all.15.received_ref.refs_0_) | copy-start | bytes 589828
  41.0 11.1 %all-to-all-start.2 = ((bf16[8,2,16,384]{3,2,1,0:T(8,128)(2,1)}), bf16[8,2,16,384]{3,2,1,0:T(8,128)(2,1)S(1)}, u32[]{:S(2)}, u32[]{:S(2)}) async-start(bf16[8,2,16,384]{3,2,1,0:T(8,128)(2,1)} %run_experts.1), calls=%async_computation.2 | async-start | bytes 393216 | tf_op jit(solution)/shard_map/all_to_all | solution.py:743
  44.6 25.5 %collective-permute-start = (bf16[8,2,16,384]{3,2,1,0:T(8,128)(2,1)S(1)}, bf16[8,2,16,384]{3,2,1,0:T(8,128)(2,1)S(1)}, u32[]{:S(2)}, u32[]{:S(2)}) collective-permute-start(bf16[8,2,16,384]{3,2,1,0:T(8,128)(2,1)S(1)} %all_to_all.15.received_ref.refs_0_), channel_id=1, source_target_pairs={{0,1},{1,0},{2,3},{3,2},{4,5},{5,4},{6,7},{7,6},{8,9},{9,8},{10,11... | collective-permute-start | bytes 589832 | tf_op jit(solution)/shard_map/ppermute | solution.py:745
  44.7 25.4 %collective-permute-start.1 = (bf16[8,2,16,384]{3,2,1,0:T(8,128)(2,1)S(1)}, bf16[8,2,16,384]{3,2,1,0:T(8,128)(2,1)S(1)}, u32[]{:S(2)}, u32[]{:S(2)}) collective-permute-start(bf16[8,2,16,384]{3,2,1,0:T(8,128)(2,1)S(1)} %all_to_all.15.received_ref.refs_0_), channel_id=1, source_target_pairs={{0,2},{1,3},{2,0},{3,1},{4,6},{5,7},{6,4},{7,5},{8,10},{9,11},{10,... | collective-permute-start | bytes 589832 | tf_op jit(solution)/shard_map/ppermute | solution.py:745
  46.3 23.9 %collective-permute-start.2 = (bf16[8,2,16,384]{3,2,1,0:T(8,128)(2,1)S(1)}, bf16[8,2,16,384]{3,2,1,0:T(8,128)(2,1)S(1)}, u32[]{:S(2)}, u32[]{:S(2)}) collective-permute-start(bf16[8,2,16,384]{3,2,1,0:T(8,128)(2,1)S(1)} %all_to_all.15.received_ref.refs_0_), channel_id=1, source_target_pairs={{0,3},{1,2},{2,1},{3,0},{4,7},{5,6},{6,5},{7,4},{8,11},{9,10},{10,... | collective-permute-start | bytes 589832 | tf_op jit(solution)/shard_map/ppermute | solution.py:745
  70.1 12.8 %copy-start.5 = (bf16[8,2,16,384]{3,2,1,0:T(8,128)(2,1)}, bf16[8,2,16,384]{3,2,1,0:T(8,128)(2,1)S(1)}, u32[]{:S(2)}) copy-start(bf16[8,2,16,384]{3,2,1,0:T(8,128)(2,1)S(1)} %collective-permute-done.refs_1_) | copy-start | bytes 589828
  70.1 12.8 %copy-start.6 = (bf16[8,2,16,384]{3,2,1,0:T(8,128)(2,1)}, bf16[8,2,16,384]{3,2,1,0:T(8,128)(2,1)S(1)}, u32[]{:S(2)}) copy-start(bf16[8,2,16,384]{3,2,1,0:T(8,128)(2,1)S(1)} %collective-permute-done.1.refs_2_) | copy-start | bytes 589828
  70.1 12.8 %copy-start.7 = (bf16[8,2,16,384]{3,2,1,0:T(8,128)(2,1)}, bf16[8,2,16,384]{3,2,1,0:T(8,128)(2,1)S(1)}, u32[]{:S(2)}) copy-start(bf16[8,2,16,384]{3,2,1,0:T(8,128)(2,1)S(1)} %collective-permute-done.2.refs_3_) | copy-start | bytes 589828
  70.2 3.0 %collective-permute-start.3 = (bf16[4736,128]{1,0:T(8,128)(2,1)S(1)}, bf16[4736,128]{1,0:T(8,128)(2,1)S(1)}, u32[]{:S(2)}, u32[]{:S(2)}) collective-permute-start(bf16[4736,128]{1,0:T(8,128)(2,1)S(1)} %get-tuple-element.71.mine_ref), channel_id=1, source_target_pairs={{0,1},{1,0},{2,3},{3,2},{4,5},{5,4},{6,7},{7,6},{8,9},{9,8},{10,11... | collective-permute-start | bytes 3637256 | tf_op jit(solution)/shard_map/ppermute | solution.py:760
  73.8 9.1 %collective-permute-start.4 = (bf16[592,128]{1,0:T(8,128)(2,1)S(1)}, bf16[592,128]{1,0:T(8,128)(2,1)S(1)}, u32[]{:S(2)}, u32[]{:S(2)}) collective-permute-start(bf16[592,128]{1,0:T(8,128)(2,1)S(1)} %get-tuple-element.72), channel_id=1, source_target_pairs={{0,4},{1,5},{2,6},{3,7},{4,0},{5,1},{6,2},{7,3},{8,12},{9,13},{10,... | collective-permute-start | bytes 454664 | tf_op jit(solution)/shard_map/ppermute | solution.py:760
  73.9 9.1 %collective-permute-start.5 = (bf16[592,128]{1,0:T(8,128)(2,1)S(1)}, bf16[592,128]{1,0:T(8,128)(2,1)S(1)}, u32[]{:S(2)}, u32[]{:S(2)}) collective-permute-start(bf16[592,128]{1,0:T(8,128)(2,1)S(1)} %get-tuple-element.73), channel_id=1, source_target_pairs={{0,2},{1,3},{2,0},{3,1},{4,6},{5,7},{6,4},{7,5},{8,10},{9,11},{10,... | collective-permute-start | bytes 454664 | tf_op jit(solution)/shard_map/ppermute | solution.py:760
  75.5 8.6 %collective-permute-start.6 = (bf16[592,128]{1,0:T(8,128)(2,1)S(1)}, bf16[592,128]{1,0:T(8,128)(2,1)S(1)}, u32[]{:S(2)}, u32[]{:S(2)}) collective-permute-start(bf16[592,128]{1,0:T(8,128)(2,1)S(1)} %get-tuple-element.74), channel_id=1, source_target_pairs={{0,6},{1,7},{2,4},{3,5},{4,2},{5,3},{6,0},{7,1},{8,14},{9,15},{10,... | collective-permute-start | bytes 454664 | tf_op jit(solution)/shard_map/ppermute | solution.py:760
  84.7 5.3 %collective-permute-start.7 = (bf16[592,128]{1,0:T(8,128)(2,1)S(1)}, bf16[592,128]{1,0:T(8,128)(2,1)S(1)}, u32[]{:S(2)}, u32[]{:S(2)}) collective-permute-start(bf16[592,128]{1,0:T(8,128)(2,1)S(1)} %add_plane.1.mine_ref), channel_id=1, source_target_pairs={{0,8},{1,9},{2,10},{3,11},{4,12},{5,13},{6,14},{7,15},{8,0},{9,1},... | collective-permute-start | bytes 454664 | tf_op jit(solution)/shard_map/ppermute | solution.py:760
  90.5 18.9 %copy-start.1 = (bf16[384,1152]{1,0:T(8,128)(2,1)S(1)}, bf16[384,1152]{1,0:T(8,128)(2,1)}, u32[]{:S(2)}) copy-start(bf16[384,1152]{1,0:T(8,128)(2,1)} %refs_1_.3) | copy-start | bytes 2654212
  90.5 18.9 %copy-start.4 = (f32[384]{0:T(512)S(1)}, f32[384]{0:T(512)}, u32[]{:S(2)}) copy-start(f32[384]{0:T(512)} %refs_2_.3) | copy-start | bytes 4612
  90.5 8.2 %collective-permute-start.8 = (bf16[592,128]{1,0:T(8,128)(2,1)S(1)}, bf16[592,128]{1,0:T(8,128)(2,1)S(1)}, u32[]{:S(2)}, u32[]{:S(2)}) collective-permute-start(bf16[592,128]{1,0:T(8,128)(2,1)S(1)} %add_line_1.1.mine_ref), channel_id=1, source_target_pairs={{0,16},{1,17},{2,18},{3,19},{4,20},{5,21},{6,22},{7,23},{8,24},{9,... | collective-permute-start | bytes 454664 | tf_op jit(solution)/shard_map/ppermute | solution.py:760
  99.3 6.6 %collective-permute-start.9 = (bf16[592,128]{1,0:T(8,128)(2,1)S(1)}, bf16[592,128]{1,0:T(8,128)(2,1)S(1)}, u32[]{:S(2)}, u32[]{:S(2)}) collective-permute-start(bf16[592,128]{1,0:T(8,128)(2,1)S(1)} %add_line_2.1.refs_3_), channel_id=1, source_target_pairs={{0,4},{1,5},{2,6},{3,7},{4,0},{5,1},{6,2},{7,3},{8,12},{9,13},{10,... | collective-permute-start | bytes 454664 | tf_op jit(solution)/shard_map/ppermute | solution.py:760
  99.8 8.1 %collective-permute-start.10 = (bf16[592,128]{1,0:T(8,128)(2,1)S(1)}, bf16[592,128]{1,0:T(8,128)(2,1)S(1)}, u32[]{:S(2)}, u32[]{:S(2)}) collective-permute-start(bf16[592,128]{1,0:T(8,128)(2,1)S(1)} %add_line_2.1.refs_3_), channel_id=1, source_target_pairs={{0,2},{1,3},{2,0},{3,1},{4,6},{5,7},{6,4},{7,5},{8,10},{9,11},{10,... | collective-permute-start | bytes 454664 | tf_op jit(solution)/shard_map/ppermute | solution.py:760
  101.1 6.7 %collective-permute-start.11 = (bf16[592,128]{1,0:T(8,128)(2,1)S(1)}, bf16[592,128]{1,0:T(8,128)(2,1)S(1)}, u32[]{:S(2)}, u32[]{:S(2)}) collective-permute-start(bf16[592,128]{1,0:T(8,128)(2,1)S(1)} %add_line_2.1.refs_3_), channel_id=1, source_target_pairs={{0,6},{1,7},{2,4},{3,5},{4,2},{5,3},{6,0},{7,1},{8,14},{9,15},{10,... | collective-permute-start | bytes 454664 | tf_op jit(solution)/shard_map/ppermute | solution.py:760
  102.9 5.4 %collective-permute-start.12 = (bf16[592,128]{1,0:T(8,128)(2,1)S(1)}, bf16[592,128]{1,0:T(8,128)(2,1)S(1)}, u32[]{:S(2)}, u32[]{:S(2)}) collective-permute-start(bf16[592,128]{1,0:T(8,128)(2,1)S(1)} %add_line_2.1.refs_3_), channel_id=1, source_target_pairs={{0,1},{1,0},{2,3},{3,2},{4,5},{5,4},{6,7},{7,6},{8,9},{9,8},{10,11... | collective-permute-start | bytes 454664 | tf_op jit(solution)/shard_map/ppermute | solution.py:760
  105.9 2.4 %collective-permute-start.13 = (bf16[592,128]{1,0:T(8,128)(2,1)S(1)}, bf16[592,128]{1,0:T(8,128)(2,1)S(1)}, u32[]{:S(2)}, u32[]{:S(2)}) collective-permute-start(bf16[592,128]{1,0:T(8,128)(2,1)S(1)} %collective-permute-done.9.refs_4_), channel_id=1, source_target_pairs={{0,1},{1,0},{2,3},{3,2},{4,5},{5,4},{6,7},{7,6},{8,9},{9,8},{10,11... | collective-permute-start | bytes 454664 | tf_op jit(solution)/shard_map/ppermute | solution.py:760
  107.8 1.4 %collective-permute-start.14 = (bf16[592,128]{1,0:T(8,128)(2,1)S(1)}, bf16[592,128]{1,0:T(8,128)(2,1)S(1)}, u32[]{:S(2)}, u32[]{:S(2)}) collective-permute-start(bf16[592,128]{1,0:T(8,128)(2,1)S(1)} %collective-permute-done.10.refs_5_), channel_id=1, source_target_pairs={{0,1},{1,0},{2,3},{3,2},{4,5},{5,4},{6,7},{7,6},{8,9},{9,8},{10,11... | collective-permute-start | bytes 454664 | tf_op jit(solution)/shard_map/ppermute | solution.py:760
  107.8 1.6 %collective-permute-start.15 = (bf16[592,128]{1,0:T(8,128)(2,1)S(1)}, bf16[592,128]{1,0:T(8,128)(2,1)S(1)}, u32[]{:S(2)}, u32[]{:S(2)}) collective-permute-start(bf16[592,128]{1,0:T(8,128)(2,1)S(1)} %collective-permute-done.11.refs_6_), channel_id=1, source_target_pairs={{0,1},{1,0},{2,3},{3,2},{4,5},{5,4},{6,7},{7,6},{8,9},{9,8},{10,11... | collective-permute-start | bytes 454664 | tf_op jit(solution)/shard_map/ppermute | solution.py:760

commit v7 on v6

--- a/solution.py
+++ b/solution.py
@@ -104,25 +104,27 @@
 
     for load in loads[:2]:
         load.wait()
-    normed, _ = norm_parts(x_ref[...].astype(full))
-    first_in = (normed * gain_ref[...].reshape(1, width)).astype(low)
-    loads[2].wait()
-    turned = dot(weight_ref[...], first_in, 0, 1)
-    turned = turned.astype(low)
-    scaled = turned[:width] * jnp.asarray(half**-0.5, low)
-    turned = turned[width:]
-    queries_ref[...] = scaled.reshape(pairs, LANES, length)
-    keys_ref[...] = turned[:width].reshape(pairs, LANES, length)
-    values[...] = turned[width:].reshape(pairs, LANES, length)
+    gain = gain_ref[...].reshape(1, width)
+    for start in range(0, length, length // 2):
+        span = slice(start, start + length // 2)
+        normed, _ = norm_parts(x_ref[span].astype(full))
+        first_in = (normed * gain).astype(low)
+        if start == 0:
+            loads[2].wait()
+            weight = weight_ref[...].T
+        turned = dot(weight, first_in, 1, 1).astype(low).reshape(3, pairs, LANES, length // 2)
+        queries_ref[:, :, span] = turned[0] * jnp.asarray(half**-0.5, low)
+        keys_ref[:, :, span] = turned[1]
+        values[:, :, span] = turned[2]
+        first_ref[:, span] = first_in.T
     norms = []
-    for part in (scaled, turned[:width]):
-        square = part.astype(full).reshape(2 * pairs, half, length)
+    for part in (queries_ref, keys_ref):
+        square = part[...].astype(full).reshape(2 * pairs, half, length)
         norms.append(jnp.max(jnp.sum(square * square, axis=1), axis=1, keepdims=True))
     bound[0] = jnp.max(norms[0] * norms[1])
     for index in range(pairs):
         key_rows[index] = keys_ref[index].T
         value_rows_ref[index] = values[index].T
-    first_ref[...] = first_in.T
     for save in saves[:4]:
         save.start()
     loads[3].wait()
@@ -356,7 +358,7 @@
 
 def backward_kernel(back_ref, *refs):
     sources, probs_source, refs = refs[:16], refs[16], refs[17:]
-    (output_out, grad_resid_out, grads_out, sums_ref), refs = refs[:4], refs[4:]
+    (output_out, grad_resid_out, grads_out, sums_ref, send_ref), refs = refs[:5], refs[5:]
     targets, refs = refs[:16], refs[16:]
     probs_ref, output_ref, grad_resid_ref, grads_ref, grad_attn, delta, grad_scores = refs[:7]
     turned_scores, turned_probs, semaphores, probs_semaphores, saves_semaphores = refs[7:]
@@ -495,6 +497,8 @@
         return carry
 
     lax.fori_loop(0, pairs, one_pair, 0)
+    core, _, _ = position()
+    send_ref[...] = sums_ref[rows_at(1 - core, send_ref.shape[0])]
     for save in saves + [save_grads(pair) for pair in range(pairs)]:
         save.wait()
 
@@ -512,8 +516,9 @@
     return pl.pallas_call(
         backward_kernel,
         in_specs=[whole_vmem] + [anywhere] * (len(arrays) + 1),
-        out_specs=[anywhere] * 3 + [whole_vmem],
-        out_shape=[kept(*entry) for entry in saved] + [shape_of((rows, LANES), low)],
+        out_specs=[anywhere] * 3 + [whole_vmem] * 2,
+        out_shape=[kept(*entry) for entry in saved]
+        + [shape_of((count, LANES), low) for count in (rows, rows // 2)],
         scratch_shapes=[pltpu.VMEM(array.shape, array.dtype) for array in (*arrays, probs)]
         + [pltpu.VMEM(*entry) for entry in saved]
         + [
@@ -603,8 +608,8 @@
     )(*keep(*received, up, down))
 
 
-def position(place_ref):
-    expert, row = place_ref[0], place_ref[1]
+def position():
+    expert, row = lax.axis_index("expert"), lax.axis_index("rows")
     return row % 2, row // 2 * 2 + expert % 2, expert // 2
 
 
@@ -619,7 +624,7 @@
 def small_call(kernel, out_shape, name, *arrays):
     return pl.pallas_call(
         kernel,
-        in_specs=[pl.BlockSpec(memory_space=pltpu.SMEM)] + [whole_vmem] * (len(arrays) - 1),
+        in_specs=[whole_vmem] * len(arrays),
         out_specs=jax.tree.map(lambda _: whole_vmem, out_shape),
         out_shape=out_shape,
         compiler_params=params(16),
@@ -628,38 +633,39 @@
     )(*arrays)
 
 
-def core_kernel(place_ref, mine_ref, other_ref, *outs):
-    core, quarter, _ = position(place_ref)
+def core_kernel(mine_ref, other_ref, *outs):
+    core, quarter, _ = position()
     count = outs[0].shape[0]
     for step, out in enumerate(outs):
-        rows = rows_at(core * 4 + flipped(quarter, step), count)
-        out[...] = (mine_ref[rows].astype(full) + other_ref[rows].astype(full)).astype(out.dtype)
-
-
-def plane_kernel(place_ref, *refs):
+        mine = mine_ref[rows_at(core * 4 + flipped(quarter, step), count)].astype(full)
+        other = other_ref[rows_at(flipped(quarter, step), count)].astype(full)
+        out[...] = (mine + other).astype(out.dtype)
+
+
+def plane_kernel(*refs):
     total = refs[0][...]
     for other in refs[1:-1]:
         total = total + other[...].astype(full)
     refs[-1][...] = total.astype(low)
 
 
-def line_kernel(place_ref, mine_ref, other_ref, out_ref):
+def line_kernel(mine_ref, other_ref, out_ref):
     out_ref[...] = (mine_ref[...].astype(full) + other_ref[...].astype(full)).astype(low)
 
 
-def finish_parts(place_ref, parts, whole):
-    core, quarter, _ = position(place_ref)
+def finish_parts(parts, whole):
+    core, quarter, _ = position()
     for index, part in enumerate(parts):
         half = flipped(core, index // 4)
         whole[rows_at(half * 4 + flipped(quarter, index % 4), part.shape[0])] = part[...]
 
 
 def finish_kernel(
-    total, place_ref, weight_ref, gain_ref, *refs
+    total, weight_ref, gain_ref, *refs
 ):
     parts = refs[:8]
     first_ref, qkv_ref, proj_ref, second_ref, slot_ref, sums = refs[8:]
-    finish_parts(place_ref, parts, sums)
+    finish_parts(parts, sums)
     width = weight_ref.shape[0]
     pairs = width // LANES
     own = slot_ref.shape[0]
@@ -671,7 +677,7 @@
         start = (width + total) * pairs + index * 16
         seconds.append(sums[start : start + 16].astype(full)[0:1])
         start = width * pairs + index * total
-        row = lax.broadcasted_iota(jnp.int32, (own, total), 0) + place_ref[0] * own
+        row = lax.broadcasted_iota(jnp.int32, (own, total), 0) + lax.axis_index("expert") * own
         column = lax.broadcasted_iota(jnp.int32, (own, total), 1)
         chosen = (row == column).astype(full).astype(low)
         slot_ref[:, lanes] = dot(chosen, sums[start : start + total])
@@ -688,7 +694,7 @@
     first_ref[...] = (row / gain_ref[...].reshape(1, width)).reshape(width)
 
 
-def finish(place, parts, weight, gain, experts, own):
+def finish(parts, weight, gain, experts, own):
     width = weight.shape[0]
 
     def kernel(*refs):
@@ -696,7 +702,7 @@
 
     return pl.pallas_call(
         kernel,
-        in_specs=[pl.BlockSpec(memory_space=pltpu.SMEM)] + [whole_vmem] * (2 + len(parts)),
+        in_specs=[whole_vmem] * (2 + len(parts)),
         out_specs=[whole_vmem] * 5,
         out_shape=[
             shape_of((width,), full),
@@ -709,7 +715,7 @@
         compiler_params=params(20),
         cost_estimate=cost(3),
         name="finish",
-    )(place, weight, gain, *parts)
+    )(weight, gain, *parts)
 
 
 def per_device(
@@ -748,8 +754,7 @@
     saved = [image_ids, cotangent, combine, second_in, dispatch, slots]
     saved += [resid, second_gain, attn, rest, proj_weight, inverse]
     saved += [values, keys, queries, first_in]
-    output, grad_resid, grads, terms = backward(back, saved, probs)
-    place = jnp.stack([lax.axis_index("expert"), lax.axis_index("rows")]).astype(jnp.int32)
+    output, grad_resid, grads, terms, away = backward(back, saved, probs)
     layers = groups // 2
 
     def flip(array, expert, row):
@@ -759,17 +764,17 @@
         ]
         return lax.ppermute(array, both_axes, pairs)
 
-    terms, others = lax.optimization_barrier((terms, others))
+    away, others = lax.optimization_barrier((away, others))
     quarter = (terms.shape[0] // 8, LANES)
     mine, *sends = small_call(
         core_kernel, [shape_of(quarter, full)] + [shape_of(quarter, low)] * 3, "add_core",
-        place, terms, flip(terms, 0, 1),
+        terms, flip(away, 0, 1),
     )
     arrived = [flip(send, step % 2, step // 2 * 2) for step, send in enumerate(sends, 1)]
     grads, _ = lax.optimization_barrier((grads, mine))
     patch_grad = patch_back(patches, first_gain, qkv_weight, grad_resid, grads)
     arrived, patch_grad = lax.optimization_barrier((arrived, patch_grad))
-    mine = small_call(plane_kernel, shape_of(quarter, low), "add_plane", place, mine, *arrived)
+    mine = small_call(plane_kernel, shape_of(quarter, low), "add_plane", mine, *arrived)
     step = 1
     while step < layers:
         arrived = flip(mine, step * 2, 0)
@@ -778,14 +783,14 @@
             up_grad, down_grad = weight_grads([received] + others, up_weight, down_weight)
             arrived, up_grad, down_grad = lax.optimization_barrier((arrived, up_grad, down_grad))
         mine = small_call(
-            line_kernel, shape_of(quarter, low), f"add_line_{step}", place, mine, arrived
+            line_kernel, shape_of(quarter, low), f"add_line_{step}", mine, arrived
         )
         step *= 2
     arrived = [flip(mine, step % 2, step // 2 * 2) for step in range(1, 4)]
     parts = [mine] + arrived
     parts = parts + [flip(part, 0, 1) for part in parts]
     first_grad, qkv_grad, proj_grad, second_grad, slot_grad = finish(
-        place, parts, qkv_weight, first_gain, experts, own
+        parts, qkv_weight, first_gain, experts, own
     )
     return (
         output[None],

time: 112 us -> 108 us (0.964)
  Pallas kernels: 53.1 us -> 50.1 us
    pallas_call x5, Pallas kernels: 4.73 us -> 2.02 us  [the longest x1 1.73 us: finish(): pl.pallas_call(kernel, in_specs=[whole_vmem] * (2 + len(parts)), out_spec...]
  transfers between devices with their start and end apart: 18 -> 18, of which waited for: 9 -> 9; matrix products, arithmetic and copies ran while one was open for 0% -> 0% of each run, Pallas kernels for 38% -> 39%
where the time goes in v7:
time: 108 us
  Pallas kernels  50.1 us (46%)
  starting transfers between devices  21.1 us (20%)
  waiting for transfers between devices  20.9 us (19%)
  blocking collectives  13.6 us (13%)
  local copies, waits for them, and re-layouts  1.49 us (1%)
    pallas_call x1, Pallas kernels, backward(): pl.pallas_call(backward_kernel, in_specs=[whole_vmem] + [anywhere] * (len...  18 us
    ppermute x13, waiting for transfers between devices, flip(): return lax.ppermute(array, both_axes, pairs)  15.3 us
    all_to_all x1, blocking collectives, per_device(): received = lax.all_to_all(send, 'expert', 0, 0, tiled=True)  13.6 us
    pallas_call x1, Pallas kernels, attend(): pl.pallas_call(attend_kernel, in_specs=[anywhere] * 6, out_specs=[anywher...  11.4 us
    ppermute x13, starting transfers between devices, flip(): return lax.ppermute(array, both_axes, pairs)  8.36 us
    all_to_all x1, starting transfers between devices, per_device(): lax.all_to_all(spread, 'expert', 0, 0, tiled=True).reshape(experts, width)  7.25 us
    pallas_call x1, Pallas kernels, weight_grads(): pl.pallas_call(kernel, grid=(experts, steps), in_specs=[whole_vmem] * cop...  6.89 us
    all_to_all x1, waiting for transfers between devices, per_device(): back = lax.all_to_all(back, 'expert', 0, 0, tiled=True)  5.61 us
  transfers between devices with their start and end apart: 18, of which 9 were waited for; matrix products, arithmetic and copies ran while one was open for 0% of the time, Pallas kernels for 39%

profile of v7, /device:TPU:0, one launch (start us, length us, event | category | flops | bytes accessed | tf_op | source)
XLA Modules:
  0.0 108.0 jit_solution(13624027280844489353)
XLA Ops:
  0.6 0.0 copy-start
  0.7 1.4 %broadcast_in_dim.12 = bf16[8,2,384]{2,1,0:T(2,128)(2,1)} broadcast(bf16[2,384]{1,0:T(2,128)(2,1)} %bitcast.11), dimensions={1,2} | broadcast | bytes 13824 | tf_op jit(solution)/shard_map/broadcast_in_dim | solution.py:739
  2.1 7.3 %all-to-all-start = ((bf16[8,2,384]{2,1,0:T(2,128)(2,1)}), bf16[8,2,384]{2,1,0:T(2,128)(2,1)S(1)}, u32[]{:S(2)}, u32[]{:S(2)}) async-start(bf16[8,2,384]{2,1,0:T(2,128)(2,1)} %broadcast_in_dim.12), calls=%async_computation | async-start | bytes 24576 | tf_op jit(solution)/shard_map/all_to_all | solution.py:740
  9.3 11.4 %attend.1 = (bf16[6,1024,1024]{2,1,0:T(8,128)(2,1)}, bf16[3,128,1024]{2,1,0:T(8,128)(2,1)}, bf16[3,128,1024]{2,1,0:T(8,128)(2,1)}, bf16[3,1024,128]{2,1,0:T(8,12...) custom-call(bf16[1024,384]{1,0:T(8,128)(2,1)} %bitcast.6, ...), custom_call_target="tpu_custom_call" | custom-call | bytes 43200000 | tf_op jit(solution)/shard_map/attend/pallas_call | solution.py:211
  20.7 0.0 all-to-all-done
  20.7 0.0 copy-start.3
  20.7 1.8 %route.1 = (bf16[1024,384]{1,0:T(8,128)(2,1)}, f32[16,8,1024]{2,1,0:T(8,128)}, f32[16,8,1024]{2,1,0:T(8,128)}, bf16[8,2,16,384]{3,2,1,0:T(8,128)(2,1)S(1)}) custom-call(bf16[1024,384]{1,0:T(8,128)(2,1)S(1)} %get-tuple-element.55.second_ref, bf16[16,384]{1,0:T(8,128)(2,1)S(1)} %reshape.22.slots_ref.refs_5_, bf16[128,1024]{1,0:T(8,128)(2,1)S(1)} %get-tuple-element.56.same_ref, ...), custom_call_target="tpu_custom_call" | custom-call | bytes 10800000 | tf_op jit(solution)/shard_map/route/pallas_call | solution.py:289
  22.6 13.6 %all_to_all.15.received_ref.refs_0_ = bf16[8,2,16,384]{3,2,1,0:T(8,128)(2,1)S(1)} all-to-all(bf16[8,2,16,384]{3,2,1,0:T(8,128)(2,1)S(1)} %get-tuple-element.57), channel_id=1, replica_groups=mesh['expert'=8,'rows'=4] {'expert'}, dimensions={0} | all-to-all | bytes 393216 | tf_op jit(solution)/shard_map/all_to_all | solution.py:747
  36.2 0.0 copy-done
  36.2 0.0 copy-start.2
  36.2 4.5 %run_experts.1 = bf16[8,2,16,384]{3,2,1,0:T(8,128)(2,1)} custom-call(bf16[8,2,16,384]{3,2,1,0:T(8,128)(2,1)S(1)} %all_to_all.15.received_ref.refs_0_, bf16[2,384,1536]{2,1,0:T(8,128)(2,1)S(1)} %copy-done, bf16[2,1536,384]{2,1,0:T(8,128)(2,1)} %refs_5_.3), custom_call_target="tpu_custom_call" | custom-call | bytes 10800000 | tf_op jit(solution)/shard_map/run_experts/pallas_call | solution.py:343
  40.6 0.0 copy-done.3
  40.6 3.6 %all-to-all-start.2 = ((bf16[8,2,16,384]{3,2,1,0:T(8,128)(2,1)}), bf16[8,2,16,384]{3,2,1,0:T(8,128)(2,1)S(1)}, u32[]{:S(2)}, u32[]{:S(2)}) async-start(bf16[8,2,16,384]{3,2,1,0:T(8,128)(2,1)} %run_experts.1), calls=%async_computation.2 | async-start | bytes 393216 | tf_op jit(solution)/shard_map/all_to_all | solution.py:749
  44.2 0.1 collective-permute-start.2
  44.3 1.6 %collective-permute-start.1 = (bf16[8,2,16,384]{3,2,1,0:T(8,128)(2,1)S(1)}, bf16[8,2,16,384]{3,2,1,0:T(8,128)(2,1)S(1)}, u32[]{:S(2)}, u32[]{:S(2)}) collective-permute-start(bf16[8,2,16,384]{3,2,1,0:T(8,128)(2,1)S(1)} %all_to_all.15.received_ref.refs_0_), channel_id=1, source_target_pairs={{0,2},{1,3},{2,0},{3,1},{4,6},{5,7},{6,4},{7,5},{8,10},{9,11},{10,... | collective-permute-start | bytes 589832 | tf_op jit(solution)/shard_map/ppermute | solution.py:751
  45.9 0.0 copy-done.2
  45.9 0.3 collective-permute-start
  46.2 5.6 %all-to-all-done.2.back_ref = bf16[8,2,16,384]{3,2,1,0:T(8,128)(2,1)S(1)} async-done(((bf16[8,2,16,384]{3,2,1,0:T(8,128)(2,1)}), bf16[8,2,16,384]{3,2,1,0:T(8,128)(2,1)S(1)}, u32[]{:S(2)}, u32[]{:S(2)}) %all-to-all-start.2) | async-done | bytes 196640 | tf_op jit(solution)/shard_map/all_to_all | solution.py:749
  51.8 18.0 %backward.1 = (bf16[1024,384]{1,0:T(8,128)(2,1)}, f32[1024,384]{1,0:T(8,128)}, bf16[3,3,128,1024]{3,2,1,0:T(8,128)(2,1)}, bf16[4736,128]{1,0:T(8,128)(2,1)S(1)}, bf16[2368,128]{1,0:T(8,128)(2,1)S(1)}) custom-call(bf16[8,2,16,384]{3,2,1,0:T(8,128)(2,1)S(1)} %all-to-all-done.2.back_ref, s32[1,1024]{1,0:T(1,128)} %refs_0_.2, bf16[1024,384]{1,0:T(8,128)(2,1)} %bitcast.9, ...), custom_call_target="tpu_custom_call" | custom-call | bytes 72000000 | tf_op jit(solution)/shard_map/backward/pallas_call | solution.py:516
  69.7 0.0 collective-permute-done.2.refs_3_
  69.8 0.0 copy-start.5
  69.8 0.0 collective-permute-done.1.refs_2_
  69.8 0.0 copy-start.6
  69.8 0.0 collective-permute-done.refs_1_
  69.8 0.0 copy-start.7
  69.8 0.1 collective-permute-start.3
  69.9 2.0 %collective-permute-done.3.other_ref = bf16[2368,128]{1,0:T(8,128)(2,1)S(1)} collective-permute-done((bf16[2368,128]{1,0:T(8,128)(2,1)S(1)}, bf16[2368,128]{1,0:T(8,128)(2,1)S(1)}, u32[]{:S(2)}, u32[]{:S(2)}) %collective-permute-start.3) | collective-permute-done | bytes 606240 | tf_op jit(solution)/shard_map/ppermute | solution.py:765
  71.9 0.1 add_core.1
  72.0 0.1 collective-permute-start.4
  72.1 1.6 %collective-permute-start.5 = (bf16[592,128]{1,0:T(8,128)(2,1)S(1)}, bf16[592,128]{1,0:T(8,128)(2,1)S(1)}, u32[]{:S(2)}, u32[]{:S(2)}) collective-permute-start(bf16[592,128]{1,0:T(8,128)(2,1)S(1)} %get-tuple-element.75), channel_id=1, source_target_pairs={{0,2},{1,3},{2,0},{3,1},{4,6},{5,7},{6,4},{7,5},{8,10},{9,11},{10,... | collective-permute-start | bytes 454664 | tf_op jit(solution)/shard_map/ppermute | solution.py:765
  73.7 1.9 %collective-permute-start.6 = (bf16[592,128]{1,0:T(8,128)(2,1)S(1)}, bf16[592,128]{1,0:T(8,128)(2,1)S(1)}, u32[]{:S(2)}, u32[]{:S(2)}) collective-permute-start(bf16[592,128]{1,0:T(8,128)(2,1)S(1)} %get-tuple-element.76), channel_id=1, source_target_pairs={{0,6},{1,7},{2,4},{3,5},{4,2},{5,3},{6,0},{7,1},{8,14},{9,15},{10,... | collective-permute-start | bytes 454664 | tf_op jit(solution)/shard_map/ppermute | solution.py:765
  75.6 5.6 %patch_back.1 = f32[1024,384]{1,0:T(8,128)} custom-call(bf16[1024,384]{1,0:T(8,128)(2,1)} %bitcast.7, f32[384]{0:T(512)} %refs_1_.3, bf16[384,1152]{1,0:T(8,128)(2,1)} %refs_0_.3, f32[1024,384]{1,0:T(8,128)} %get-tuple-element.77.resid_ref, bf16[3,3,128,1024]{3,2,1,0:T(8,128)(2,1)} %get-tuple-element.80.grads_ref), custom_call_target="tpu_custom_call" | custom-call | bytes 10800000 | tf_op jit(solution)/shard_map/patch_back/pallas_call | solution.py:551
  81.2 0.0 copy-done.5
  81.2 0.0 copy-done.6
  81.2 0.0 copy-done.7
  81.2 0.0 collective-permute-done.4.refs_1_
  81.2 0.0 collective-permute-done.5.refs_2_
  81.2 1.1 collective-permute-done.6.refs_3_
  82.3 0.1 add_plane.1.mine_ref
  82.4 0.2 collective-permute-start.7
  82.6 5.0 %collective-permute-done.7.other_ref = bf16[592,128]{1,0:T(8,128)(2,1)S(1)} collective-permute-done((bf16[592,128]{1,0:T(8,128)(2,1)S(1)}, bf16[592,128]{1,0:T(8,128)(2,1)S(1)}, u32[]{:S(2)}, u32[]{:S(2)}) %collective-permute-start.7) | collective-permute-done | bytes 151584 | tf_op jit(solution)/shard_map/ppermute | solution.py:765
  87.7 0.0 copy-start.1
  87.7 0.0 copy-start.4
  87.7 0.4 collective-permute-start.8
  88.1 6.9 %weight_grads.1 = (f32[2,384,1536]{2,1,0:T(8,128)}, f32[2,1536,384]{2,1,0:T(8,128)}) custom-call(bf16[8,2,16,384]{3,2,1,0:T(8,128)(2,1)} %copy-done.2, bf16[8,2,16,384]{3,2,1,0:T(8,128)(2,1)} %copy-done.7, bf16[8,2,16,384]{3,2,1,0:T(8,128)(2,1)} %copy-done.6, bf16[8,2,16,384]{3,2,1,0:T(8,128)(2,1)} %copy-done.5, bf16[2,384,1536]{2,1,0:T(8,128)(2,1)} %refs_4_.3, ...), custom_call_target="tpu_custom_call" | custom-call | bytes 32400000 | tf_op jit(solution)/shard_map/weight_grads/pallas_call | solution.py:598
  95.0 0.9 collective-permute-done.8.other_ref
  95.9 1.2 %collective-permute-start.11 = (bf16[592,128]{1,0:T(8,128)(2,1)S(1)}, bf16[592,128]{1,0:T(8,128)(2,1)S(1)}, u32[]{:S(2)}, u32[]{:S(2)}) collective-permute-start(bf16[592,128]{1,0:T(8,128)(2,1)S(1)} %add_line_2.1.refs_2_), channel_id=1, source_target_pairs={{0,6},{1,7},{2,4},{3,5},{4,2},{5,3},{6,0},{7,1},{8,14},{9,15},{10,... | collective-permute-start | bytes 454664 | tf_op jit(solution)/shard_map/ppermute | solution.py:765
  97.1 0.7 collective-permute-start.10
  97.8 1.7 %collective-permute-start.9 = (bf16[592,128]{1,0:T(8,128)(2,1)S(1)}, bf16[592,128]{1,0:T(8,128)(2,1)S(1)}, u32[]{:S(2)}, u32[]{:S(2)}) collective-permute-start(bf16[592,128]{1,0:T(8,128)(2,1)S(1)} %add_line_2.1.refs_2_), channel_id=1, source_target_pairs={{0,4},{1,5},{2,6},{3,7},{4,0},{5,1},{6,2},{7,3},{8,12},{9,13},{10,... | collective-permute-start | bytes 454664 | tf_op jit(solution)/shard_map/ppermute | solution.py:765
  99.5 0.0 collective-permute-start.12
  99.5 4.0 %collective-permute-done.11.refs_5_ = bf16[592,128]{1,0:T(8,128)(2,1)S(1)} collective-permute-done((bf16[592,128]{1,0:T(8,128)(2,1)S(1)}, bf16[592,128]{1,0:T(8,128)(2,1)S(1)}, u32[]{:S(2)}, u32[]{:S(2)}) %collective-permute-start.11) | collective-permute-done | bytes 151584 | tf_op jit(solution)/shard_map/ppermute | solution.py:765
  103.5 0.0 collective-permute-start.15
  103.5 1.2 %collective-permute-done.10.refs_4_ = bf16[592,128]{1,0:T(8,128)(2,1)S(1)} collective-permute-done((bf16[592,128]{1,0:T(8,128)(2,1)S(1)}, bf16[592,128]{1,0:T(8,128)(2,1)S(1)}, u32[]{:S(2)}, u32[]{:S(2)}) %collective-permute-start.10) | collective-permute-done | bytes 151584 | tf_op jit(solution)/shard_map/ppermute | solution.py:765
  104.7 0.0 collective-permute-start.14
  104.7 0.0 collective-permute-done.9.refs_3_
  104.7 0.5 collective-permute-start.13
  105.2 0.0 collective-permute-done.12.refs_6_
  105.2 0.0 collective-permute-done.15.refs_9_
  105.2 0.9 collective-permute-done.14.refs_8_
  106.1 0.2 collective-permute-done.13.refs_7_
  106.3 0.0 copy-done.1
  106.3 0.0 copy-done.4
  106.3 1.7 %finish.1 = (f32[384]{0:T(512)}, f32[384,1152]{1,0:T(8,128)}, f32[384,384]{1,0:T(8,128)}, f32[384]{0:T(512)}, f32[2,384]{1,0:T(2,128)}) custom-call(bf16[384,1152]{1,0:T(8,128)(2,1)S(1)} %copy-done.1, f32[384]{0:T(512)S(1)} %copy-done.4, bf16[592,128]{1,0:T(8,128)(2,1)S(1)} %add_line_2.1.refs_2_, bf16[592,128]{1,0:T(8,128)(2,1)S(1)} %collective-permute-done.9.refs_3_, ...), custom_call_target="tpu_custom_call" | custom-call | bytes 10800000 | tf_op jit(solution)/shard_map/finish/pallas_call | solution.py:703
  (3 shorter events, 0.1 us)
Async XLA Ops:
  0.6 35.5 %copy-start = (bf16[2,384,1536]{2,1,0:T(8,128)(2,1)S(1)}, bf16[2,384,1536]{2,1,0:T(8,128)(2,1)}, u32[]{:S(2)}) copy-start(bf16[2,384,1536]{2,1,0:T(8,128)(2,1)} %refs_4_.3) | copy-start | bytes 7077892
  2.1 18.6 %all-to-all-start = ((bf16[8,2,384]{2,1,0:T(2,128)(2,1)}), bf16[8,2,384]{2,1,0:T(2,128)(2,1)S(1)}, u32[]{:S(2)}, u32[]{:S(2)}) async-start(bf16[8,2,384]{2,1,0:T(2,128)(2,1)} %broadcast_in_dim.12), calls=%async_computation | async-start | bytes 24576 | tf_op jit(solution)/shard_map/all_to_all | solution.py:740
  20.7 19.9 %copy-start.3 = (bf16[16,384]{1,0:T(8,128)(2,1)}, bf16[16,384]{1,0:T(8,128)(2,1)S(1)}, u32[]{:S(2)}) copy-start(bf16[16,384]{1,0:T(8,128)(2,1)S(1)} %reshape.22.slots_ref.refs_5_) | copy-start | bytes 36868
  36.2 9.7 %copy-start.2 = (bf16[8,2,16,384]{3,2,1,0:T(8,128)(2,1)}, bf16[8,2,16,384]{3,2,1,0:T(8,128)(2,1)S(1)}, u32[]{:S(2)}) copy-start(bf16[8,2,16,384]{3,2,1,0:T(8,128)(2,1)S(1)} %all_to_all.15.received_ref.refs_0_) | copy-start | bytes 589828
  40.6 11.1 %all-to-all-start.2 = ((bf16[8,2,16,384]{3,2,1,0:T(8,128)(2,1)}), bf16[8,2,16,384]{3,2,1,0:T(8,128)(2,1)S(1)}, u32[]{:S(2)}, u32[]{:S(2)}) async-start(bf16[8,2,16,384]{3,2,1,0:T(8,128)(2,1)} %run_experts.1), calls=%async_computation.2 | async-start | bytes 393216 | tf_op jit(solution)/shard_map/all_to_all | solution.py:749
  44.2 25.5 %collective-permute-start.2 = (bf16[8,2,16,384]{3,2,1,0:T(8,128)(2,1)S(1)}, bf16[8,2,16,384]{3,2,1,0:T(8,128)(2,1)S(1)}, u32[]{:S(2)}, u32[]{:S(2)}) collective-permute-start(bf16[8,2,16,384]{3,2,1,0:T(8,128)(2,1)S(1)} %all_to_all.15.received_ref.refs_0_), channel_id=1, source_target_pairs={{0,3},{1,2},{2,1},{3,0},{4,7},{5,6},{6,5},{7,4},{8,11},{9,10},{10,... | collective-permute-start | bytes 589832 | tf_op jit(solution)/shard_map/ppermute | solution.py:751
  44.3 25.4 %collective-permute-start.1 = (bf16[8,2,16,384]{3,2,1,0:T(8,128)(2,1)S(1)}, bf16[8,2,16,384]{3,2,1,0:T(8,128)(2,1)S(1)}, u32[]{:S(2)}, u32[]{:S(2)}) collective-permute-start(bf16[8,2,16,384]{3,2,1,0:T(8,128)(2,1)S(1)} %all_to_all.15.received_ref.refs_0_), channel_id=1, source_target_pairs={{0,2},{1,3},{2,0},{3,1},{4,6},{5,7},{6,4},{7,5},{8,10},{9,11},{10,... | collective-permute-start | bytes 589832 | tf_op jit(solution)/shard_map/ppermute | solution.py:751
  45.9 23.9 %collective-permute-start = (bf16[8,2,16,384]{3,2,1,0:T(8,128)(2,1)S(1)}, bf16[8,2,16,384]{3,2,1,0:T(8,128)(2,1)S(1)}, u32[]{:S(2)}, u32[]{:S(2)}) collective-permute-start(bf16[8,2,16,384]{3,2,1,0:T(8,128)(2,1)S(1)} %all_to_all.15.received_ref.refs_0_), channel_id=1, source_target_pairs={{0,1},{1,0},{2,3},{3,2},{4,5},{5,4},{6,7},{7,6},{8,9},{9,8},{10,11... | collective-permute-start | bytes 589832 | tf_op jit(solution)/shard_map/ppermute | solution.py:751
  69.8 11.4 %copy-start.5 = (bf16[8,2,16,384]{3,2,1,0:T(8,128)(2,1)}, bf16[8,2,16,384]{3,2,1,0:T(8,128)(2,1)S(1)}, u32[]{:S(2)}) copy-start(bf16[8,2,16,384]{3,2,1,0:T(8,128)(2,1)S(1)} %collective-permute-done.2.refs_3_) | copy-start | bytes 589828
  69.8 11.4 %copy-start.6 = (bf16[8,2,16,384]{3,2,1,0:T(8,128)(2,1)}, bf16[8,2,16,384]{3,2,1,0:T(8,128)(2,1)S(1)}, u32[]{:S(2)}) copy-start(bf16[8,2,16,384]{3,2,1,0:T(8,128)(2,1)S(1)} %collective-permute-done.1.refs_2_) | copy-start | bytes 589828
  69.8 11.4 %copy-start.7 = (bf16[8,2,16,384]{3,2,1,0:T(8,128)(2,1)}, bf16[8,2,16,384]{3,2,1,0:T(8,128)(2,1)S(1)}, u32[]{:S(2)}) copy-start(bf16[8,2,16,384]{3,2,1,0:T(8,128)(2,1)S(1)} %collective-permute-done.refs_1_) | copy-start | bytes 589828
  69.8 2.1 %collective-permute-start.3 = (bf16[2368,128]{1,0:T(8,128)(2,1)S(1)}, bf16[2368,128]{1,0:T(8,128)(2,1)S(1)}, u32[]{:S(2)}, u32[]{:S(2)}) collective-permute-start(bf16[2368,128]{1,0:T(8,128)(2,1)S(1)} %get-tuple-element.73), channel_id=1, source_target_pairs={{0,1},{1,0},{2,3},{3,2},{4,5},{5,4},{6,7},{7,6},{8,9},{9,8},{10,11... | collective-permute-start | bytes 1818632 | tf_op jit(solution)/shard_map/ppermute | solution.py:765
  72.0 9.1 %collective-permute-start.4 = (bf16[592,128]{1,0:T(8,128)(2,1)S(1)}, bf16[592,128]{1,0:T(8,128)(2,1)S(1)}, u32[]{:S(2)}, u32[]{:S(2)}) collective-permute-start(bf16[592,128]{1,0:T(8,128)(2,1)S(1)} %get-tuple-element.74), channel_id=1, source_target_pairs={{0,4},{1,5},{2,6},{3,7},{4,0},{5,1},{6,2},{7,3},{8,12},{9,13},{10,... | collective-permute-start | bytes 454664 | tf_op jit(solution)/shard_map/ppermute | solution.py:765
  72.1 9.1 %collective-permute-start.5 = (bf16[592,128]{1,0:T(8,128)(2,1)S(1)}, bf16[592,128]{1,0:T(8,128)(2,1)S(1)}, u32[]{:S(2)}, u32[]{:S(2)}) collective-permute-start(bf16[592,128]{1,0:T(8,128)(2,1)S(1)} %get-tuple-element.75), channel_id=1, source_target_pairs={{0,2},{1,3},{2,0},{3,1},{4,6},{5,7},{6,4},{7,5},{8,10},{9,11},{10,... | collective-permute-start | bytes 454664 | tf_op jit(solution)/shard_map/ppermute | solution.py:765
  73.7 8.6 %collective-permute-start.6 = (bf16[592,128]{1,0:T(8,128)(2,1)S(1)}, bf16[592,128]{1,0:T(8,128)(2,1)S(1)}, u32[]{:S(2)}, u32[]{:S(2)}) collective-permute-start(bf16[592,128]{1,0:T(8,128)(2,1)S(1)} %get-tuple-element.76), channel_id=1, source_target_pairs={{0,6},{1,7},{2,4},{3,5},{4,2},{5,3},{6,0},{7,1},{8,14},{9,15},{10,... | collective-permute-start | bytes 454664 | tf_op jit(solution)/shard_map/ppermute | solution.py:765
  82.4 5.3 %collective-permute-start.7 = (bf16[592,128]{1,0:T(8,128)(2,1)S(1)}, bf16[592,128]{1,0:T(8,128)(2,1)S(1)}, u32[]{:S(2)}, u32[]{:S(2)}) collective-permute-start(bf16[592,128]{1,0:T(8,128)(2,1)S(1)} %add_plane.1.mine_ref), channel_id=1, source_target_pairs={{0,8},{1,9},{2,10},{3,11},{4,12},{5,13},{6,14},{7,15},{8,0},{9,1},... | collective-permute-start | bytes 454664 | tf_op jit(solution)/shard_map/ppermute | solution.py:765
  87.7 18.6 %copy-start.1 = (bf16[384,1152]{1,0:T(8,128)(2,1)S(1)}, bf16[384,1152]{1,0:T(8,128)(2,1)}, u32[]{:S(2)}) copy-start(bf16[384,1152]{1,0:T(8,128)(2,1)} %refs_0_.3) | copy-start | bytes 2654212
  87.7 18.6 %copy-start.4 = (f32[384]{0:T(512)S(1)}, f32[384]{0:T(512)}, u32[]{:S(2)}) copy-start(f32[384]{0:T(512)} %refs_1_.3) | copy-start | bytes 4612
  87.7 8.2 %collective-permute-start.8 = (bf16[592,128]{1,0:T(8,128)(2,1)S(1)}, bf16[592,128]{1,0:T(8,128)(2,1)S(1)}, u32[]{:S(2)}, u32[]{:S(2)}) collective-permute-start(bf16[592,128]{1,0:T(8,128)(2,1)S(1)} %add_line_1.1.mine_ref), channel_id=1, source_target_pairs={{0,16},{1,17},{2,18},{3,19},{4,20},{5,21},{6,22},{7,23},{8,24},{9,... | collective-permute-start | bytes 454664 | tf_op jit(solution)/shard_map/ppermute | solution.py:765
  95.9 7.6 %collective-permute-start.11 = (bf16[592,128]{1,0:T(8,128)(2,1)S(1)}, bf16[592,128]{1,0:T(8,128)(2,1)S(1)}, u32[]{:S(2)}, u32[]{:S(2)}) collective-permute-start(bf16[592,128]{1,0:T(8,128)(2,1)S(1)} %add_line_2.1.refs_2_), channel_id=1, source_target_pairs={{0,6},{1,7},{2,4},{3,5},{4,2},{5,3},{6,0},{7,1},{8,14},{9,15},{10,... | collective-permute-start | bytes 454664 | tf_op jit(solution)/shard_map/ppermute | solution.py:765
  97.1 7.5 %collective-permute-start.10 = (bf16[592,128]{1,0:T(8,128)(2,1)S(1)}, bf16[592,128]{1,0:T(8,128)(2,1)S(1)}, u32[]{:S(2)}, u32[]{:S(2)}) collective-permute-start(bf16[592,128]{1,0:T(8,128)(2,1)S(1)} %add_line_2.1.refs_2_), channel_id=1, source_target_pairs={{0,2},{1,3},{2,0},{3,1},{4,6},{5,7},{6,4},{7,5},{8,10},{9,11},{10,... | collective-permute-start | bytes 454664 | tf_op jit(solution)/shard_map/ppermute | solution.py:765
  97.8 6.9 %collective-permute-start.9 = (bf16[592,128]{1,0:T(8,128)(2,1)S(1)}, bf16[592,128]{1,0:T(8,128)(2,1)S(1)}, u32[]{:S(2)}, u32[]{:S(2)}) collective-permute-start(bf16[592,128]{1,0:T(8,128)(2,1)S(1)} %add_line_2.1.refs_2_), channel_id=1, source_target_pairs={{0,4},{1,5},{2,6},{3,7},{4,0},{5,1},{6,2},{7,3},{8,12},{9,13},{10,... | collective-permute-start | bytes 454664 | tf_op jit(solution)/shard_map/ppermute | solution.py:765
  99.5 5.7 %collective-permute-start.12 = (bf16[592,128]{1,0:T(8,128)(2,1)S(1)}, bf16[592,128]{1,0:T(8,128)(2,1)S(1)}, u32[]{:S(2)}, u32[]{:S(2)}) collective-permute-start(bf16[592,128]{1,0:T(8,128)(2,1)S(1)} %add_line_2.1.refs_2_), channel_id=1, source_target_pairs={{0,1},{1,0},{2,3},{3,2},{4,5},{5,4},{6,7},{7,6},{8,9},{9,8},{10,11... | collective-permute-start | bytes 454664 | tf_op jit(solution)/shard_map/ppermute | solution.py:765
  103.5 1.7 %collective-permute-start.15 = (bf16[592,128]{1,0:T(8,128)(2,1)S(1)}, bf16[592,128]{1,0:T(8,128)(2,1)S(1)}, u32[]{:S(2)}, u32[]{:S(2)}) collective-permute-start(bf16[592,128]{1,0:T(8,128)(2,1)S(1)} %collective-permute-done.11.refs_5_), channel_id=1, source_target_pairs={{0,1},{1,0},{2,3},{3,2},{4,5},{5,4},{6,7},{7,6},{8,9},{9,8},{10,11... | collective-permute-start | bytes 454664 | tf_op jit(solution)/shard_map/ppermute | solution.py:765
  104.7 1.4 %collective-permute-start.14 = (bf16[592,128]{1,0:T(8,128)(2,1)S(1)}, bf16[592,128]{1,0:T(8,128)(2,1)S(1)}, u32[]{:S(2)}, u32[]{:S(2)}) collective-permute-start(bf16[592,128]{1,0:T(8,128)(2,1)S(1)} %collective-permute-done.10.refs_4_), channel_id=1, source_target_pairs={{0,1},{1,0},{2,3},{3,2},{4,5},{5,4},{6,7},{7,6},{8,9},{9,8},{10,11... | collective-permute-start | bytes 454664 | tf_op jit(solution)/shard_map/ppermute | solution.py:765
  104.7 1.6 %collective-permute-start.13 = (bf16[592,128]{1,0:T(8,128)(2,1)S(1)}, bf16[592,128]{1,0:T(8,128)(2,1)S(1)}, u32[]{:S(2)}, u32[]{:S(2)}) collective-permute-start(bf16[592,128]{1,0:T(8,128)(2,1)S(1)} %collective-permute-done.9.refs_3_), channel_id=1, source_target_pairs={{0,1},{1,0},{2,3},{3,2},{4,5},{5,4},{6,7},{7,6},{8,9},{9,8},{10,11... | collective-permute-start | bytes 454664 | tf_op jit(solution)/shard_map/ppermute | solution.py:765
